TPU v7x, 32 devices: a whole 2x2x4 slice. The times are simulated.
32 devices in a mesh: groups: 2 (over x), rep: 16 (over z, y, core).
Axes of the slice: x: 2, y: 2, z: 4, core: 2. Of those that a mesh axis runs over, the one named last changes fastest.
Arguments:
- queries: bfloat16 [256, 8192], P(('groups', 'rep')), parts along dimension 0, may hold values from -200 to 200
- incoming_pair: bfloat16 [256, 2, 1024], P(('groups', 'rep')), parts along dimension 0, may hold values from -6 to 6
- cache_key_value: bfloat16 [256, 2, 128, 1024], P(('groups', 'rep')), parts along dimension 0, may hold values from -40 to 40
- cache_length: int32 [256], P(('groups', 'rep')), parts along dimension 0, may hold values from 2 to 128, as said below
- out_weight: bfloat16 [8192, 8192], P('rep'), may hold values from -0.0625 to 0.0625
- adapter_down: bfloat16 [64, 8192, 64], P(('groups', 'rep')), parts along dimension 0, may hold values from -0.0625 to 0.0625
- adapter_up: bfloat16 [64, 64, 8192], P(('groups', 'rep')), parts along dimension 0, may hold values from -0.75 to 0.75
- request_adapter: int32 [256], P(('groups', 'rep')), parts along dimension 0, may hold values from 0 to 31
- adapter_slot: int32 [64], P('groups'), parts along dimension 0, may hold values from 0 to 31, each once
Outputs:
- projected: bfloat16 [256, 8192], P(('groups', 'rep')), parts along dimension 0
There are 2 independent parts, one for each index of `groups`. A program takes and returns all parts, laid end to end along the dimension named above; an argument that names none is the same for every part. Nothing has to cross between parts.
Inputs may be any that keep to these rules, and one draw needn't show every extreme that they name: `cache_length`: some request has all 128 slots live. `adapter_slot`: each of the 32 slots once; slot s is stored with index s on dimension 0.
All inputs are finite; a program needn't handle non-finite values.
Results may differ from a plain program's by a relative error of at most 0.007.
Values may be sent and summed in bfloat16 or wider, within the bound.
No kernel may reach another device: no remote copies, remote signals or barrier semaphores. Data moves between devices by JAX's collectives and lax.ppermute only.
A program may use at most 128 MiB of HBM per device.

v0:
```python
import jax
import jax.numpy as jnp
from jax import lax
from jax.sharding import PartitionSpec as P

QUERY_HEADS = 64
KEY_VALUE_HEADS = 8
HEAD_SIZE = 128
ADP_DEV = 2
CACHE_SLOTS = 128


ADAPTER_GAIN = 2.0
MASKED_SCORE = -1e30


def attend(queries, incoming_pair, cache_key_value, cache_length):
    request_batch = queries.shape[0]
    grouped_query = QUERY_HEADS // KEY_VALUE_HEADS
    scaling = HEAD_SIZE ** (-0.5)
    query_head_rows = queries.reshape(request_batch, KEY_VALUE_HEADS, grouped_query, HEAD_SIZE)
    cache_key_rows = cache_key_value[:, 0].reshape(
        request_batch, CACHE_SLOTS, KEY_VALUE_HEADS, HEAD_SIZE
    )
    cache_value_rows = cache_key_value[:, 1].reshape(
        request_batch, CACHE_SLOTS, KEY_VALUE_HEADS, HEAD_SIZE
    )
    incoming_key = incoming_pair[:, 0].reshape(request_batch, KEY_VALUE_HEADS, HEAD_SIZE)
    incoming_value = incoming_pair[:, 1].reshape(request_batch, KEY_VALUE_HEADS, HEAD_SIZE)
    scores = (
        jnp.einsum(
            "rkgd,rlkd->rkgl", query_head_rows, cache_key_rows, preferred_element_type=jnp.float32
        )
        * scaling
    )
    live_slot = jnp.arange(CACHE_SLOTS, dtype=jnp.int32)[None, :] < cache_length[:, None]
    scores = jnp.where(live_slot[:, None, None, :], scores, MASKED_SCORE)
    own_score = (
        jnp.einsum(
            "rkgd,rkd->rkg", query_head_rows, incoming_key, preferred_element_type=jnp.float32
        )
        * scaling
    )
    highest = jnp.maximum(jnp.max(scores, axis=-1), own_score)
    weights_cache = jnp.where(
        live_slot[:, None, None, :], jnp.exp(scores - highest[..., None]), 0.0
    )
    own_weight = jnp.exp(own_score - highest)
    totals = jnp.sum(weights_cache, axis=-1) + own_weight
    probs_cache = (weights_cache / totals[..., None]).astype(jnp.bfloat16)
    probs_own = (own_weight / totals).astype(jnp.bfloat16)
    mixed_values = jnp.einsum(
        "rkgl,rlkd->rkgd", probs_cache, cache_value_rows, preferred_element_type=jnp.float32
    )
    mixed_values = (
        mixed_values
        + probs_own.astype(jnp.float32)[..., None]
        * incoming_value.astype(jnp.float32)[:, :, None, :]
    )
    return mixed_values.reshape(request_batch, QUERY_HEADS * HEAD_SIZE).astype(jnp.bfloat16)


def per_device(
    queries,
    incoming_pair,
    cache_key_value,
    cache_length,
    out_weight,
    adapter_down,
    adapter_up,
    request_adapter,
    adapter_slot,
):
    attended = attend(queries, incoming_pair, cache_key_value, cache_length)
    adapters = adapter_slot.shape[0]
    matches = request_adapter[:, None] == jnp.arange(adapters, dtype=jnp.int32)[None, :]
    token_slot = jnp.sum(jnp.where(matches, adapter_slot[None, :], 0), axis=1)
    slot_wire = token_slot.astype(jnp.bfloat16)
    gathered, slot_all = (
        lax.all_gather(attended, "rep", axis=0, tiled=True),
        lax.all_gather(slot_wire, "rep", axis=0, tiled=True),
    )
    device = lax.axis_index("rep")
    own_slots = (device * ADP_DEV + jnp.arange(ADP_DEV, dtype=jnp.int32)).astype(jnp.float32)
    owned = slot_all.astype(jnp.float32)[:, None] == own_slots[None, :]
    shrink_terms = jnp.einsum(
        "td,adr->tar", gathered, adapter_down, preferred_element_type=jnp.float32
    )
    shrink_own = jnp.sum(jnp.where(owned[:, :, None], shrink_terms, 0.0), axis=1)
    head_width = out_weight.shape[0]
    masked = jnp.where(
        owned[:, :, None], shrink_own.astype(jnp.bfloat16)[:, None, :], jnp.zeros((), jnp.bfloat16)
    )
    head_block = lax.dynamic_slice_in_dim(gathered, device * head_width, head_width, 1)
    base_part = jnp.dot(head_block, out_weight, preferred_element_type=jnp.float32)
    delta_part = jnp.einsum("tar,ard->td", masked, adapter_up, preferred_element_type=jnp.float32)
    return lax.psum_scatter(
        base_part + ADAPTER_GAIN * delta_part, "rep", scatter_dimension=0, tiled=True
    ).astype(jnp.bfloat16)


def solution(mesh):
    in_specs = (
        P(("groups", "rep"), None),
        P(("groups", "rep"), None, None),
        P(("groups", "rep"), None, None, None),
        P(("groups", "rep")),
        P("rep", None),
        P(("groups", "rep"), None, None),
        P(("groups", "rep"), None, None),
        P(("groups", "rep")),
        P("groups"),
    )
    out_specs = P(("groups", "rep"), None)
    return jax.shard_map(
        per_device, mesh=mesh, in_specs=in_specs, out_specs=out_specs, check_vma=False
    )
```

profile of v0, /device:TPU:0, one launch (start us, length us, event | category | flops | bytes accessed | tf_op | source)
XLA Modules:
  0.0 161.0 jit_solution(2959169299717746279)
XLA Ops:
  6.5 0.0 copy-start
  6.5 0.0 all-gather.2.cloned.1.call-start
  6.5 0.9 iota_compare_fusion.1
  7.4 4.8 %fusion.24 = (bf16[8,1,128,1024]{3,2,1,0:T(8,128)(2,1)}, bf16[8,1,128,1024]{3,2,1,0:T(8,128)(2,1)}) fusion(bf16[8,2,128,1024]{3,2,1,0:T(8,128)(2,1)} %param.11), kind=kLoop, calls=%fused_computation.41 | loop fusion | bytes 8388608 | tf_op jit(solution)/shard_map/slice | solution.py:22
  12.2 0.0 copy-start.3
  12.2 0.0 copy-start.2
  12.2 4.0 %copy.25 = bf16[8,1,128,1024]{2,3,0,1:T(8,128)(2,1)} copy(bf16[8,1,128,1024]{3,2,1,0:T(8,128)(2,1)} %get-tuple-element.5) | data formatting | bytes 4194304
  16.2 0.0 copy-done.3
  16.3 0.0 copy-done.2
  16.3 0.2 fusion.10
  16.5 2.3 %fusion.25 = (f32[8,8,8]{2,1,0:T(8,128)S(1)}, f32[8,8,8,128]{3,2,1,0:T(8,128)S(1)}) fusion(bf16[8,128,8,128]{1,3,2,0:T(8,128)(2,1)} %bitcast.31, bf16[8,8,8,128]{3,0,2,1:T(8,128)(2,1)S(1)} %bitcast.36, pred[8,128]{1,0:T(8,128)(4,1)S(1)} %iota_compare_fusion.1), kind=kOutput, calls=%fused_computation.42 | convolution fusion | flops 16973312 | bytes 2493440 | tf_op jit(solution)/shard_map/rkgd,rlkd->rkgl/dot_general | solution.py:31
  18.8 0.3 fusion.4
  19.1 3.9 %copy.26 = bf16[8,1,128,1024]{2,3,0,1:T(8,128)(2,1)} copy(bf16[8,1,128,1024]{3,2,1,0:T(8,128)(2,1)} %get-tuple-element.6) | data formatting | bytes 4194304
  23.1 0.0 copy-start.4
  23.1 0.0 copy-start.5
  23.1 0.0 copy-start.6
  23.1 2.9 %fusion.3 = bf16[1,8,64,128]{3,2,1,0:T(8,128)(2,1)S(1)} fusion(bf16[8,128,8,128]{1,3,2,0:T(8,128)(2,1)} %bitcast.32, f32[8,8,8,128]{3,2,1,0:T(8,128)S(1)} %get-tuple-element.10, f32[8,8,128]{2,1,0:T(8,128)S(1)} %bitcast.39, f32[8,8,8]{2,1,0:T(8,128)S(1)} %get-tuple-element.8, f32[8,8,8]{2,1,0:T(8,128)S(1)} %get-tuple-element.7, ...), kind=kOutput, calls=%fused_computation.7 | convolution fusion | flops 17235968 | bytes 2530304 | tf_op jit(solution)/shard_map/rkgl,rlkd->rkgd/dot_general | solution.py:52
  25.9 0.8 copy.35
  26.7 0.0 all-gather.2.cloned.1.call-update
  26.7 0.0 reduce-scatter.2.cloned.1.call-start
  26.8 0.0 copy-done.4
  26.8 0.0 copy-done.5
  26.8 0.2 select_reduce_fusion.1
  27.0 0.0 copy-done.6
  27.0 0.7 dynamic-slice
  28.3 0.2 dynamic-update-slice
  28.6 35.2 %all-reduce = bf16[128]{0:T(256)(128)(2,1)S(1)} all-reduce(bf16[128]{0:T(256)(128)(2,1)S(1)} %dynamic-update-slice), channel_id=1, replica_groups=mesh['groups'=2,'rep'=16] {'rep'}, use_global_device_ids=true, to_apply=%add | all-reduce | flops 128 | bytes 512
  63.8 0.1 broadcast_compare_fusion
  63.9 7.0 %all-gather.2.cloned.1.call-done = bf16[128,8192]{1,0:T(8,128)(2,1)} async-done(((bf16[8,8192]{1,0:T(8,128)(2,1)}), bf16[128,8192]{1,0:T(8,128)(2,1)}) %all-gather.2.cloned.1.call-update) | async-done | bytes 2097168 | tf_op jit(solution)/shard_map/all_gather | solution.py:80
  70.9 0.0 copy-done
  70.9 0.0 copy-start.1
  70.9 2.4 %fusion.26 = f32[128,128]{0,1:S(1)} fusion(bf16[128,8192]{1,0:T(8,128)(2,1)} %all-gather.2.cloned.1.call-done, bf16[8192,128]{0,1:T(8,128)(2,1)S(1)} %bitcast.30), kind=kOutput, calls=%fused_computation.43 | convolution fusion | flops 268435456 | bytes 4259840
  73.4 0.0 copy-done.1
  73.4 0.7 fusion
  74.1 7.0 %convolution_add_fusion = f32[128,8192]{1,0:T(8,128)} fusion(f32[128,8192]{1,0:T(8,128)S(1)} %fusion, bf16[512,8192]{1,0:T(8,128)(2,1)} %param.13, bf16[128,8192]{1,0:T(8,128)(2,1)} %all-gather.2.cloned.1.call-done, s32[]{:T(128)S(6)} %select_n.24), kind=kOutput, calls=%fused_computation.1 | convolution fusion | flops 1074790400 | bytes 16908292 | tf_op jit(solution)/shard_map/dot_general | solution.py:95
  81.1 0.0 reduce-scatter.2.cloned.1.call-update
  81.1 71.4 %reduce-scatter.2.cloned.1.call-done = f32[8,8192]{1,0:T(8,128)} async-done(((f32[128,8192]{1,0:T(8,128)}), f32[8,8192]{1,0:T(8,128)}) %reduce-scatter.2.cloned.1.call-update) | async-done | bytes 262160 | tf_op jit(solution)/shard_map/reduce_scatter | solution.py:97
  152.5 1.6 %convert_element_type.59 = bf16[8,8192]{1,0:T(8,128)(2,1)} convert(f32[8,8192]{1,0:T(8,128)} %reduce-scatter.2.cloned.1.call-done) | non-fusion elementwise | flops 65536 | bytes 393216 | tf_op jit(solution)/shard_map/convert_element_type | solution.py:99
  (8 shorter events, 0.1 us)
Async XLA Ops:
  6.5 64.4 %copy-start = (bf16[2,8192,64]{1,2,0:T(8,128)(2,1)S(1)}, bf16[2,8192,64]{1,2,0:T(8,128)(2,1)}, u32[]{:S(2)}) copy-start(bf16[2,8192,64]{1,2,0:T(8,128)(2,1)} %param.14) | copy-start | bytes 6291460
  6.5 64.4 %all-gather.2.cloned.1.call-start = ((), (), s32[]{:S(2)}) async-start(), calls=%async_computation.1 | async-start | bytes 2228224 | tf_op jit(solution)/shard_map/all_gather | solution.py:80
  12.2 4.0 %copy-start.3 = (bf16[8,2,1024]{2,1,0:T(2,128)(2,1)S(1)}, bf16[8,2,1024]{2,1,0:T(2,128)(2,1)}, u32[]{:S(2)}) copy-start(bf16[8,2,1024]{2,1,0:T(2,128)(2,1)} %param.10) | copy-start | bytes 98308
  12.2 4.0 %copy-start.2 = (bf16[8,8192]{1,0:T(8,128)(2,1)S(1)}, bf16[8,8192]{1,0:T(8,128)(2,1)}, u32[]{:S(2)}) copy-start(bf16[8,8192]{1,0:T(8,128)(2,1)} %param.9) | copy-start | bytes 393220
  23.1 3.7 %copy-start.4 = (s32[32]{0:T(128)S(1)}, s32[32]{0:T(128)}, u32[]{:S(2)}) copy-start(s32[32]{0:T(128)} %param.17) | copy-start | bytes 388
  23.1 3.7 %copy-start.5 = (s32[8]{0:T(128)S(1)}, s32[8]{0:T(128)}, u32[]{:S(2)}) copy-start(s32[8]{0:T(128)} %param.16) | copy-start | bytes 100
  23.1 3.9 %copy-start.6 = (u32[32]{0:T(128)S(1)}, u32[32]{0:T(128)}, u32[]{:S(2)}) copy-start(u32[32]{0:T(128)} %constant.34) | copy-start | bytes 388
  26.7 125.8 %reduce-scatter.2.cloned.1.call-start = ((), (), s32[]{:S(2)}) async-start(), calls=%async_computation.2 | async-start | bytes 4456448 | tf_op jit(solution)/shard_map/reduce_scatter | solution.py:97
  70.9 2.5 %copy-start.1 = (bf16[2,64,8192]{2,1,0:T(8,128)(2,1)S(1)}, bf16[2,64,8192]{2,1,0:T(8,128)(2,1)}, u32[]{:S(2)}) copy-start(bf16[2,64,8192]{2,1,0:T(8,128)(2,1)} %param.15) | copy-start | bytes 6291460
Sparse Core Ops, SparseCore 0:
  26.8 44.0 all-gather.1
  81.2 71.2 reduce-scatter.1
where the time goes:
time: 161 us
  waiting for transfers between devices  78.5 us (49%)
  blocking collectives  35.2 us (22%)
  matrix products  15.5 us (10%)
  local copies, waits for them, and re-layouts  14.4 us (9%)
  between operations  14.2 us (9%)
  other arithmetic  3.12 us (2%)
    reduce_scatter x1, waiting for transfers between devices, per_device(): lax.psum_scatter(base_part + ADAPTER_GAIN * delta_part, 'rep', scatter_di...  71.4 us
    unnamed x1, blocking collectives  35.2 us
    unnamed x20, local copies, waits for them, and re-layouts  9.62 us
    all_gather x1, waiting for transfers between devices, per_device(): lax.all_gather(attended, 'rep', axis=0, tiled=True)  7.04 us
    dot_general x1, matrix products, per_device(): jnp.dot(head_block, out_weight, preferred_element_type=jnp.float32)  6.95 us
    slice x1, local copies, waits for them, and re-layouts, attend(): cache_key_value[:, 0]  4.8 us
  transfers between devices with their start and end apart: 2, of which 2 were waited for; matrix products, arithmetic and copies ran while one was open for 1% of the time, Pallas kernels for 0%

commit v1 on v0

v1 whole, which is shorter than its diff:
```python
import functools

import jax
import jax.numpy as jnp
from jax import lax
from jax.experimental import pallas as pl
from jax.experimental.pallas import tpu as pltpu
from jax.sharding import PartitionSpec as P

QUERY_HEADS = 64
KEY_VALUE_HEADS = 8
HEAD_SIZE = 128
GROUP = QUERY_HEADS // KEY_VALUE_HEADS
WIDTH = QUERY_HEADS * HEAD_SIZE
LANES = 128
ADAPTER_GAIN = 2.0
MASKED_SCORE = -1e30

CUT = 5632

NT = (((1,), (1,)), ((), ()))
VMEM = pl.BlockSpec(memory_space=pltpu.VMEM)
SMEM = pl.BlockSpec(memory_space=pltpu.SMEM)


def attend_kernel(
    length_ref, adapter_ref, slot_ref, query_ref, pair_ref, cache_ref,
    a_ref, b_ref, cache, spread, mixed, sems,
):
    requests = query_ref.shape[0]
    slots = cache.shape[2]

    def fetch(r):
        return pltpu.make_async_copy(cache_ref.at[r], cache.at[r], sems.at[r])

    for r in range(requests):
        fetch(r).start()
    scaling = HEAD_SIZE ** (-0.5)
    for h in range(QUERY_HEADS):
        spread[pl.ds(h, requests, stride=QUERY_HEADS), :] = query_ref[
            :, h * HEAD_SIZE : (h + 1) * HEAD_SIZE
        ].astype(jnp.float32)
    position = lax.broadcasted_iota(jnp.int32, (QUERY_HEADS, slots), 1)
    blank = jnp.zeros((GROUP, HEAD_SIZE), jnp.float32)
    pairs = KEY_VALUE_HEADS // 2
    for r in range(requests):
        rows = spread[r * QUERY_HEADS : (r + 1) * QUERY_HEADS, :]
        new = pair_ref[r].astype(jnp.float32)
        own_key = jnp.concatenate(
            [
                jnp.broadcast_to(new[0:1, k * HEAD_SIZE : (k + 1) * HEAD_SIZE], (GROUP, HEAD_SIZE))
                for k in range(KEY_VALUE_HEADS)
            ],
            axis=0,
        )
        own_score = jnp.sum(rows * own_key, axis=1, keepdims=True) * scaling
        fetch(r).wait()
        scores = []
        for j in range(pairs):
            upper = rows[2 * j * GROUP : (2 * j + 1) * GROUP]
            lower = rows[(2 * j + 1) * GROUP : (2 * j + 2) * GROUP]
            both = jnp.concatenate(
                [
                    jnp.concatenate([upper, blank], axis=1),
                    jnp.concatenate([blank, lower], axis=1),
                ],
                axis=0,
            ).astype(jnp.bfloat16)
            keys = cache[r, 0, :, 2 * j * HEAD_SIZE : (2 * j + 2) * HEAD_SIZE]
            scores.append(lax.dot_general(both, keys, NT, preferred_element_type=jnp.float32))
        score = jnp.concatenate(scores, axis=0) * scaling
        live = position < length_ref[r]
        score = jnp.where(live, score, MASKED_SCORE)
        top = jnp.maximum(jnp.max(score, axis=1, keepdims=True), own_score)
        weight = jnp.where(live, jnp.exp(score - top), 0.0)
        own_weight = jnp.exp(own_score - top)
        total = jnp.sum(weight, axis=1, keepdims=True) + own_weight
        prob = (weight / total).astype(jnp.bfloat16)
        own_prob = (own_weight / total).astype(jnp.bfloat16).astype(jnp.float32)
        outs = []
        for j in range(pairs):
            values = cache[r, 1, :, 2 * j * HEAD_SIZE : (2 * j + 2) * HEAD_SIZE]
            both = jnp.dot(
                prob[2 * j * GROUP : (2 * j + 2) * GROUP], values,
                preferred_element_type=jnp.float32,
            )
            outs += [both[:GROUP, :HEAD_SIZE], both[GROUP:, HEAD_SIZE:]]
        own_value = jnp.concatenate(
            [
                jnp.broadcast_to(new[1:2, k * HEAD_SIZE : (k + 1) * HEAD_SIZE], (GROUP, HEAD_SIZE))
                for k in range(KEY_VALUE_HEADS)
            ],
            axis=0,
        )
        mixed[r * QUERY_HEADS : (r + 1) * QUERY_HEADS, :] = (
            jnp.concatenate(outs, axis=0) + own_prob * own_value
        )
    for h in range(QUERY_HEADS):
        column = h * HEAD_SIZE
        out = mixed[pl.ds(h, requests, stride=QUERY_HEADS), :].astype(jnp.bfloat16)
        if column < a_ref.shape[1]:
            a_ref[:, column : column + HEAD_SIZE] = out
        else:
            column -= a_ref.shape[1]
            b_ref[:, column : column + HEAD_SIZE] = out
    row = lax.broadcasted_iota(jnp.int32, (requests, LANES), 0)
    tag = jnp.zeros((requests, LANES), jnp.int32)
    for r in range(requests):
        tag = jnp.where(row == r, slot_ref[adapter_ref[r]], tag)
    b_ref[:, b_ref.shape[1] - LANES :] = tag.astype(jnp.float32).astype(jnp.bfloat16)


def attend(queries, incoming_pair, cache_key_value, cache_length, request_adapter, adapter_slot):
    requests = queries.shape[0]
    bf16 = jnp.bfloat16
    return pl.pallas_call(
        attend_kernel,
        out_shape=(
            jax.ShapeDtypeStruct((requests, CUT), bf16),
            jax.ShapeDtypeStruct((requests, WIDTH - CUT + LANES), bf16),
        ),
        in_specs=[SMEM, SMEM, SMEM, VMEM, VMEM, pl.BlockSpec(memory_space=pl.ANY)],
        out_specs=(VMEM, VMEM),
        scratch_shapes=[
            pltpu.VMEM(cache_key_value.shape, bf16),
            pltpu.VMEM((requests * QUERY_HEADS, HEAD_SIZE), jnp.float32),
            pltpu.VMEM((requests * QUERY_HEADS, HEAD_SIZE), jnp.float32),
            pltpu.SemaphoreType.DMA((requests,)),
        ],
        compiler_params=pltpu.CompilerParams(vmem_limit_bytes=24 << 20),
        name="attend",
    )(cache_length, request_adapter, adapter_slot, queries, incoming_pair, cache_key_value)


def shrink_kernel(device_ref, rows_ref, other_ref, down_ref, head_ref, shrunk_ref):
    held, rank = down_ref.shape[0], down_ref.shape[1]
    half = rows_ref.shape[0]
    head = head_ref.shape[1]
    device = device_ref[0]
    down = down_ref[...].reshape(held * rank, WIDTH)
    start = pl.multiple_of(device * head, head)
    for i, ref in enumerate((rows_ref, other_ref)):
        at = slice(i * half, (i + 1) * half)
        terms = lax.dot_general(ref[:, :WIDTH], down, NT, preferred_element_type=jnp.float32)
        column = lax.broadcasted_iota(jnp.int32, (half, held * rank), 1)
        slot = ref[:, WIDTH : WIDTH + LANES].astype(jnp.float32)[:, :1]
        own = (device * held + column // rank).astype(jnp.float32)
        shrunk = jnp.where(slot == own, terms, 0.0).astype(jnp.bfloat16)
        shrunk_ref[at, :] = shrunk * jnp.bfloat16(ADAPTER_GAIN)
        head_ref[at, :] = ref[:, pl.ds(start, head)]


def shrink(device, rows, other, down, head):
    half = rows.shape[0]
    held, rank = down.shape[0], down.shape[1]
    bf16 = jnp.bfloat16
    return pl.pallas_call(
        shrink_kernel,
        out_shape=(
            jax.ShapeDtypeStruct((2 * half, head), bf16),
            jax.ShapeDtypeStruct((2 * half, held * rank), bf16),
        ),
        in_specs=[SMEM, VMEM, VMEM, VMEM],
        out_specs=(VMEM, VMEM),
        compiler_params=pltpu.CompilerParams(vmem_limit_bytes=24 << 20),
        name="shrink",
    )(device, rows, other, down)


def project_kernel(head_ref, shrunk_ref, weight_ref, up_ref, own_ref, other_ref):
    half = own_ref.shape[0]
    held, rank, tile = up_ref.shape
    out = jnp.dot(head_ref[...], weight_ref[...], preferred_element_type=jnp.float32)
    out += jnp.dot(
        shrunk_ref[...], up_ref[...].reshape(held * rank, tile),
        preferred_element_type=jnp.float32,
    )
    own_ref[...] = out[:half]
    other_ref[...] = out[half:].astype(jnp.bfloat16)


def project(head, shrunk, weight, up, first, columns, tile):
    rows = head.shape[0]
    half = rows // 2
    skip = first // tile
    held, rank = up.shape[0], up.shape[1]
    return pl.pallas_call(
        project_kernel,
        grid=(columns // tile,),
        out_shape=(
            jax.ShapeDtypeStruct((half, columns), jnp.float32),
            jax.ShapeDtypeStruct((half, columns), jnp.bfloat16),
        ),
        in_specs=[
            pl.BlockSpec(head.shape, lambda i: (0, 0)),
            pl.BlockSpec(shrunk.shape, lambda i: (0, 0)),
            pl.BlockSpec((weight.shape[0], tile), lambda i: (0, i + skip)),
            pl.BlockSpec((held, rank, tile), lambda i: (0, 0, i + skip)),
        ],
        out_specs=(
            pl.BlockSpec((half, tile), lambda i: (0, i)),
            pl.BlockSpec((half, tile), lambda i: (0, i)),
        ),
        compiler_params=pltpu.CompilerParams(vmem_limit_bytes=32 << 20),
        name="project",
    )(head, shrunk, weight, up)


def per_device(
    queries, incoming_pair, cache_key_value, cache_length, out_weight,
    adapter_down, adapter_up, request_adapter, adapter_slot, *, members,
):
    depths = members // 4
    f32, bf16 = jnp.float32, jnp.bfloat16

    def swap(x, mask):
        return lax.ppermute(x, "rep", [(i, i ^ mask) for i in range(members)])

    requests = queries.shape[0]
    a, b = attend(
        queries, incoming_pair, cache_key_value, cache_length, request_adapter, adapter_slot
    )

    b_sides = jnp.concatenate([b, swap(b, 2)], axis=0)
    a_depths = jnp.concatenate([a] + [swap(a, 4 * d) for d in range(1, depths)], axis=0)
    a_all = jnp.concatenate([a_depths, swap(a_depths, 2)], axis=0)
    b_all = jnp.stack([b_sides] + [swap(b_sides, 4 * d) for d in range(1, depths)], axis=0)
    b_all = jnp.swapaxes(b_all.reshape(depths, 2, requests, -1), 0, 1)
    rows = jnp.concatenate([a_all, b_all.reshape(2 * depths * requests, -1)], axis=1)
    other = swap(rows, 1)

    device = lax.axis_index("rep").astype(jnp.int32).reshape(1)
    head, shrunk = shrink(
        device, rows, other, jnp.swapaxes(adapter_down, 1, 2), out_weight.shape[0]
    )

    b_width = WIDTH - CUT
    b_own, b_other = project(head, shrunk, out_weight, adapter_up, CUT, b_width, 512)
    b_sum = (b_own + swap(b_other, 1).astype(f32)).reshape(2, depths, requests, b_width)
    a_own, a_other = project(head, shrunk, out_weight, adapter_up, 0, CUT, 512)
    b_send = b_sum.astype(bf16)
    b_part = b_sum[:, 0]
    for d in range(1, depths):
        b_part = b_part + swap(b_send[:, d], 4 * d).astype(f32)
    a_sum = (a_own + swap(a_other, 1).astype(f32)).reshape(2, depths, requests, CUT)
    a_part = a_sum[0] + swap(a_sum[1].astype(bf16), 2).astype(f32)
    a_send = a_part.astype(bf16)
    a_out = a_part[0]
    for d in range(1, depths):
        a_out = a_out + swap(a_send[d], 4 * d).astype(f32)
    b_out = b_part[0] + swap(b_part[1].astype(bf16), 2).astype(f32)
    return jnp.concatenate([a_out, b_out], axis=1).astype(bf16)


def solution(mesh):
    in_specs = (
        P(("groups", "rep"), None),
        P(("groups", "rep"), None, None),
        P(("groups", "rep"), None, None, None),
        P(("groups", "rep")),
        P("rep", None),
        P(("groups", "rep"), None, None),
        P(("groups", "rep"), None, None),
        P(("groups", "rep")),
        P("groups"),
    )
    out_specs = P(("groups", "rep"), None)
    return jax.shard_map(
        functools.partial(per_device, members=mesh.shape["rep"]),
        mesh=mesh, in_specs=in_specs, out_specs=out_specs, check_vma=False,
    )
```

time: 161 us -> 79.6 us (0.49)
  waiting for transfers between devices: 78.5 us -> 32.6 us
  blocking collectives: 35.2 us -> 0 us
  starting transfers between devices: 0.04 us -> 22.9 us
  matrix products: 15.5 us -> 0 us
  between operations: 14.2 us -> 0.21 us
  Pallas kernels: 0 us -> 13.1 us
  local copies, waits for them, and re-layouts: 14.4 us -> 9.36 us
  other arithmetic: 3.12 us -> 1.19 us
    reduce_scatter x1 -> x0, waiting for transfers between devices: 71.4 us -> none  [per_device(): lax.psum_scatter(base_part + ADAPTER_GAIN * delta_part, 'rep', scatter_di...]
    unnamed x1 -> x0, blocking collectives: 35.2 us -> none
    ppermute x0 -> x19, waiting for transfers between devices: none -> 32.6 us  [swap(): return lax.ppermute(x, 'rep', [(i, i ^ mask) for i in range(members)])]
    ppermute x0 -> x19, starting transfers between devices: none -> 22.9 us  [swap(): return lax.ppermute(x, 'rep', [(i, i ^ mask) for i in range(members)])]
    pallas_call x0 -> x4, Pallas kernels: none -> 13.1 us  [the longest x2 5.17 us: project(): pl.pallas_call(project_kernel, grid=(columns // tile,), out_shape=(jax.Sh...]
    dot_general x5 -> x0, matrix products: 13.1 us -> none  [the longest x1 6.95 us: per_device(): jnp.dot(head_block, out_weight, preferred_element_type=jnp.float32)]
    all_gather x1 -> x0, waiting for transfers between devices: 7.04 us -> none  [per_device(): lax.all_gather(attended, 'rep', axis=0, tiled=True)]
    slice x1 -> x0, local copies, waits for them, and re-layouts: 4.8 us -> none  [attend(): cache_key_value[:, 0]]
  transfers between devices with their start and end apart: 2 -> 19, of which waited for: 2 -> 12; matrix products, arithmetic and copies ran while one was open for 1% -> 0% of each run, Pallas kernels for 0% -> 4%
where the time goes in v1:
time: 79.6 us; the launch traced here: 79.3 us
  waiting for transfers between devices  32.6 us (41%)
  starting transfers between devices  22.9 us (29%)
  Pallas kernels  13.1 us (16%)
  local copies, waits for them, and re-layouts  9.36 us (12%)
  other arithmetic  1.19 us (1%)
    ppermute x19, waiting for transfers between devices, swap(): return lax.ppermute(x, 'rep', [(i, i ^ mask) for i in range(members)])  32.6 us
    ppermute x19, starting transfers between devices, swap(): return lax.ppermute(x, 'rep', [(i, i ^ mask) for i in range(members)])  22.9 us
    unnamed x23, local copies, waits for them, and re-layouts  9.23 us
    pallas_call x2, Pallas kernels, project(): pl.pallas_call(project_kernel, grid=(columns // tile,), out_shape=(jax.Sh...  5.17 us
    pallas_call x1, Pallas kernels, attend(): pl.pallas_call(attend_kernel, out_shape=(jax.ShapeDtypeStruct((requests,...  5 us
    pallas_call x1, Pallas kernels, shrink(): pl.pallas_call(shrink_kernel, out_shape=(jax.ShapeDtypeStruct((2 * half,...  2.92 us
  transfers between devices with their start and end apart: 19, of which 12 were waited for; matrix products, arithmetic and copies ran while one was open for 0% of the time, Pallas kernels for 4%

profile of v1, /device:TPU:0, one launch (start us, length us, event | category | flops | bytes accessed | tf_op | source)
XLA Modules:
  0.0 79.3 jit_solution(5273153730752316287)
XLA Ops:
  0.0 0.0 copy-start.2
  0.0 2.2 %copy-done.2 = bf16[8,2,128,1024]{3,2,1,0:T(8,128)(2,1)S(1)} copy-done((bf16[8,2,128,1024]{3,2,1,0:T(8,128)(2,1)S(1)}, bf16[8,2,128,1024]{3,2,1,0:T(8,128)(2,1)}, u32[]{:S(2)}) %copy-start.2) | copy-done | bytes 4194328
  2.2 0.0 copy-start.4
  2.2 0.9 %copy-done.4 = bf16[8,8192]{1,0:T(8,128)(2,1)S(1)} copy-done((bf16[8,8192]{1,0:T(8,128)(2,1)S(1)}, bf16[8,8192]{1,0:T(8,128)(2,1)}, u32[]{:S(2)}) %copy-start.4) | copy-done | bytes 131096
  3.1 0.0 copy-start.5
  3.1 0.8 copy-done.5
  3.9 0.0 copy-start.6
  3.9 0.7 copy-done.6
  4.5 0.7 copy-done.7
  5.2 0.0 copy-start.8
  5.2 0.7 copy-done.8
  5.8 5.0 %attend.1 = (bf16[8,5632]{1,0:T(8,128)(2,1)S(1)}, bf16[8,2688]{1,0:T(8,128)(2,1)S(1)}) custom-call(s32[8]{0:T(128)S(1)} %copy-done.6, s32[8]{0:T(128)S(1)} %copy-done.7, s32[32]{0:T(128)S(1)} %copy-done.8, bf16[8,8192]{1,0:T(8,128)(2,1)S(1)} %copy-done.4, bf16[8,2,1024]{2,1,0:T(2,128)(2,1)S(1)} %copy-done.5, bf16[8,2,128,1024]{3,2,1,0:T(8,128)(2,1)S(1)} %copy-done.2), custom_call_target="tpu_custom_call" | custom-call | tf_op jit(solution)/shard_map/attend/pallas_call | solution.py:116
  10.8 5.1 %collective-permute-start.2 = (bf16[8,5632]{1,0:T(8,128)(2,1)S(1)}, bf16[8,5632]{1,0:T(8,128)(2,1)S(1)}, u32[]{:S(2)}, u32[]{:S(2)}) collective-permute-start(bf16[8,5632]{1,0:T(8,128)(2,1)S(1)} %get-tuple-element.13), channel_id=1, source_target_pairs={{0,12},{1,13},{2,14},{3,15},{4,8},{5,9},{6,10},{7,11},{8,4},{9,5},... | collective-permute-start | bytes 270344 | tf_op jit(solution)/shard_map/ppermute | solution.py:217
  15.9 0.0 collective-permute-start.1
  15.9 0.6 collective-permute-start
  16.6 1.7 %collective-permute-start.4 = (bf16[8,2688]{1,0:T(8,128)(2,1)S(1)}, bf16[8,2688]{1,0:T(8,128)(2,1)S(1)}, u32[]{:S(2)}, u32[]{:S(2)}) collective-permute-start(bf16[8,2688]{1,0:T(8,128)(2,1)S(1)} %get-tuple-element.14), channel_id=1, source_target_pairs={{0,2},{1,3},{2,0},{3,1},{4,6},{5,7},{6,4},{7,5},{8,10},{9,11},{10,... | collective-permute-start | bytes 129032 | tf_op jit(solution)/shard_map/ppermute | solution.py:217
  18.3 2.3 %collective-permute-done.4 = bf16[8,2688]{1,0:T(8,128)(2,1)S(1)} collective-permute-done((bf16[8,2688]{1,0:T(8,128)(2,1)S(1)}, bf16[8,2688]{1,0:T(8,128)(2,1)S(1)}, u32[]{:S(2)}, u32[]{:S(2)}) %collective-permute-start.4) | collective-permute-done | bytes 43040 | tf_op jit(solution)/shard_map/ppermute | solution.py:217
  20.6 3.7 %collective-permute-start.7 = (bf16[16,2688]{1,0:T(8,128)(2,1)S(1)}, bf16[16,2688]{1,0:T(8,128)(2,1)S(1)}, u32[]{:S(2)}, u32[]{:S(2)}) collective-permute-start(bf16[16,2688]{1,0:T(8,128)(2,1)S(1)} %constant_dynamic-update-slice_fusion.5), channel_id=1, source_target_pairs={{0,12},{1,13},{2,14},{3,15},{4,8},{5,9},{6,10},{7,11},{8,4},{9,5},... | collective-permute-start | bytes 258056 | tf_op jit(solution)/shard_map/ppermute | solution.py:217
  24.4 0.0 collective-permute-start.6
  24.4 0.0 collective-permute-done.2
  24.4 0.6 collective-permute-start.5
  25.0 2.2 %collective-permute-done.1 = bf16[8,5632]{1,0:T(8,128)(2,1)S(1)} collective-permute-done((bf16[8,5632]{1,0:T(8,128)(2,1)S(1)}, bf16[8,5632]{1,0:T(8,128)(2,1)S(1)}, u32[]{:S(2)}, u32[]{:S(2)}) %collective-permute-start.1) | collective-permute-done | bytes 90144 | tf_op jit(solution)/shard_map/ppermute | solution.py:217
  27.2 0.0 collective-permute-done
  27.3 1.5 %collective-permute-start.3 = (bf16[32,5632]{1,0:T(8,128)(2,1)S(1)}, bf16[32,5632]{1,0:T(8,128)(2,1)S(1)}, u32[]{:S(2)}, u32[]{:S(2)}) collective-permute-start(bf16[32,5632]{1,0:T(8,128)(2,1)S(1)} %pad_maximum_fusion.1), channel_id=1, source_target_pairs={{0,2},{1,3},{2,0},{3,1},{4,6},{5,7},{6,4},{7,5},{8,10},{9,11},{10,... | collective-permute-start | bytes 1081352 | tf_op jit(solution)/shard_map/ppermute | solution.py:217
  28.8 0.0 collective-permute-done.7
  28.8 2.1 %collective-permute-done.6 = bf16[16,2688]{1,0:T(8,128)(2,1)S(1)} collective-permute-done((bf16[16,2688]{1,0:T(8,128)(2,1)S(1)}, bf16[16,2688]{1,0:T(8,128)(2,1)S(1)}, u32[]{:S(2)}, u32[]{:S(2)}) %collective-permute-start.6) | collective-permute-done | bytes 86048 | tf_op jit(solution)/shard_map/ppermute | solution.py:217
  30.9 0.0 collective-permute-done.5
  30.9 0.1 pad_maximum_fusion.2
  30.9 0.0 copy-start.3
  31.0 3.8 %collective-permute-done.3 = bf16[32,5632]{1,0:T(8,128)(2,1)S(1)} collective-permute-done((bf16[32,5632]{1,0:T(8,128)(2,1)S(1)}, bf16[32,5632]{1,0:T(8,128)(2,1)S(1)}, u32[]{:S(2)}, u32[]{:S(2)}) %collective-permute-start.3) | collective-permute-done | bytes 360480 | tf_op jit(solution)/shard_map/ppermute | solution.py:217
  34.8 0.1 pad_maximum_fusion.rows_ref
  34.9 0.1 collective-permute-start.8
  34.9 2.8 %collective-permute-done.8.other_ref = bf16[64,8320]{1,0:T(8,128)(2,1)} collective-permute-done((bf16[64,8320]{1,0:T(8,128)(2,1)S(1)}, bf16[64,8320]{1,0:T(8,128)(2,1)}, u32[]{:S(2)}, u32[]{:S(2)}) %collective-permute-start.8) | collective-permute-done | bytes 1064992 | tf_op jit(solution)/shard_map/ppermute | solution.py:217
  37.7 0.0 copy-done.3
  37.7 2.9 %shrink.1 = (bf16[128,512]{1,0:T(8,128)(2,1)S(1)}, bf16[128,128]{1,0:T(8,128)(2,1)S(1)}) custom-call(s32[1]{0:T(128)} %bitcast.device_ref, bf16[64,8320]{1,0:T(8,128)(2,1)S(1)} %pad_maximum_fusion.rows_ref, bf16[64,8320]{1,0:T(8,128)(2,1)} %collective-permute-done.8.other_ref, bf16[2,64,8192]{2,1,0:T(8,128)(2,1)S(1)} %bitcast.63), custom_call_target="tpu_custom_call" | custom-call | tf_op jit(solution)/shard_map/shrink/pallas_call | solution.py:157
  40.7 0.0 copy-done.1
  40.7 0.0 copy-start
  40.7 3.4 %copy-done = bf16[512,8192]{1,0:T(8,128)(2,1)S(1)} copy-done((bf16[512,8192]{1,0:T(8,128)(2,1)S(1)}, bf16[512,8192]{1,0:T(8,128)(2,1)}, u32[]{:S(2)}) %copy-start) | copy-done | bytes 8388632
  44.1 1.6 %project.3 = (f32[64,2560]{1,0:T(8,128)S(1)}, bf16[64,2560]{1,0:T(8,128)(2,1)S(1)}) custom-call(bf16[128,512]{1,0:T(8,128)(2,1)S(1)} %get-tuple-element.15.head_ref, bf16[128,128]{1,0:T(8,128)(2,1)S(1)} %get-tuple-element.16.shrunk_ref, bf16[512,8192]{1,0:T(8,128)(2,1)S(1)} %copy-done, bf16[2,64,8192]{2,1,0:T(8,128)(2,1)S(1)} %copy-done.1), custom_call_target="tpu_custom_call" | custom-call | tf_op jit(solution)/shard_map/project/pallas_call | solution.py:187
  45.7 0.2 collective-permute-start.14
  45.9 1.5 %collective-permute-done.14 = bf16[64,2560]{1,0:T(8,128)(2,1)S(1)} collective-permute-done((bf16[64,2560]{1,0:T(8,128)(2,1)S(1)}, bf16[64,2560]{1,0:T(8,128)(2,1)S(1)}, u32[]{:S(2)}, u32[]{:S(2)}) %collective-permute-start.14) | collective-permute-done | bytes 327712 | tf_op jit(solution)/shard_map/ppermute | solution.py:217
  47.4 0.1 convert_add_fusion.1
  47.5 0.1 collective-permute-start.15
  47.6 2.0 %collective-permute-start.17 = (bf16[2,8,2560]{2,1,0:T(8,128)(2,1)S(1)}, bf16[2,8,2560]{2,1,0:T(8,128)(2,1)S(1)}, u32[]{:S(2)}, u32[]{:S(2)}) collective-permute-start(bf16[2,8,2560]{2,1,0:T(8,128)(2,1)S(1)} %get-tuple-element.27), channel_id=1, source_target_pairs={{0,12},{1,13},{2,14},{3,15},{4,8},{5,9},{6,10},{7,11},{8,4},{9,5},... | collective-permute-start | bytes 245768 | tf_op jit(solution)/shard_map/ppermute | solution.py:217
  49.6 1.5 %collective-permute-start.16 = (bf16[2,8,2560]{2,1,0:T(8,128)(2,1)S(1)}, bf16[2,8,2560]{2,1,0:T(8,128)(2,1)S(1)}, u32[]{:S(2)}, u32[]{:S(2)}) collective-permute-start(bf16[2,8,2560]{2,1,0:T(8,128)(2,1)S(1)} %get-tuple-element.28), channel_id=1, source_target_pairs={{0,8},{1,9},{2,10},{3,11},{4,12},{5,13},{6,14},{7,15},{8,0},{9,1},... | collective-permute-start | bytes 245768 | tf_op jit(solution)/shard_map/ppermute | solution.py:217
  51.1 3.5 %project.2 = (f32[64,5632]{1,0:T(8,128)S(1)}, bf16[64,5632]{1,0:T(8,128)(2,1)S(1)}) custom-call(bf16[128,512]{1,0:T(8,128)(2,1)S(1)} %get-tuple-element.15.head_ref, bf16[128,128]{1,0:T(8,128)(2,1)S(1)} %get-tuple-element.16.shrunk_ref, bf16[512,8192]{1,0:T(8,128)(2,1)S(1)} %copy-done, bf16[2,64,8192]{2,1,0:T(8,128)(2,1)S(1)} %copy-done.1), custom_call_target="tpu_custom_call" | custom-call | tf_op jit(solution)/shard_map/project/pallas_call | solution.py:187
  54.6 0.1 collective-permute-start.9
  54.7 0.0 collective-permute-done.15
  54.7 0.1 collective-permute-done.17
  54.8 3.7 %collective-permute-done.16 = bf16[2,8,2560]{2,1,0:T(8,128)(2,1)S(1)} collective-permute-done((bf16[2,8,2560]{2,1,0:T(8,128)(2,1)S(1)}, bf16[2,8,2560]{2,1,0:T(8,128)(2,1)S(1)}, u32[]{:S(2)}, u32[]{:S(2)}) %collective-permute-start.16) | collective-permute-done | bytes 81952 | tf_op jit(solution)/shard_map/ppermute | solution.py:217
  58.5 0.0 collective-permute-done.9
  58.6 0.1 convert_add_fusion
  58.8 1.5 %collective-permute-start.10 = (bf16[4,8,5632]{2,1,0:T(8,128)(2,1)S(1)}, bf16[4,8,5632]{2,1,0:T(8,128)(2,1)S(1)}, u32[]{:S(2)}, u32[]{:S(2)}) collective-permute-start(bf16[4,8,5632]{2,1,0:T(8,128)(2,1)S(1)} %fusion.1), channel_id=1, source_target_pairs={{0,2},{1,3},{2,0},{3,1},{4,6},{5,7},{6,4},{7,5},{8,10},{9,11},{10,... | collective-permute-start | bytes 1081352 | tf_op jit(solution)/shard_map/ppermute | solution.py:217
  60.3 0.6 collective-permute-start.18
  60.9 8.0 %collective-permute-done.10 = bf16[4,8,5632]{2,1,0:T(8,128)(2,1)S(1)} collective-permute-done((bf16[4,8,5632]{2,1,0:T(8,128)(2,1)S(1)}, bf16[4,8,5632]{2,1,0:T(8,128)(2,1)S(1)}, u32[]{:S(2)}, u32[]{:S(2)}) %collective-permute-start.10) | collective-permute-done | bytes 360480 | tf_op jit(solution)/shard_map/ppermute | solution.py:217
  68.9 0.1 fusion.12
  69.0 0.2 collective-permute-start.11
  69.2 1.9 %collective-permute-start.13 = (bf16[8,5632]{1,0:T(8,128)(2,1)S(1)}, bf16[8,5632]{1,0:T(8,128)(2,1)S(1)}, u32[]{:S(2)}, u32[]{:S(2)}) collective-permute-start(bf16[8,5632]{1,0:T(8,128)(2,1)S(1)} %get-tuple-element.24), channel_id=1, source_target_pairs={{0,12},{1,13},{2,14},{3,15},{4,8},{5,9},{6,10},{7,11},{8,4},{9,5},... | collective-permute-start | bytes 270344 | tf_op jit(solution)/shard_map/ppermute | solution.py:217
  71.1 1.4 %collective-permute-start.12 = (bf16[8,5632]{1,0:T(8,128)(2,1)S(1)}, bf16[8,5632]{1,0:T(8,128)(2,1)S(1)}, u32[]{:S(2)}, u32[]{:S(2)}) collective-permute-start(bf16[8,5632]{1,0:T(8,128)(2,1)S(1)} %get-tuple-element.25), channel_id=1, source_target_pairs={{0,8},{1,9},{2,10},{3,11},{4,12},{5,13},{6,14},{7,15},{8,0},{9,1},... | collective-permute-start | bytes 270344 | tf_op jit(solution)/shard_map/ppermute | solution.py:217
  72.5 0.0 collective-permute-done.18
  72.6 1.9 %collective-permute-done.11 = bf16[8,5632]{1,0:T(8,128)(2,1)S(1)} collective-permute-done((bf16[8,5632]{1,0:T(8,128)(2,1)S(1)}, bf16[8,5632]{1,0:T(8,128)(2,1)S(1)}, u32[]{:S(2)}, u32[]{:S(2)}) %collective-permute-start.11) | collective-permute-done | bytes 90144 | tf_op jit(solution)/shard_map/ppermute | solution.py:217
  74.5 1.2 %collective-permute-done.13 = bf16[8,5632]{1,0:T(8,128)(2,1)S(1)} collective-permute-done((bf16[8,5632]{1,0:T(8,128)(2,1)S(1)}, bf16[8,5632]{1,0:T(8,128)(2,1)S(1)}, u32[]{:S(2)}, u32[]{:S(2)}) %collective-permute-start.13) | collective-permute-done | bytes 90144 | tf_op jit(solution)/shard_map/ppermute | solution.py:217
  75.7 2.9 %collective-permute-done.12 = bf16[8,5632]{1,0:T(8,128)(2,1)S(1)} collective-permute-done((bf16[8,5632]{1,0:T(8,128)(2,1)S(1)}, bf16[8,5632]{1,0:T(8,128)(2,1)S(1)}, u32[]{:S(2)}, u32[]{:S(2)}) %collective-permute-start.12) | collective-permute-done | bytes 90144 | tf_op jit(solution)/shard_map/ppermute | solution.py:217
  78.6 0.7 pad_maximum_fusion.3
  (17 shorter events, 0.3 us)
Async XLA Ops:
  0.0 2.2 %copy-start.2 = (bf16[8,2,128,1024]{3,2,1,0:T(8,128)(2,1)S(1)}, bf16[8,2,128,1024]{3,2,1,0:T(8,128)(2,1)}, u32[]{:S(2)}) copy-start(bf16[8,2,128,1024]{3,2,1,0:T(8,128)(2,1)} %cache_ref.1) | copy-start | bytes 12582916
  2.2 0.9 %copy-start.4 = (bf16[8,8192]{1,0:T(8,128)(2,1)S(1)}, bf16[8,8192]{1,0:T(8,128)(2,1)}, u32[]{:S(2)}) copy-start(bf16[8,8192]{1,0:T(8,128)(2,1)} %query_ref.1) | copy-start | bytes 393220
  3.1 0.8 copy-start.5
  3.9 0.7 copy-start.6
  4.5 0.7 copy-start.7
  5.2 0.7 copy-start.8
  10.8 13.5 %collective-permute-start.2 = (bf16[8,5632]{1,0:T(8,128)(2,1)S(1)}, bf16[8,5632]{1,0:T(8,128)(2,1)S(1)}, u32[]{:S(2)}, u32[]{:S(2)}) collective-permute-start(bf16[8,5632]{1,0:T(8,128)(2,1)S(1)} %get-tuple-element.13), channel_id=1, source_target_pairs={{0,12},{1,13},{2,14},{3,15},{4,8},{5,9},{6,10},{7,11},{8,4},{9,5},... | collective-permute-start | bytes 270344 | tf_op jit(solution)/shard_map/ppermute | solution.py:217
  15.9 11.3 %collective-permute-start.1 = (bf16[8,5632]{1,0:T(8,128)(2,1)S(1)}, bf16[8,5632]{1,0:T(8,128)(2,1)S(1)}, u32[]{:S(2)}, u32[]{:S(2)}) collective-permute-start(bf16[8,5632]{1,0:T(8,128)(2,1)S(1)} %get-tuple-element.13), channel_id=1, source_target_pairs={{0,8},{1,9},{2,10},{3,11},{4,12},{5,13},{6,14},{7,15},{8,0},{9,1},... | collective-permute-start | bytes 270344 | tf_op jit(solution)/shard_map/ppermute | solution.py:217
  15.9 11.3 %collective-permute-start = (bf16[8,5632]{1,0:T(8,128)(2,1)S(1)}, bf16[8,5632]{1,0:T(8,128)(2,1)S(1)}, u32[]{:S(2)}, u32[]{:S(2)}) collective-permute-start(bf16[8,5632]{1,0:T(8,128)(2,1)S(1)} %get-tuple-element.13), channel_id=1, source_target_pairs={{0,4},{1,5},{2,6},{3,7},{4,0},{5,1},{6,2},{7,3},{8,12},{9,13},{10,... | collective-permute-start | bytes 270344 | tf_op jit(solution)/shard_map/ppermute | solution.py:217
  16.6 4.0 %collective-permute-start.4 = (bf16[8,2688]{1,0:T(8,128)(2,1)S(1)}, bf16[8,2688]{1,0:T(8,128)(2,1)S(1)}, u32[]{:S(2)}, u32[]{:S(2)}) collective-permute-start(bf16[8,2688]{1,0:T(8,128)(2,1)S(1)} %get-tuple-element.14), channel_id=1, source_target_pairs={{0,2},{1,3},{2,0},{3,1},{4,6},{5,7},{6,4},{7,5},{8,10},{9,11},{10,... | collective-permute-start | bytes 129032 | tf_op jit(solution)/shard_map/ppermute | solution.py:217
  20.6 8.2 %collective-permute-start.7 = (bf16[16,2688]{1,0:T(8,128)(2,1)S(1)}, bf16[16,2688]{1,0:T(8,128)(2,1)S(1)}, u32[]{:S(2)}, u32[]{:S(2)}) collective-permute-start(bf16[16,2688]{1,0:T(8,128)(2,1)S(1)} %constant_dynamic-update-slice_fusion.5), channel_id=1, source_target_pairs={{0,12},{1,13},{2,14},{3,15},{4,8},{5,9},{6,10},{7,11},{8,4},{9,5},... | collective-permute-start | bytes 258056 | tf_op jit(solution)/shard_map/ppermute | solution.py:217
  24.4 6.5 %collective-permute-start.6 = (bf16[16,2688]{1,0:T(8,128)(2,1)S(1)}, bf16[16,2688]{1,0:T(8,128)(2,1)S(1)}, u32[]{:S(2)}, u32[]{:S(2)}) collective-permute-start(bf16[16,2688]{1,0:T(8,128)(2,1)S(1)} %constant_dynamic-update-slice_fusion.5), channel_id=1, source_target_pairs={{0,8},{1,9},{2,10},{3,11},{4,12},{5,13},{6,14},{7,15},{8,0},{9,1},... | collective-permute-start | bytes 258056 | tf_op jit(solution)/shard_map/ppermute | solution.py:217
  24.4 6.5 %collective-permute-start.5 = (bf16[16,2688]{1,0:T(8,128)(2,1)S(1)}, bf16[16,2688]{1,0:T(8,128)(2,1)S(1)}, u32[]{:S(2)}, u32[]{:S(2)}) collective-permute-start(bf16[16,2688]{1,0:T(8,128)(2,1)S(1)} %constant_dynamic-update-slice_fusion.5), channel_id=1, source_target_pairs={{0,4},{1,5},{2,6},{3,7},{4,0},{5,1},{6,2},{7,3},{8,12},{9,13},{10,... | collective-permute-start | bytes 258056 | tf_op jit(solution)/shard_map/ppermute | solution.py:217
  27.3 7.5 %collective-permute-start.3 = (bf16[32,5632]{1,0:T(8,128)(2,1)S(1)}, bf16[32,5632]{1,0:T(8,128)(2,1)S(1)}, u32[]{:S(2)}, u32[]{:S(2)}) collective-permute-start(bf16[32,5632]{1,0:T(8,128)(2,1)S(1)} %pad_maximum_fusion.1), channel_id=1, source_target_pairs={{0,2},{1,3},{2,0},{3,1},{4,6},{5,7},{6,4},{7,5},{8,10},{9,11},{10,... | collective-permute-start | bytes 1081352 | tf_op jit(solution)/shard_map/ppermute | solution.py:217
  30.9 6.8 %copy-start.3 = (bf16[2,8192,64]{1,2,0:T(8,128)(2,1)S(1)}, bf16[2,8192,64]{1,2,0:T(8,128)(2,1)}, u32[]{:S(2)}) copy-start(bf16[2,8192,64]{1,2,0:T(8,128)(2,1)} %param.14) | copy-start | bytes 6291460
  34.9 2.9 %collective-permute-start.8 = (bf16[64,8320]{1,0:T(8,128)(2,1)S(1)}, bf16[64,8320]{1,0:T(8,128)(2,1)}, u32[]{:S(2)}, u32[]{:S(2)}) collective-permute-start(bf16[64,8320]{1,0:T(8,128)(2,1)S(1)} %pad_maximum_fusion.rows_ref), channel_id=1, source_target_pairs={{0,1},{1,0},{2,3},{3,2},{4,5},{5,4},{6,7},{7,6},{8,9},{9,8},{10,11... | collective-permute-start | bytes 3194888 | tf_op jit(solution)/shard_map/ppermute | solution.py:217
  37.7 2.9 %copy-start.1 = (bf16[2,64,8192]{2,1,0:T(8,128)(2,1)S(1)}, bf16[2,64,8192]{2,1,0:T(8,128)(2,1)}, u32[]{:S(2)}) copy-start(bf16[2,64,8192]{2,1,0:T(8,128)(2,1)} %up_ref.3) | copy-start | bytes 6291460
  40.7 3.4 %copy-start = (bf16[512,8192]{1,0:T(8,128)(2,1)S(1)}, bf16[512,8192]{1,0:T(8,128)(2,1)}, u32[]{:S(2)}) copy-start(bf16[512,8192]{1,0:T(8,128)(2,1)} %weight_ref.3) | copy-start | bytes 25165828
  45.7 1.7 %collective-permute-start.14 = (bf16[64,2560]{1,0:T(8,128)(2,1)S(1)}, bf16[64,2560]{1,0:T(8,128)(2,1)S(1)}, u32[]{:S(2)}, u32[]{:S(2)}) collective-permute-start(bf16[64,2560]{1,0:T(8,128)(2,1)S(1)} %get-tuple-element.20), channel_id=1, source_target_pairs={{0,1},{1,0},{2,3},{3,2},{4,5},{5,4},{6,7},{7,6},{8,9},{9,8},{10,11... | collective-permute-start | bytes 983048 | tf_op jit(solution)/shard_map/ppermute | solution.py:217
  47.5 7.2 %collective-permute-start.15 = (bf16[2,8,2560]{2,1,0:T(8,128)(2,1)S(1)}, bf16[2,8,2560]{2,1,0:T(8,128)(2,1)S(1)}, u32[]{:S(2)}, u32[]{:S(2)}) collective-permute-start(bf16[2,8,2560]{2,1,0:T(8,128)(2,1)S(1)} %get-tuple-element.26), channel_id=1, source_target_pairs={{0,4},{1,5},{2,6},{3,7},{4,0},{5,1},{6,2},{7,3},{8,12},{9,13},{10,... | collective-permute-start | bytes 245768 | tf_op jit(solution)/shard_map/ppermute | solution.py:217
  47.6 7.3 %collective-permute-start.17 = (bf16[2,8,2560]{2,1,0:T(8,128)(2,1)S(1)}, bf16[2,8,2560]{2,1,0:T(8,128)(2,1)S(1)}, u32[]{:S(2)}, u32[]{:S(2)}) collective-permute-start(bf16[2,8,2560]{2,1,0:T(8,128)(2,1)S(1)} %get-tuple-element.27), channel_id=1, source_target_pairs={{0,12},{1,13},{2,14},{3,15},{4,8},{5,9},{6,10},{7,11},{8,4},{9,5},... | collective-permute-start | bytes 245768 | tf_op jit(solution)/shard_map/ppermute | solution.py:217
  49.6 8.9 %collective-permute-start.16 = (bf16[2,8,2560]{2,1,0:T(8,128)(2,1)S(1)}, bf16[2,8,2560]{2,1,0:T(8,128)(2,1)S(1)}, u32[]{:S(2)}, u32[]{:S(2)}) collective-permute-start(bf16[2,8,2560]{2,1,0:T(8,128)(2,1)S(1)} %get-tuple-element.28), channel_id=1, source_target_pairs={{0,8},{1,9},{2,10},{3,11},{4,12},{5,13},{6,14},{7,15},{8,0},{9,1},... | collective-permute-start | bytes 245768 | tf_op jit(solution)/shard_map/ppermute | solution.py:217
  54.6 3.9 %collective-permute-start.9 = (bf16[64,5632]{1,0:T(8,128)(2,1)S(1)}, bf16[64,5632]{1,0:T(8,128)(2,1)S(1)}, u32[]{:S(2)}, u32[]{:S(2)}) collective-permute-start(bf16[64,5632]{1,0:T(8,128)(2,1)S(1)} %get-tuple-element.18), channel_id=1, source_target_pairs={{0,1},{1,0},{2,3},{3,2},{4,5},{5,4},{6,7},{7,6},{8,9},{9,8},{10,11... | collective-permute-start | bytes 2162696 | tf_op jit(solution)/shard_map/ppermute | solution.py:217
  58.8 10.1 %collective-permute-start.10 = (bf16[4,8,5632]{2,1,0:T(8,128)(2,1)S(1)}, bf16[4,8,5632]{2,1,0:T(8,128)(2,1)S(1)}, u32[]{:S(2)}, u32[]{:S(2)}) collective-permute-start(bf16[4,8,5632]{2,1,0:T(8,128)(2,1)S(1)} %fusion.1), channel_id=1, source_target_pairs={{0,2},{1,3},{2,0},{3,1},{4,6},{5,7},{6,4},{7,5},{8,10},{9,11},{10,... | collective-permute-start | bytes 1081352 | tf_op jit(solution)/shard_map/ppermute | solution.py:217
  60.3 12.3 %collective-permute-start.18 = (bf16[8,2560]{1,0:T(8,128)(2,1)S(1)}, bf16[8,2560]{1,0:T(8,128)(2,1)S(1)}, u32[]{:S(2)}, u32[]{:S(2)}) collective-permute-start(bf16[8,2560]{1,0:T(8,128)(2,1)S(1)} %fusion.11), channel_id=1, source_target_pairs={{0,2},{1,3},{2,0},{3,1},{4,6},{5,7},{6,4},{7,5},{8,10},{9,11},{10,... | collective-permute-start | bytes 122888 | tf_op jit(solution)/shard_map/ppermute | solution.py:217
  69.0 5.5 %collective-permute-start.11 = (bf16[8,5632]{1,0:T(8,128)(2,1)S(1)}, bf16[8,5632]{1,0:T(8,128)(2,1)S(1)}, u32[]{:S(2)}, u32[]{:S(2)}) collective-permute-start(bf16[8,5632]{1,0:T(8,128)(2,1)S(1)} %get-tuple-element.23), channel_id=1, source_target_pairs={{0,4},{1,5},{2,6},{3,7},{4,0},{5,1},{6,2},{7,3},{8,12},{9,13},{10,... | collective-permute-start | bytes 270344 | tf_op jit(solution)/shard_map/ppermute | solution.py:217
  69.2 6.6 %collective-permute-start.13 = (bf16[8,5632]{1,0:T(8,128)(2,1)S(1)}, bf16[8,5632]{1,0:T(8,128)(2,1)S(1)}, u32[]{:S(2)}, u32[]{:S(2)}) collective-permute-start(bf16[8,5632]{1,0:T(8,128)(2,1)S(1)} %get-tuple-element.24), channel_id=1, source_target_pairs={{0,12},{1,13},{2,14},{3,15},{4,8},{5,9},{6,10},{7,11},{8,4},{9,5},... | collective-permute-start | bytes 270344 | tf_op jit(solution)/shard_map/ppermute | solution.py:217
  71.1 7.5 %collective-permute-start.12 = (bf16[8,5632]{1,0:T(8,128)(2,1)S(1)}, bf16[8,5632]{1,0:T(8,128)(2,1)S(1)}, u32[]{:S(2)}, u32[]{:S(2)}) collective-permute-start(bf16[8,5632]{1,0:T(8,128)(2,1)S(1)} %get-tuple-element.25), channel_id=1, source_target_pairs={{0,8},{1,9},{2,10},{3,11},{4,12},{5,13},{6,14},{7,15},{8,0},{9,1},... | collective-permute-start | bytes 270344 | tf_op jit(solution)/shard_map/ppermute | solution.py:217

commit v2 on v1

--- a/solution.py
+++ b/solution.py
@@ -20,21 +20,43 @@
 
 NT = (((1,), (1,)), ((), ()))
 VMEM = pl.BlockSpec(memory_space=pltpu.VMEM)
+HBM = pl.BlockSpec(memory_space=pltpu.HBM)
 SMEM = pl.BlockSpec(memory_space=pltpu.SMEM)
 
 
+def held_in_vmem(x):
+    return pltpu.with_memory_space_constraint(x, pltpu.VMEM)
+
+
+def cost(flops, size):
+    return pl.CostEstimate(flops=flops, bytes_accessed=size, transcendentals=0)
+
+
 def attend_kernel(
-    length_ref, adapter_ref, slot_ref, query_ref, pair_ref, cache_ref,
-    a_ref, b_ref, cache, spread, mixed, sems,
+    length_hbm, adapter_hbm, slot_hbm, query_hbm, pair_hbm, cache_hbm, a_ref, b_ref,
+    length_ref, adapter_ref, slot_ref, query_ref, pair_ref, cache, spread, mixed, sems,
 ):
     requests = query_ref.shape[0]
     slots = cache.shape[2]
 
     def fetch(r):
-        return pltpu.make_async_copy(cache_ref.at[r], cache.at[r], sems.at[r])
-
+        return pltpu.make_async_copy(cache_hbm.at[r], cache.at[r], sems.at[r])
+
+    small = [
+        pltpu.make_async_copy(source, target, sems.at[requests + i])
+        for i, (source, target) in enumerate(
+            (
+                (query_hbm, query_ref), (pair_hbm, pair_ref), (length_hbm, length_ref),
+                (adapter_hbm, adapter_ref), (slot_hbm, slot_ref),
+            )
+        )
+    ]
+    for copy in small:
+        copy.start()
     for r in range(requests):
         fetch(r).start()
+    for copy in small:
+        copy.wait()
     scaling = HEAD_SIZE ** (-0.5)
     for h in range(QUERY_HEADS):
         spread[pl.ds(h, requests, stride=QUERY_HEADS), :] = query_ref[
@@ -112,98 +134,96 @@
 
 def attend(queries, incoming_pair, cache_key_value, cache_length, request_adapter, adapter_slot):
     requests = queries.shape[0]
-    bf16 = jnp.bfloat16
+    bf16, f32 = jnp.bfloat16, jnp.float32
+    ints = (cache_length, request_adapter, adapter_slot)
+    inputs = ints + (queries, incoming_pair, cache_key_value)
     return pl.pallas_call(
         attend_kernel,
         out_shape=(
-            jax.ShapeDtypeStruct((requests, CUT), bf16),
-            jax.ShapeDtypeStruct((requests, WIDTH - CUT + LANES), bf16),
+            pltpu.VMEM((requests, CUT), bf16),
+            pltpu.VMEM((requests, WIDTH - CUT + LANES), bf16),
         ),
-        in_specs=[SMEM, SMEM, SMEM, VMEM, VMEM, pl.BlockSpec(memory_space=pl.ANY)],
-        out_specs=(VMEM, VMEM),
-        scratch_shapes=[
+        in_specs=[HBM] * 6,
+        out_specs=(VMEM,) * 2,
+        scratch_shapes=[pltpu.SMEM(x.shape, jnp.int32) for x in ints]
+        + [
+            pltpu.VMEM(queries.shape, bf16),
+            pltpu.VMEM(incoming_pair.shape, bf16),
             pltpu.VMEM(cache_key_value.shape, bf16),
-            pltpu.VMEM((requests * QUERY_HEADS, HEAD_SIZE), jnp.float32),
-            pltpu.VMEM((requests * QUERY_HEADS, HEAD_SIZE), jnp.float32),
-            pltpu.SemaphoreType.DMA((requests,)),
+            pltpu.VMEM((requests * QUERY_HEADS, HEAD_SIZE), f32),
+            pltpu.VMEM((requests * QUERY_HEADS, HEAD_SIZE), f32),
+            pltpu.SemaphoreType.DMA((requests + 5,)),
         ],
-        compiler_params=pltpu.CompilerParams(vmem_limit_bytes=24 << 20),
+        compiler_params=pltpu.CompilerParams(vmem_limit_bytes=20 << 20),
+        cost_estimate=cost(10**9, 2 * cache_key_value.size),
         name="attend",
-    )(cache_length, request_adapter, adapter_slot, queries, incoming_pair, cache_key_value)
-
-
-def shrink_kernel(device_ref, rows_ref, other_ref, down_ref, head_ref, shrunk_ref):
+    )(*(pltpu.with_memory_space_constraint(x, pltpu.HBM) for x in inputs))
+
+
+def shrink_kernel(device_ref, rows_ref, down_ref, down_other_ref, own_ref, other_ref):
     held, rank = down_ref.shape[0], down_ref.shape[1]
     half = rows_ref.shape[0]
-    head = head_ref.shape[1]
-    device = device_ref[0]
-    down = down_ref[...].reshape(held * rank, WIDTH)
-    start = pl.multiple_of(device * head, head)
-    for i, ref in enumerate((rows_ref, other_ref)):
-        at = slice(i * half, (i + 1) * half)
-        terms = lax.dot_general(ref[:, :WIDTH], down, NT, preferred_element_type=jnp.float32)
-        column = lax.broadcasted_iota(jnp.int32, (half, held * rank), 1)
-        slot = ref[:, WIDTH : WIDTH + LANES].astype(jnp.float32)[:, :1]
-        own = (device * held + column // rank).astype(jnp.float32)
-        shrunk = jnp.where(slot == own, terms, 0.0).astype(jnp.bfloat16)
-        shrunk_ref[at, :] = shrunk * jnp.bfloat16(ADAPTER_GAIN)
-        head_ref[at, :] = ref[:, pl.ds(start, head)]
-
-
-def shrink(device, rows, other, down, head):
+    ranks = held * rank
+    head = own_ref.shape[1] - ranks
+    me = device_ref[0]
+    slot = rows_ref[:, WIDTH : WIDTH + LANES].astype(jnp.float32)[:, :1]
+    column = lax.broadcasted_iota(jnp.int32, (half, ranks), 1)
+    for device, factor, ref in ((me, down_ref, own_ref), (me ^ 1, down_other_ref, other_ref)):
+        terms = lax.dot_general(
+            rows_ref[:, :WIDTH], factor[...].reshape(ranks, WIDTH), NT,
+            preferred_element_type=jnp.float32,
+        )
+        owned = (device * held + column // rank).astype(jnp.float32)
+        shrunk = jnp.where(slot == owned, terms, 0.0).astype(jnp.bfloat16)
+        ref[:, head:] = shrunk * jnp.bfloat16(ADAPTER_GAIN)
+        ref[:, :head] = rows_ref[:, pl.ds(pl.multiple_of(device * head, head), head)]
+
+
+def shrink(device, rows, down, down_other, head):
     half = rows.shape[0]
-    held, rank = down.shape[0], down.shape[1]
-    bf16 = jnp.bfloat16
+    ranks = down.shape[0] * down.shape[1]
+    out = jax.ShapeDtypeStruct((half, head + ranks), jnp.bfloat16)
     return pl.pallas_call(
         shrink_kernel,
-        out_shape=(
-            jax.ShapeDtypeStruct((2 * half, head), bf16),
-            jax.ShapeDtypeStruct((2 * half, held * rank), bf16),
-        ),
+        out_shape=(out, out),
         in_specs=[SMEM, VMEM, VMEM, VMEM],
         out_specs=(VMEM, VMEM),
-        compiler_params=pltpu.CompilerParams(vmem_limit_bytes=24 << 20),
+        compiler_params=pltpu.CompilerParams(vmem_limit_bytes=16 << 20),
+        cost_estimate=cost(4 * half * ranks * WIDTH, 4 * ranks * WIDTH),
         name="shrink",
-    )(device, rows, other, down)
-
-
-def project_kernel(head_ref, shrunk_ref, weight_ref, up_ref, own_ref, other_ref):
-    half = own_ref.shape[0]
-    held, rank, tile = up_ref.shape
-    out = jnp.dot(head_ref[...], weight_ref[...], preferred_element_type=jnp.float32)
-    out += jnp.dot(
-        shrunk_ref[...], up_ref[...].reshape(held * rank, tile),
-        preferred_element_type=jnp.float32,
-    )
-    own_ref[...] = out[:half]
-    other_ref[...] = out[half:].astype(jnp.bfloat16)
-
-
-def project(head, shrunk, weight, up, first, columns, tile):
-    rows = head.shape[0]
-    half = rows // 2
-    skip = first // tile
-    held, rank = up.shape[0], up.shape[1]
+    )(device, rows, held_in_vmem(down), down_other)
+
+
+def project_kernel(tile, x_ref, x_other_ref, weight_ref, up_ref, own_ref, other_ref):
+    half, columns = own_ref.shape
+    held, rank, _ = up_ref.shape
+    head = weight_ref.shape[0]
+    x = jnp.concatenate([x_other_ref[...], x_ref[...]], axis=0)
+    for start in range(0, columns, tile):
+        at = slice(start, start + tile)
+        out = jnp.dot(x[:, :head], weight_ref[:, at], preferred_element_type=jnp.float32)
+        out += jnp.dot(
+            x[:, head:], up_ref[:, :, at].reshape(held * rank, tile),
+            preferred_element_type=jnp.float32,
+        )
+        other_ref[:, at] = out[:half].astype(jnp.bfloat16)
+        own_ref[:, at] = out[half:]
+
+
+def project(x, x_other, weight, up):
+    half, columns = x.shape[0], weight.shape[1]
     return pl.pallas_call(
-        project_kernel,
-        grid=(columns // tile,),
+        functools.partial(project_kernel, 512),
         out_shape=(
             jax.ShapeDtypeStruct((half, columns), jnp.float32),
             jax.ShapeDtypeStruct((half, columns), jnp.bfloat16),
         ),
-        in_specs=[
-            pl.BlockSpec(head.shape, lambda i: (0, 0)),
-            pl.BlockSpec(shrunk.shape, lambda i: (0, 0)),
-            pl.BlockSpec((weight.shape[0], tile), lambda i: (0, i + skip)),
-            pl.BlockSpec((held, rank, tile), lambda i: (0, 0, i + skip)),
-        ],
-        out_specs=(
-            pl.BlockSpec((half, tile), lambda i: (0, i)),
-            pl.BlockSpec((half, tile), lambda i: (0, i)),
-        ),
-        compiler_params=pltpu.CompilerParams(vmem_limit_bytes=32 << 20),
+        in_specs=[VMEM] * 4,
+        out_specs=(VMEM, VMEM),
+        compiler_params=pltpu.CompilerParams(vmem_limit_bytes=16 << 20),
+        cost_estimate=cost(4 * half * x.shape[1] * columns, 2 * x.shape[1] * columns),
         name="project",
-    )(head, shrunk, weight, up)
+    )(x, x_other, held_in_vmem(weight), held_in_vmem(up))
 
 
 def per_device(
@@ -217,6 +237,8 @@
         return lax.ppermute(x, "rep", [(i, i ^ mask) for i in range(members)])
 
     requests = queries.shape[0]
+    down = jnp.swapaxes(adapter_down, 1, 2)
+    down_other = swap(down, 1)
     a, b = attend(
         queries, incoming_pair, cache_key_value, cache_length, request_adapter, adapter_slot
     )
@@ -227,23 +249,19 @@
     b_all = jnp.stack([b_sides] + [swap(b_sides, 4 * d) for d in range(1, depths)], axis=0)
     b_all = jnp.swapaxes(b_all.reshape(depths, 2, requests, -1), 0, 1)
     rows = jnp.concatenate([a_all, b_all.reshape(2 * depths * requests, -1)], axis=1)
-    other = swap(rows, 1)
 
     device = lax.axis_index("rep").astype(jnp.int32).reshape(1)
-    head, shrunk = shrink(
-        device, rows, other, jnp.swapaxes(adapter_down, 1, 2), out_weight.shape[0]
-    )
-
-    b_width = WIDTH - CUT
-    b_own, b_other = project(head, shrunk, out_weight, adapter_up, CUT, b_width, 512)
-    b_sum = (b_own + swap(b_other, 1).astype(f32)).reshape(2, depths, requests, b_width)
-    a_own, a_other = project(head, shrunk, out_weight, adapter_up, 0, CUT, 512)
+    x, x_send = shrink(device, rows, down, down_other, out_weight.shape[0])
+    x_other = swap(x_send, 1)
+
+    own, send = project(x, x_other, out_weight, adapter_up)
+    sums = (own + swap(send, 1).astype(f32)).reshape(2, depths, requests, WIDTH)
+    a_sum, b_sum = sums[..., :CUT], sums[..., CUT:]
+    a_part = a_sum[0] + swap(a_sum[1].astype(bf16), 2).astype(f32)
     b_send = b_sum.astype(bf16)
     b_part = b_sum[:, 0]
     for d in range(1, depths):
         b_part = b_part + swap(b_send[:, d], 4 * d).astype(f32)
-    a_sum = (a_own + swap(a_other, 1).astype(f32)).reshape(2, depths, requests, CUT)
-    a_part = a_sum[0] + swap(a_sum[1].astype(bf16), 2).astype(f32)
     a_send = a_part.astype(bf16)
     a_out = a_part[0]
     for d in range(1, depths):

time: 79.6 us -> 66.9 us (0.84)
  local copies, waits for them, and re-layouts: 9.36 us -> 1.76 us
  waiting for transfers between devices: 32.6 us -> 28.7 us
  Pallas kernels: 13.1 us -> 10.3 us
  starting transfers between devices: 22.9 us -> 24.6 us
    unnamed x23 -> x11, local copies, waits for them, and re-layouts: 9.23 us -> 1.63 us
    ppermute x19, waiting for transfers between devices: 32.6 us -> 28.7 us  [swap(): return lax.ppermute(x, 'rep', [(i, i ^ mask) for i in range(members)])]
    pallas_call x4 -> x3, Pallas kernels: 13.1 us -> 10.3 us  [the longest x1 5.28 us: attend(): pl.pallas_call(attend_kernel, out_shape=(pltpu.VMEM((requests, CUT), bf16...]
    ppermute x19, starting transfers between devices: 22.9 us -> 24.6 us  [swap(): return lax.ppermute(x, 'rep', [(i, i ^ mask) for i in range(members)])]
  transfers between devices with their start and end apart: 19 -> 19, of which waited for: 12 -> 13; matrix products, arithmetic and copies ran while one was open for 0% -> 1% of each run, Pallas kernels for 4% -> 0%
where the time goes in v2:
time: 66.9 us; the launch traced here: 66.7 us
  waiting for transfers between devices  28.7 us (43%)
  starting transfers between devices  24.6 us (37%)
  Pallas kernels  10.3 us (15%)
  local copies, waits for them, and re-layouts  1.76 us (3%)
  other arithmetic  1.25 us (2%)
    ppermute x19, waiting for transfers between devices, swap(): return lax.ppermute(x, 'rep', [(i, i ^ mask) for i in range(members)])  28.7 us
    ppermute x19, starting transfers between devices, swap(): return lax.ppermute(x, 'rep', [(i, i ^ mask) for i in range(members)])  24.6 us
    pallas_call x1, Pallas kernels, attend(): pl.pallas_call(attend_kernel, out_shape=(pltpu.VMEM((requests, CUT), bf16...  5.28 us
    pallas_call x1, Pallas kernels, shrink(): pl.pallas_call(shrink_kernel, out_shape=(out, out), in_specs=[SMEM, VMEM,...  3.14 us
    pallas_call x1, Pallas kernels, project(): pl.pallas_call(functools.partial(project_kernel, 512), out_shape=(jax.Sha...  1.83 us
    unnamed x11, local copies, waits for them, and re-layouts  1.63 us
  transfers between devices with their start and end apart: 19, of which 13 were waited for; matrix products, arithmetic and copies ran while one was open for 1% of the time, Pallas kernels for 0%

profile of v2, /device:TPU:0, one launch (start us, length us, event | category | flops | bytes accessed | tf_op | source)
XLA Modules:
  0.0 66.7 jit_solution(11133943813271868407)
XLA Ops:
  0.0 0.0 copy-start.1
  0.0 5.3 %attend.1 = (bf16[8,5632]{1,0:T(8,128)(2,1)S(1)}, bf16[8,2688]{1,0:T(8,128)(2,1)S(1)}) custom-call(s32[8]{0:T(128)} %length_hbm.1, s32[8]{0:T(128)} %adapter_hbm.1, s32[32]{0:T(128)} %slot_hbm.1, bf16[8,8192]{1,0:T(8,128)(2,1)} %query_hbm.1, bf16[8,2,1024]{2,1,0:T(2,128)(2,1)} %pair_hbm.1, bf16[8,2,128,1024]{3,2,1,0:T(8,128)(2,1)} %cache_hbm.1), custom_call_target="tpu_custom_call" | custom-call | flops 1000000000 | bytes 4194304 | tf_op jit(solution)/shard_map/attend/pallas_call | solution.py:140
  5.3 5.1 %collective-permute-start.2 = (bf16[8,5632]{1,0:T(8,128)(2,1)S(1)}, bf16[8,5632]{1,0:T(8,128)(2,1)S(1)}, u32[]{:S(2)}, u32[]{:S(2)}) collective-permute-start(bf16[8,5632]{1,0:T(8,128)(2,1)S(1)} %get-tuple-element.11), channel_id=1, source_target_pairs={{0,12},{1,13},{2,14},{3,15},{4,8},{5,9},{6,10},{7,11},{8,4},{9,5},... | collective-permute-start | bytes 270344 | tf_op jit(solution)/shard_map/ppermute | solution.py:237
  10.4 0.0 collective-permute-start.1
  10.4 0.6 collective-permute-start
  11.1 1.7 %collective-permute-start.4 = (bf16[8,2688]{1,0:T(8,128)(2,1)S(1)}, bf16[8,2688]{1,0:T(8,128)(2,1)S(1)}, u32[]{:S(2)}, u32[]{:S(2)}) collective-permute-start(bf16[8,2688]{1,0:T(8,128)(2,1)S(1)} %get-tuple-element.12), channel_id=1, source_target_pairs={{0,2},{1,3},{2,0},{3,1},{4,6},{5,7},{6,4},{7,5},{8,10},{9,11},{10,... | collective-permute-start | bytes 129032 | tf_op jit(solution)/shard_map/ppermute | solution.py:237
  12.7 0.0 copy-done.1
  12.7 0.0 collective-permute-start.8
  12.7 2.3 %collective-permute-done.4 = bf16[8,2688]{1,0:T(8,128)(2,1)S(1)} collective-permute-done((bf16[8,2688]{1,0:T(8,128)(2,1)S(1)}, bf16[8,2688]{1,0:T(8,128)(2,1)S(1)}, u32[]{:S(2)}, u32[]{:S(2)}) %collective-permute-start.4) | collective-permute-done | bytes 43040 | tf_op jit(solution)/shard_map/ppermute | solution.py:237
  15.1 3.7 %collective-permute-start.7 = (bf16[16,2688]{1,0:T(8,128)(2,1)S(1)}, bf16[16,2688]{1,0:T(8,128)(2,1)S(1)}, u32[]{:S(2)}, u32[]{:S(2)}) collective-permute-start(bf16[16,2688]{1,0:T(8,128)(2,1)S(1)} %constant_dynamic-update-slice_fusion.5), channel_id=1, source_target_pairs={{0,12},{1,13},{2,14},{3,15},{4,8},{5,9},{6,10},{7,11},{8,4},{9,5},... | collective-permute-start | bytes 258056 | tf_op jit(solution)/shard_map/ppermute | solution.py:237
  18.8 0.0 collective-permute-done.2
  18.8 0.0 collective-permute-start.6
  18.8 2.9 %collective-permute-done.1 = bf16[8,5632]{1,0:T(8,128)(2,1)S(1)} collective-permute-done((bf16[8,5632]{1,0:T(8,128)(2,1)S(1)}, bf16[8,5632]{1,0:T(8,128)(2,1)S(1)}, u32[]{:S(2)}, u32[]{:S(2)}) %collective-permute-start.1) | collective-permute-done | bytes 90144 | tf_op jit(solution)/shard_map/ppermute | solution.py:237
  21.7 0.0 collective-permute-start.5
  21.7 0.0 collective-permute-done
  21.7 1.6 %collective-permute-start.3 = (bf16[32,5632]{1,0:T(8,128)(2,1)S(1)}, bf16[32,5632]{1,0:T(8,128)(2,1)S(1)}, u32[]{:S(2)}, u32[]{:S(2)}) collective-permute-start(bf16[32,5632]{1,0:T(8,128)(2,1)S(1)} %pad_maximum_fusion.1), channel_id=1, source_target_pairs={{0,2},{1,3},{2,0},{3,1},{4,6},{5,7},{6,4},{7,5},{8,10},{9,11},{10,... | collective-permute-start | bytes 1081352 | tf_op jit(solution)/shard_map/ppermute | solution.py:237
  23.3 0.0 collective-permute-done.7
  23.3 2.0 %collective-permute-done.6 = bf16[16,2688]{1,0:T(8,128)(2,1)S(1)} collective-permute-done((bf16[16,2688]{1,0:T(8,128)(2,1)S(1)}, bf16[16,2688]{1,0:T(8,128)(2,1)S(1)}, u32[]{:S(2)}, u32[]{:S(2)}) %collective-permute-start.6) | collective-permute-done | bytes 86048 | tf_op jit(solution)/shard_map/ppermute | solution.py:237
  25.4 0.9 %collective-permute-done.5 = bf16[16,2688]{1,0:T(8,128)(2,1)S(1)} collective-permute-done((bf16[16,2688]{1,0:T(8,128)(2,1)S(1)}, bf16[16,2688]{1,0:T(8,128)(2,1)S(1)}, u32[]{:S(2)}, u32[]{:S(2)}) %collective-permute-start.5) | collective-permute-done | bytes 86048 | tf_op jit(solution)/shard_map/ppermute | solution.py:237
  26.3 0.0 copy-start
  26.3 0.1 pad_maximum_fusion.2
  26.3 2.9 %collective-permute-done.3 = bf16[32,5632]{1,0:T(8,128)(2,1)S(1)} collective-permute-done((bf16[32,5632]{1,0:T(8,128)(2,1)S(1)}, bf16[32,5632]{1,0:T(8,128)(2,1)S(1)}, u32[]{:S(2)}, u32[]{:S(2)}) %collective-permute-start.3) | collective-permute-done | bytes 360480 | tf_op jit(solution)/shard_map/ppermute | solution.py:237
  29.3 0.1 pad_maximum_fusion.rows_ref
  29.3 0.0 collective-permute-done.8.down_other_ref
  29.4 3.1 %shrink.1 = (bf16[64,640]{1,0:T(8,128)(2,1)S(1)}, bf16[64,640]{1,0:T(8,128)(2,1)S(1)}) custom-call(s32[1]{0:T(128)} %bitcast.device_ref, bf16[64,8320]{1,0:T(8,128)(2,1)S(1)} %pad_maximum_fusion.rows_ref, bf16[2,64,8192]{2,1,0:T(8,128)(2,1)S(1)} %bitcast.64, bf16[2,64,8192]{2,1,0:T(8,128)(2,1)} %collective-permute-done.8.down_other_ref), custom_call_target="tpu_custom_call" | custom-call | flops 268435456 | bytes 4194304 | tf_op jit(solution)/shard_map/shrink/pallas_call | solution.py:186
  32.5 0.1 collective-permute-start.9
  32.6 1.3 %collective-permute-done.9.x_other_ref = bf16[64,640]{1,0:T(8,128)(2,1)S(1)} collective-permute-done((bf16[64,640]{1,0:T(8,128)(2,1)S(1)}, bf16[64,640]{1,0:T(8,128)(2,1)S(1)}, u32[]{:S(2)}, u32[]{:S(2)}) %collective-permute-start.9) | collective-permute-done | bytes 81952 | tf_op jit(solution)/shard_map/ppermute | solution.py:237
  33.8 0.0 copy-done
  33.8 0.0 copy-start.2
  33.8 1.6 %copy-done.2 = bf16[2,64,8192]{2,1,0:T(8,128)(2,1)S(1)} copy-done((bf16[2,64,8192]{2,1,0:T(8,128)(2,1)S(1)}, bf16[2,64,8192]{2,1,0:T(8,128)(2,1)}, u32[]{:S(2)}) %copy-start.2) | copy-done | bytes 2097176
  35.4 1.8 %project.1 = (f32[64,8192]{1,0:T(8,128)S(1)}, bf16[64,8192]{1,0:T(8,128)(2,1)S(1)}) custom-call(bf16[64,640]{1,0:T(8,128)(2,1)S(1)} %get-tuple-element.13.x_ref, bf16[64,640]{1,0:T(8,128)(2,1)S(1)} %collective-permute-done.9.x_other_ref, bf16[512,8192]{1,0:T(8,128)(2,1)S(1)} %copy-done, bf16[2,64,8192]{2,1,0:T(8,128)(2,1)S(1)} %copy-done.2), custom_call_target="tpu_custom_call" | custom-call | flops 1342177280 | bytes 10485760 | tf_op jit(solution)/shard_map/project/pallas_call | solution.py:215
  37.3 0.2 collective-permute-start.10
  37.5 2.5 %collective-permute-done.10 = bf16[64,8192]{1,0:T(8,128)(2,1)S(1)} collective-permute-done((bf16[64,8192]{1,0:T(8,128)(2,1)S(1)}, bf16[64,8192]{1,0:T(8,128)(2,1)S(1)}, u32[]{:S(2)}, u32[]{:S(2)}) %collective-permute-start.10) | collective-permute-done | bytes 1048608 | tf_op jit(solution)/shard_map/ppermute | solution.py:237
  40.0 0.2 convert_add_fusion
  40.3 2.1 %collective-permute-start.15 = (bf16[2,8,2560]{2,1,0:T(8,128)(2,1)S(1)}, bf16[2,8,2560]{2,1,0:T(8,128)(2,1)S(1)}, u32[]{:S(2)}, u32[]{:S(2)}) collective-permute-start(bf16[2,8,2560]{2,1,0:T(8,128)(2,1)S(1)} %get-tuple-element.19), channel_id=1, source_target_pairs={{0,4},{1,5},{2,6},{3,7},{4,0},{5,1},{6,2},{7,3},{8,12},{9,13},{10,... | collective-permute-start | bytes 245768 | tf_op jit(solution)/shard_map/ppermute | solution.py:237
  42.4 1.7 %collective-permute-start.17 = (bf16[2,8,2560]{2,1,0:T(8,128)(2,1)S(1)}, bf16[2,8,2560]{2,1,0:T(8,128)(2,1)S(1)}, u32[]{:S(2)}, u32[]{:S(2)}) collective-permute-start(bf16[2,8,2560]{2,1,0:T(8,128)(2,1)S(1)} %get-tuple-element.20), channel_id=1, source_target_pairs={{0,12},{1,13},{2,14},{3,15},{4,8},{5,9},{6,10},{7,11},{8,4},{9,5},... | collective-permute-start | bytes 245768 | tf_op jit(solution)/shard_map/ppermute | solution.py:237
  44.1 0.0 collective-permute-start.16
  44.1 1.6 %collective-permute-start.11 = (bf16[4,8,5632]{2,1,0:T(8,128)(2,1)S(1)}, bf16[4,8,5632]{2,1,0:T(8,128)(2,1)S(1)}, u32[]{:S(2)}, u32[]{:S(2)}) collective-permute-start(bf16[4,8,5632]{2,1,0:T(8,128)(2,1)S(1)} %slice_bitcast_fusion.1), channel_id=1, source_target_pairs={{0,2},{1,3},{2,0},{3,1},{4,6},{5,7},{6,4},{7,5},{8,10},{9,11},{10,... | collective-permute-start | bytes 1081352 | tf_op jit(solution)/shard_map/ppermute | solution.py:237
  45.7 0.0 collective-permute-done.15
  45.7 3.7 %collective-permute-done.17 = bf16[2,8,2560]{2,1,0:T(8,128)(2,1)S(1)} collective-permute-done((bf16[2,8,2560]{2,1,0:T(8,128)(2,1)S(1)}, bf16[2,8,2560]{2,1,0:T(8,128)(2,1)S(1)}, u32[]{:S(2)}, u32[]{:S(2)}) %collective-permute-start.17) | collective-permute-done | bytes 81952 | tf_op jit(solution)/shard_map/ppermute | solution.py:237
  49.4 2.5 %collective-permute-done.16 = bf16[2,8,2560]{2,1,0:T(8,128)(2,1)S(1)} collective-permute-done((bf16[2,8,2560]{2,1,0:T(8,128)(2,1)S(1)}, bf16[2,8,2560]{2,1,0:T(8,128)(2,1)S(1)}, u32[]{:S(2)}, u32[]{:S(2)}) %collective-permute-start.16) | collective-permute-done | bytes 81952 | tf_op jit(solution)/shard_map/ppermute | solution.py:237
  52.0 1.6 %collective-permute-start.18 = (bf16[8,2560]{1,0:T(8,128)(2,1)S(1)}, bf16[8,2560]{1,0:T(8,128)(2,1)S(1)}, u32[]{:S(2)}, u32[]{:S(2)}) collective-permute-start(bf16[8,2560]{1,0:T(8,128)(2,1)S(1)} %fusion.10), channel_id=1, source_target_pairs={{0,2},{1,3},{2,0},{3,1},{4,6},{5,7},{6,4},{7,5},{8,10},{9,11},{10,... | collective-permute-start | bytes 122888 | tf_op jit(solution)/shard_map/ppermute | solution.py:237
  53.5 0.6 collective-permute-done.11
  54.1 0.1 fusion.11
  54.2 2.9 %collective-permute-start.12 = (bf16[8,5632]{1,0:T(8,128)(2,1)S(1)}, bf16[8,5632]{1,0:T(8,128)(2,1)S(1)}, u32[]{:S(2)}, u32[]{:S(2)}) collective-permute-start(bf16[8,5632]{1,0:T(8,128)(2,1)S(1)} %get-tuple-element.22), channel_id=1, source_target_pairs={{0,4},{1,5},{2,6},{3,7},{4,0},{5,1},{6,2},{7,3},{8,12},{9,13},{10,... | collective-permute-start | bytes 270344 | tf_op jit(solution)/shard_map/ppermute | solution.py:237
  57.1 1.7 %collective-permute-start.14 = (bf16[8,5632]{1,0:T(8,128)(2,1)S(1)}, bf16[8,5632]{1,0:T(8,128)(2,1)S(1)}, u32[]{:S(2)}, u32[]{:S(2)}) collective-permute-start(bf16[8,5632]{1,0:T(8,128)(2,1)S(1)} %get-tuple-element.23), channel_id=1, source_target_pairs={{0,12},{1,13},{2,14},{3,15},{4,8},{5,9},{6,10},{7,11},{8,4},{9,5},... | collective-permute-start | bytes 270344 | tf_op jit(solution)/shard_map/ppermute | solution.py:237
  58.8 0.0 collective-permute-start.13
  58.8 0.0 collective-permute-done.18
  58.9 1.8 %collective-permute-done.12 = bf16[8,5632]{1,0:T(8,128)(2,1)S(1)} collective-permute-done((bf16[8,5632]{1,0:T(8,128)(2,1)S(1)}, bf16[8,5632]{1,0:T(8,128)(2,1)S(1)}, u32[]{:S(2)}, u32[]{:S(2)}) %collective-permute-start.12) | collective-permute-done | bytes 90144 | tf_op jit(solution)/shard_map/ppermute | solution.py:237
  60.6 2.9 %collective-permute-done.14 = bf16[8,5632]{1,0:T(8,128)(2,1)S(1)} collective-permute-done((bf16[8,5632]{1,0:T(8,128)(2,1)S(1)}, bf16[8,5632]{1,0:T(8,128)(2,1)S(1)}, u32[]{:S(2)}, u32[]{:S(2)}) %collective-permute-start.14) | collective-permute-done | bytes 90144 | tf_op jit(solution)/shard_map/ppermute | solution.py:237
  63.5 2.4 %collective-permute-done.13 = bf16[8,5632]{1,0:T(8,128)(2,1)S(1)} collective-permute-done((bf16[8,5632]{1,0:T(8,128)(2,1)S(1)}, bf16[8,5632]{1,0:T(8,128)(2,1)S(1)}, u32[]{:S(2)}, u32[]{:S(2)}) %collective-permute-start.13) | collective-permute-done | bytes 90144 | tf_op jit(solution)/shard_map/ppermute | solution.py:237
  66.0 0.7 pad_maximum_fusion.3
  (15 shorter events, 0.3 us)
Async XLA Ops:
  0.0 12.7 %copy-start.1 = (bf16[2,8192,64]{1,2,0:T(8,128)(2,1)S(1)}, bf16[2,8192,64]{1,2,0:T(8,128)(2,1)}, u32[]{:S(2)}) copy-start(bf16[2,8192,64]{1,2,0:T(8,128)(2,1)} %param.14) | copy-start | bytes 6291460
  5.3 13.5 %collective-permute-start.2 = (bf16[8,5632]{1,0:T(8,128)(2,1)S(1)}, bf16[8,5632]{1,0:T(8,128)(2,1)S(1)}, u32[]{:S(2)}, u32[]{:S(2)}) collective-permute-start(bf16[8,5632]{1,0:T(8,128)(2,1)S(1)} %get-tuple-element.11), channel_id=1, source_target_pairs={{0,12},{1,13},{2,14},{3,15},{4,8},{5,9},{6,10},{7,11},{8,4},{9,5},... | collective-permute-start | bytes 270344 | tf_op jit(solution)/shard_map/ppermute | solution.py:237
  10.4 11.3 %collective-permute-start.1 = (bf16[8,5632]{1,0:T(8,128)(2,1)S(1)}, bf16[8,5632]{1,0:T(8,128)(2,1)S(1)}, u32[]{:S(2)}, u32[]{:S(2)}) collective-permute-start(bf16[8,5632]{1,0:T(8,128)(2,1)S(1)} %get-tuple-element.11), channel_id=1, source_target_pairs={{0,8},{1,9},{2,10},{3,11},{4,12},{5,13},{6,14},{7,15},{8,0},{9,1},... | collective-permute-start | bytes 270344 | tf_op jit(solution)/shard_map/ppermute | solution.py:237
  10.4 11.3 %collective-permute-start = (bf16[8,5632]{1,0:T(8,128)(2,1)S(1)}, bf16[8,5632]{1,0:T(8,128)(2,1)S(1)}, u32[]{:S(2)}, u32[]{:S(2)}) collective-permute-start(bf16[8,5632]{1,0:T(8,128)(2,1)S(1)} %get-tuple-element.11), channel_id=1, source_target_pairs={{0,4},{1,5},{2,6},{3,7},{4,0},{5,1},{6,2},{7,3},{8,12},{9,13},{10,... | collective-permute-start | bytes 270344 | tf_op jit(solution)/shard_map/ppermute | solution.py:237
  11.1 4.0 %collective-permute-start.4 = (bf16[8,2688]{1,0:T(8,128)(2,1)S(1)}, bf16[8,2688]{1,0:T(8,128)(2,1)S(1)}, u32[]{:S(2)}, u32[]{:S(2)}) collective-permute-start(bf16[8,2688]{1,0:T(8,128)(2,1)S(1)} %get-tuple-element.12), channel_id=1, source_target_pairs={{0,2},{1,3},{2,0},{3,1},{4,6},{5,7},{6,4},{7,5},{8,10},{9,11},{10,... | collective-permute-start | bytes 129032 | tf_op jit(solution)/shard_map/ppermute | solution.py:237
  12.7 16.6 %collective-permute-start.8 = (bf16[2,64,8192]{2,1,0:T(8,128)(2,1)S(1)}, bf16[2,64,8192]{2,1,0:T(8,128)(2,1)}, u32[]{:S(2)}, u32[]{:S(2)}) collective-permute-start(bf16[2,64,8192]{2,1,0:T(8,128)(2,1)S(1)} %bitcast.63), channel_id=1, source_target_pairs={{0,1},{1,0},{2,3},{3,2},{4,5},{5,4},{6,7},{7,6},{8,9},{9,8},{10,11... | collective-permute-start | bytes 6291464 | tf_op jit(solution)/shard_map/ppermute | solution.py:237
  15.1 8.2 %collective-permute-start.7 = (bf16[16,2688]{1,0:T(8,128)(2,1)S(1)}, bf16[16,2688]{1,0:T(8,128)(2,1)S(1)}, u32[]{:S(2)}, u32[]{:S(2)}) collective-permute-start(bf16[16,2688]{1,0:T(8,128)(2,1)S(1)} %constant_dynamic-update-slice_fusion.5), channel_id=1, source_target_pairs={{0,12},{1,13},{2,14},{3,15},{4,8},{5,9},{6,10},{7,11},{8,4},{9,5},... | collective-permute-start | bytes 258056 | tf_op jit(solution)/shard_map/ppermute | solution.py:237
  18.8 6.5 %collective-permute-start.6 = (bf16[16,2688]{1,0:T(8,128)(2,1)S(1)}, bf16[16,2688]{1,0:T(8,128)(2,1)S(1)}, u32[]{:S(2)}, u32[]{:S(2)}) collective-permute-start(bf16[16,2688]{1,0:T(8,128)(2,1)S(1)} %constant_dynamic-update-slice_fusion.5), channel_id=1, source_target_pairs={{0,8},{1,9},{2,10},{3,11},{4,12},{5,13},{6,14},{7,15},{8,0},{9,1},... | collective-permute-start | bytes 258056 | tf_op jit(solution)/shard_map/ppermute | solution.py:237
  21.7 4.6 %collective-permute-start.5 = (bf16[16,2688]{1,0:T(8,128)(2,1)S(1)}, bf16[16,2688]{1,0:T(8,128)(2,1)S(1)}, u32[]{:S(2)}, u32[]{:S(2)}) collective-permute-start(bf16[16,2688]{1,0:T(8,128)(2,1)S(1)} %constant_dynamic-update-slice_fusion.5), channel_id=1, source_target_pairs={{0,4},{1,5},{2,6},{3,7},{4,0},{5,1},{6,2},{7,3},{8,12},{9,13},{10,... | collective-permute-start | bytes 258056 | tf_op jit(solution)/shard_map/ppermute | solution.py:237
  21.7 7.5 %collective-permute-start.3 = (bf16[32,5632]{1,0:T(8,128)(2,1)S(1)}, bf16[32,5632]{1,0:T(8,128)(2,1)S(1)}, u32[]{:S(2)}, u32[]{:S(2)}) collective-permute-start(bf16[32,5632]{1,0:T(8,128)(2,1)S(1)} %pad_maximum_fusion.1), channel_id=1, source_target_pairs={{0,2},{1,3},{2,0},{3,1},{4,6},{5,7},{6,4},{7,5},{8,10},{9,11},{10,... | collective-permute-start | bytes 1081352 | tf_op jit(solution)/shard_map/ppermute | solution.py:237
  26.3 7.6 %copy-start = (bf16[512,8192]{1,0:T(8,128)(2,1)S(1)}, bf16[512,8192]{1,0:T(8,128)(2,1)}, u32[]{:S(2)}) copy-start(bf16[512,8192]{1,0:T(8,128)(2,1)} %weight_ref.1) | copy-start | bytes 25165828
  32.5 1.3 %collective-permute-start.9 = (bf16[64,640]{1,0:T(8,128)(2,1)S(1)}, bf16[64,640]{1,0:T(8,128)(2,1)S(1)}, u32[]{:S(2)}, u32[]{:S(2)}) collective-permute-start(bf16[64,640]{1,0:T(8,128)(2,1)S(1)} %get-tuple-element.14), channel_id=1, source_target_pairs={{0,1},{1,0},{2,3},{3,2},{4,5},{5,4},{6,7},{7,6},{8,9},{9,8},{10,11... | collective-permute-start | bytes 245768 | tf_op jit(solution)/shard_map/ppermute | solution.py:237
  33.8 1.6 %copy-start.2 = (bf16[2,64,8192]{2,1,0:T(8,128)(2,1)S(1)}, bf16[2,64,8192]{2,1,0:T(8,128)(2,1)}, u32[]{:S(2)}) copy-start(bf16[2,64,8192]{2,1,0:T(8,128)(2,1)} %up_ref.1) | copy-start | bytes 6291460
  37.3 2.7 %collective-permute-start.10 = (bf16[64,8192]{1,0:T(8,128)(2,1)S(1)}, bf16[64,8192]{1,0:T(8,128)(2,1)S(1)}, u32[]{:S(2)}, u32[]{:S(2)}) collective-permute-start(bf16[64,8192]{1,0:T(8,128)(2,1)S(1)} %get-tuple-element.16), channel_id=1, source_target_pairs={{0,1},{1,0},{2,3},{3,2},{4,5},{5,4},{6,7},{7,6},{8,9},{9,8},{10,11... | collective-permute-start | bytes 3145736 | tf_op jit(solution)/shard_map/ppermute | solution.py:237
  40.3 5.4 %collective-permute-start.15 = (bf16[2,8,2560]{2,1,0:T(8,128)(2,1)S(1)}, bf16[2,8,2560]{2,1,0:T(8,128)(2,1)S(1)}, u32[]{:S(2)}, u32[]{:S(2)}) collective-permute-start(bf16[2,8,2560]{2,1,0:T(8,128)(2,1)S(1)} %get-tuple-element.19), channel_id=1, source_target_pairs={{0,4},{1,5},{2,6},{3,7},{4,0},{5,1},{6,2},{7,3},{8,12},{9,13},{10,... | collective-permute-start | bytes 245768 | tf_op jit(solution)/shard_map/ppermute | solution.py:237
  42.4 7.0 %collective-permute-start.17 = (bf16[2,8,2560]{2,1,0:T(8,128)(2,1)S(1)}, bf16[2,8,2560]{2,1,0:T(8,128)(2,1)S(1)}, u32[]{:S(2)}, u32[]{:S(2)}) collective-permute-start(bf16[2,8,2560]{2,1,0:T(8,128)(2,1)S(1)} %get-tuple-element.20), channel_id=1, source_target_pairs={{0,12},{1,13},{2,14},{3,15},{4,8},{5,9},{6,10},{7,11},{8,4},{9,5},... | collective-permute-start | bytes 245768 | tf_op jit(solution)/shard_map/ppermute | solution.py:237
  44.1 7.8 %collective-permute-start.16 = (bf16[2,8,2560]{2,1,0:T(8,128)(2,1)S(1)}, bf16[2,8,2560]{2,1,0:T(8,128)(2,1)S(1)}, u32[]{:S(2)}, u32[]{:S(2)}) collective-permute-start(bf16[2,8,2560]{2,1,0:T(8,128)(2,1)S(1)} %get-tuple-element.21), channel_id=1, source_target_pairs={{0,8},{1,9},{2,10},{3,11},{4,12},{5,13},{6,14},{7,15},{8,0},{9,1},... | collective-permute-start | bytes 245768 | tf_op jit(solution)/shard_map/ppermute | solution.py:237
  44.1 10.0 %collective-permute-start.11 = (bf16[4,8,5632]{2,1,0:T(8,128)(2,1)S(1)}, bf16[4,8,5632]{2,1,0:T(8,128)(2,1)S(1)}, u32[]{:S(2)}, u32[]{:S(2)}) collective-permute-start(bf16[4,8,5632]{2,1,0:T(8,128)(2,1)S(1)} %slice_bitcast_fusion.1), channel_id=1, source_target_pairs={{0,2},{1,3},{2,0},{3,1},{4,6},{5,7},{6,4},{7,5},{8,10},{9,11},{10,... | collective-permute-start | bytes 1081352 | tf_op jit(solution)/shard_map/ppermute | solution.py:237
  52.0 6.9 %collective-permute-start.18 = (bf16[8,2560]{1,0:T(8,128)(2,1)S(1)}, bf16[8,2560]{1,0:T(8,128)(2,1)S(1)}, u32[]{:S(2)}, u32[]{:S(2)}) collective-permute-start(bf16[8,2560]{1,0:T(8,128)(2,1)S(1)} %fusion.10), channel_id=1, source_target_pairs={{0,2},{1,3},{2,0},{3,1},{4,6},{5,7},{6,4},{7,5},{8,10},{9,11},{10,... | collective-permute-start | bytes 122888 | tf_op jit(solution)/shard_map/ppermute | solution.py:237
  54.2 6.4 %collective-permute-start.12 = (bf16[8,5632]{1,0:T(8,128)(2,1)S(1)}, bf16[8,5632]{1,0:T(8,128)(2,1)S(1)}, u32[]{:S(2)}, u32[]{:S(2)}) collective-permute-start(bf16[8,5632]{1,0:T(8,128)(2,1)S(1)} %get-tuple-element.22), channel_id=1, source_target_pairs={{0,4},{1,5},{2,6},{3,7},{4,0},{5,1},{6,2},{7,3},{8,12},{9,13},{10,... | collective-permute-start | bytes 270344 | tf_op jit(solution)/shard_map/ppermute | solution.py:237
  57.1 6.4 %collective-permute-start.14 = (bf16[8,5632]{1,0:T(8,128)(2,1)S(1)}, bf16[8,5632]{1,0:T(8,128)(2,1)S(1)}, u32[]{:S(2)}, u32[]{:S(2)}) collective-permute-start(bf16[8,5632]{1,0:T(8,128)(2,1)S(1)} %get-tuple-element.23), channel_id=1, source_target_pairs={{0,12},{1,13},{2,14},{3,15},{4,8},{5,9},{6,10},{7,11},{8,4},{9,5},... | collective-permute-start | bytes 270344 | tf_op jit(solution)/shard_map/ppermute | solution.py:237
  58.8 7.2 %collective-permute-start.13 = (bf16[8,5632]{1,0:T(8,128)(2,1)S(1)}, bf16[8,5632]{1,0:T(8,128)(2,1)S(1)}, u32[]{:S(2)}, u32[]{:S(2)}) collective-permute-start(bf16[8,5632]{1,0:T(8,128)(2,1)S(1)} %get-tuple-element.24), channel_id=1, source_target_pairs={{0,8},{1,9},{2,10},{3,11},{4,12},{5,13},{6,14},{7,15},{8,0},{9,1},... | collective-permute-start | bytes 270344 | tf_op jit(solution)/shard_map/ppermute | solution.py:237

commit v3 on v2

v3 whole, which is shorter than its diff:
```python
import functools

import jax
import jax.numpy as jnp
from jax import lax
from jax.experimental import pallas as pl
from jax.experimental.pallas import tpu as pltpu
from jax.sharding import PartitionSpec as P

QUERY_HEADS = 64
KEY_VALUE_HEADS = 8
HEAD_SIZE = 128
GROUP = QUERY_HEADS // KEY_VALUE_HEADS
WIDTH = QUERY_HEADS * HEAD_SIZE
LANES = 128
BATCH = 4
ADAPTER_GAIN = 2.0
MASKED_SCORE = -1e30

CUT = 5888

NT = (((1,), (1,)), ((), ()))
VMEM = pl.BlockSpec(memory_space=pltpu.VMEM)
HBM = pl.BlockSpec(memory_space=pltpu.HBM)
SMEM = pl.BlockSpec(memory_space=pltpu.SMEM)


def held_in_vmem(x):
    return pltpu.with_memory_space_constraint(x, pltpu.VMEM)


def cost(flops, size):
    return pl.CostEstimate(flops=flops, bytes_accessed=size, transcendentals=0)


def per_head(row):
    return jnp.concatenate(
        [
            jnp.broadcast_to(row[:, k * HEAD_SIZE : (k + 1) * HEAD_SIZE], (GROUP, HEAD_SIZE))
            for k in range(KEY_VALUE_HEADS)
        ],
        axis=0,
    )


def attend_kernel(
    length_hbm, adapter_hbm, slot_hbm, query_hbm, pair_hbm, cache_hbm, a_ref, all_ref,
    length_ref, adapter_ref, slot_ref, query_ref, pair_ref, cache, spread, mixed, sems,
):
    requests = query_ref.shape[0]
    slots = cache.shape[2]

    def fetch(r):
        return pltpu.make_async_copy(cache_hbm.at[r], cache.at[r], sems.at[r])

    small = [
        pltpu.make_async_copy(source, target, sems.at[requests + i])
        for i, (source, target) in enumerate(
            (
                (query_hbm, query_ref), (pair_hbm, pair_ref), (length_hbm, length_ref),
                (adapter_hbm, adapter_ref), (slot_hbm, slot_ref),
            )
        )
    ]
    for copy in small:
        copy.start()
    for r in range(requests):
        fetch(r).start()
    for copy in small:
        copy.wait()
    scaling = HEAD_SIZE ** (-0.5)
    for h in range(QUERY_HEADS):
        spread[pl.ds(h, requests, stride=QUERY_HEADS), :] = query_ref[
            :, h * HEAD_SIZE : (h + 1) * HEAD_SIZE
        ].astype(jnp.float32)
    position = lax.broadcasted_iota(jnp.int32, (QUERY_HEADS, slots), 1)
    blank = jnp.zeros((GROUP, HEAD_SIZE), jnp.float32)
    pairs = KEY_VALUE_HEADS // 2
    for r in range(0, requests, BATCH):
        batch = range(r, r + BATCH)
        for t in batch:
            fetch(t).wait()
        scores = []
        for t in batch:
            rows = spread[t * QUERY_HEADS : (t + 1) * QUERY_HEADS, :]
            parts = []
            for j in range(pairs):
                upper = rows[2 * j * GROUP : (2 * j + 1) * GROUP]
                lower = rows[(2 * j + 1) * GROUP : (2 * j + 2) * GROUP]
                both = jnp.concatenate(
                    [
                        jnp.concatenate([upper, blank], axis=1),
                        jnp.concatenate([blank, lower], axis=1),
                    ],
                    axis=0,
                ).astype(jnp.bfloat16)
                keys = cache[t, 0, :, 2 * j * HEAD_SIZE : (2 * j + 2) * HEAD_SIZE]
                parts.append(lax.dot_general(both, keys, NT, preferred_element_type=jnp.float32))
            live = position < length_ref[t]
            score = jnp.concatenate(parts, axis=0) * scaling
            scores.append((rows, live, jnp.where(live, score, MASKED_SCORE)))
        probs = []
        for t, (rows, live, score) in zip(batch, scores):
            new = pair_ref[t].astype(jnp.float32)
            own_score = jnp.sum(rows * per_head(new[0:1]), axis=1, keepdims=True) * scaling
            top = jnp.maximum(jnp.max(score, axis=1, keepdims=True), own_score)
            weight = jnp.where(live, jnp.exp(score - top), 0.0)
            own_weight = jnp.exp(own_score - top)
            total = jnp.sum(weight, axis=1, keepdims=True) + own_weight
            prob = (weight / total).astype(jnp.bfloat16)
            own_prob = (own_weight / total).astype(jnp.bfloat16).astype(jnp.float32)
            probs.append((prob, own_prob * per_head(new[1:2])))
        for t, (prob, own_part) in zip(batch, probs):
            outs = []
            for j in range(pairs):
                values = cache[t, 1, :, 2 * j * HEAD_SIZE : (2 * j + 2) * HEAD_SIZE]
                both = jnp.dot(
                    prob[2 * j * GROUP : (2 * j + 2) * GROUP], values,
                    preferred_element_type=jnp.float32,
                )
                outs += [both[:GROUP, :HEAD_SIZE], both[GROUP:, HEAD_SIZE:]]
            mixed[t * QUERY_HEADS : (t + 1) * QUERY_HEADS, :] = (
                jnp.concatenate(outs, axis=0) + own_part
            )
    for h in range(QUERY_HEADS):
        column = h * HEAD_SIZE
        out = mixed[pl.ds(h, requests, stride=QUERY_HEADS), :].astype(jnp.bfloat16)
        all_ref[:, column : column + HEAD_SIZE] = out
        if column < a_ref.shape[1]:
            a_ref[:, column : column + HEAD_SIZE] = out
    row = lax.broadcasted_iota(jnp.int32, (requests, LANES), 0)
    tag = jnp.zeros((requests, LANES), jnp.int32)
    for r in range(requests):
        tag = jnp.where(row == r, slot_ref[adapter_ref[r]], tag)
    all_ref[:, WIDTH:] = tag.astype(jnp.float32).astype(jnp.bfloat16)


def attend(queries, incoming_pair, cache_key_value, cache_length, request_adapter, adapter_slot):
    requests = queries.shape[0]
    bf16, f32 = jnp.bfloat16, jnp.float32
    ints = (cache_length, request_adapter, adapter_slot)
    inputs = ints + (queries, incoming_pair, cache_key_value)
    return pl.pallas_call(
        attend_kernel,
        out_shape=(
            pltpu.VMEM((requests, CUT), bf16),
            pltpu.VMEM((requests, WIDTH + LANES), bf16),
        ),
        in_specs=[HBM] * 6,
        out_specs=(VMEM,) * 2,
        scratch_shapes=[pltpu.SMEM(x.shape, jnp.int32) for x in ints]
        + [
            pltpu.VMEM(queries.shape, bf16),
            pltpu.VMEM(incoming_pair.shape, bf16),
            pltpu.VMEM(cache_key_value.shape, bf16),
            pltpu.VMEM((requests * QUERY_HEADS, HEAD_SIZE), f32),
            pltpu.VMEM((requests * QUERY_HEADS, HEAD_SIZE), f32),
            pltpu.SemaphoreType.DMA((requests + 5,)),
        ],
        compiler_params=pltpu.CompilerParams(vmem_limit_bytes=20 << 20),
        cost_estimate=cost(10**9, 2 * cache_key_value.size),
        name="attend",
    )(*(pltpu.with_memory_space_constraint(x, pltpu.HBM) for x in inputs))


def shrink_kernel(device_ref, rows_ref, down_ref, down_other_ref, up_ref, own_ref, other_ref):
    del up_ref
    held, rank = down_ref.shape[0], down_ref.shape[1]
    half = rows_ref.shape[0]
    ranks = held * rank
    head = own_ref.shape[1] - ranks
    me = device_ref[0]
    terms = jnp.zeros((half, 2 * ranks), jnp.float32)
    for k in range(0, WIDTH, 512):
        at = slice(k, k + 512)
        factors = jnp.concatenate(
            [ref[:, :, at].reshape(ranks, 512) for ref in (down_ref, down_other_ref)], axis=0
        )
        terms += lax.dot_general(
            rows_ref[:, at], factors, NT, preferred_element_type=jnp.float32
        )
    slot = rows_ref[:, WIDTH : WIDTH + LANES].astype(jnp.float32)[:, :1]
    column = lax.broadcasted_iota(jnp.int32, (half, ranks), 1)
    for i, (device, ref) in enumerate(((me, own_ref), (me ^ 1, other_ref))):
        owned = (device * held + column // rank).astype(jnp.float32)
        part = terms[:, i * ranks : (i + 1) * ranks]
        shrunk = jnp.where(slot == owned, part, 0.0).astype(jnp.bfloat16)
        ref[:, head:] = shrunk * jnp.bfloat16(ADAPTER_GAIN)
        ref[:, :head] = rows_ref[:, pl.ds(pl.multiple_of(device * head, head), head)]


def shrink(device, rows, down, down_other, up, head):
    half = rows.shape[0]
    ranks = down.shape[0] * down.shape[1]
    out = jax.ShapeDtypeStruct((half, head + ranks), jnp.bfloat16)
    return pl.pallas_call(
        shrink_kernel,
        out_shape=(out, out),
        in_specs=[SMEM] + [VMEM] * 4,
        out_specs=(VMEM, VMEM),
        compiler_params=pltpu.CompilerParams(vmem_limit_bytes=16 << 20),
        cost_estimate=cost(4 * half * ranks * WIDTH, 4 * ranks * WIDTH),
        name="shrink",
    )(device, rows, held_in_vmem(down), held_in_vmem(down_other), held_in_vmem(up))


def project_kernel(tile, x_ref, x_other_ref, weight_ref, up_ref, own_ref, other_ref):
    half, columns = own_ref.shape
    held, rank, _ = up_ref.shape
    head = weight_ref.shape[0]
    x = jnp.concatenate([x_other_ref[...], x_ref[...]], axis=0)
    for start in range(0, columns, tile):
        at = slice(start, start + tile)
        out = jnp.dot(x[:, :head], weight_ref[:, at], preferred_element_type=jnp.float32)
        out += jnp.dot(
            x[:, head:], up_ref[:, :, at].reshape(held * rank, tile),
            preferred_element_type=jnp.float32,
        )
        other_ref[:, at] = out[:half].astype(jnp.bfloat16)
        own_ref[:, at] = out[half:]


def project(x, x_other, weight, up):
    half, columns = x.shape[0], weight.shape[1]
    return pl.pallas_call(
        functools.partial(project_kernel, 512),
        out_shape=(
            jax.ShapeDtypeStruct((half, columns), jnp.float32),
            jax.ShapeDtypeStruct((half, columns), jnp.bfloat16),
        ),
        in_specs=[VMEM] * 4,
        out_specs=(VMEM, VMEM),
        compiler_params=pltpu.CompilerParams(vmem_limit_bytes=16 << 20),
        cost_estimate=cost(4 * half * x.shape[1] * columns, 2 * x.shape[1] * columns),
        name="project",
    )(x, x_other, held_in_vmem(weight), held_in_vmem(up))


def per_device(
    queries, incoming_pair, cache_key_value, cache_length, out_weight,
    adapter_down, adapter_up, request_adapter, adapter_slot, *, members,
):
    depths = members // 4
    f32, bf16 = jnp.float32, jnp.bfloat16

    def swap(x, mask):
        return lax.ppermute(x, "rep", [(i, i ^ mask) for i in range(members)])

    requests = queries.shape[0]
    down = jnp.swapaxes(adapter_down, 1, 2)
    down_other = swap(down, 1)
    a, own = attend(
        queries, incoming_pair, cache_key_value, cache_length, request_adapter, adapter_slot
    )

    apart = range(1, depths)
    a_far = jnp.concatenate([swap(a, 4 * d) for d in apart], axis=0)
    side = swap(own, 2)
    b_sides = jnp.concatenate([own[:, CUT:], side[:, CUT:]], axis=0)
    b_far = jnp.stack([swap(b_sides, 4 * d) for d in apart], axis=0)
    b_far = jnp.swapaxes(b_far.reshape(depths - 1, 2, requests, -1), 0, 1)
    b_far = b_far.reshape(2, (depths - 1) * requests, -1)
    rows = jnp.concatenate(
        [
            own, jnp.concatenate([a_far, b_far[0]], axis=1),
            side, jnp.concatenate([swap(a_far, 2), b_far[1]], axis=1),
        ],
        axis=0,
    )

    device = lax.axis_index("rep").astype(jnp.int32).reshape(1)
    x, x_send = shrink(device, rows, down, down_other, adapter_up, out_weight.shape[0])
    x_other = swap(x_send, 1)

    mine, send = project(x, x_other, out_weight, adapter_up)
    sums = (mine + swap(send, 1).astype(f32)).reshape(2, depths, requests, WIDTH)
    a_sum, b_sum = sums[..., :CUT], sums[..., CUT:]
    a_part = a_sum[0, 1:] + swap(a_sum[1, 1:].astype(bf16), 2).astype(f32)
    b_send = b_sum.astype(bf16)
    b_part = b_sum[:, 0]
    for d in apart:
        b_part = b_part + swap(b_send[:, d], 4 * d).astype(f32)
    a_send = a_part.astype(bf16)
    a_out = a_sum[0, 0]
    for d in apart:
        a_out = a_out + swap(a_send[d - 1], 4 * d).astype(f32)
    side = swap(jnp.concatenate([a_sum[1, 0], b_part[1]], axis=1).astype(bf16), 2)
    return (jnp.concatenate([a_out, b_part[0]], axis=1) + side.astype(f32)).astype(bf16)


def solution(mesh):
    in_specs = (
        P(("groups", "rep"), None),
        P(("groups", "rep"), None, None),
        P(("groups", "rep"), None, None, None),
        P(("groups", "rep")),
        P("rep", None),
        P(("groups", "rep"), None, None),
        P(("groups", "rep"), None, None),
        P(("groups", "rep")),
        P("groups"),
    )
    out_specs = P(("groups", "rep"), None)
    return jax.shard_map(
        functools.partial(per_device, members=mesh.shape["rep"]),
        mesh=mesh, in_specs=in_specs, out_specs=out_specs, check_vma=False,
    )
```

time: 66.9 us -> 63 us (0.942)
  local copies, waits for them, and re-layouts: 1.76 us -> 0.16 us
  Pallas kernels: 10.3 us -> 8.76 us
  starting transfers between devices: 24.6 us -> 23.7 us
    pallas_call x1, Pallas kernels: 5.28 us -> 3.18 us  [attend(): pl.pallas_call(attend_kernel, out_shape=(pltpu.VMEM((requests, CUT), bf16...]
    unnamed x11 -> x6, local copies, waits for them, and re-layouts: 1.63 us -> 0.03 us
    ppermute x19, starting transfers between devices: 24.6 us -> 23.7 us  [swap(): return lax.ppermute(x, 'rep', [(i, i ^ mask) for i in range(members)])]
    convert_element_type x0 -> x1, other arithmetic: none -> 0.68 us  [per_device(): (jnp.concatenate([a_out, b_part[0]], axis=1) + side.astype(f32)).astype(b...]
  transfers between devices with their start and end apart: 19 -> 19, of which waited for: 13 -> 12; matrix products, arithmetic and copies ran while one was open for 1% -> 0% of each run, Pallas kernels for 0% -> 0%
where the time goes in v3:
time: 63 us; the launch traced here: 62.9 us
  waiting for transfers between devices  28.9 us (46%)
  starting transfers between devices  23.7 us (38%)
  Pallas kernels  8.76 us (14%)
  other arithmetic  1.13 us (2%)
    ppermute x19, waiting for transfers between devices, swap(): return lax.ppermute(x, 'rep', [(i, i ^ mask) for i in range(members)])  28.9 us
    ppermute x19, starting transfers between devices, swap(): return lax.ppermute(x, 'rep', [(i, i ^ mask) for i in range(members)])  23.7 us
    pallas_call x1, Pallas kernels, shrink(): pl.pallas_call(shrink_kernel, out_shape=(out, out), in_specs=[SMEM] + [VM...  3.75 us
    pallas_call x1, Pallas kernels, attend(): pl.pallas_call(attend_kernel, out_shape=(pltpu.VMEM((requests, CUT), bf16...  3.18 us
    pallas_call x1, Pallas kernels, project(): pl.pallas_call(functools.partial(project_kernel, 512), out_shape=(jax.Sha...  1.83 us
  transfers between devices with their start and end apart: 19, of which 12 were waited for; matrix products, arithmetic and copies ran while one was open for 0% of the time, Pallas kernels for 0%

profile of v3, /device:TPU:0, one launch (start us, length us, event | category | flops | bytes accessed | tf_op | source)
XLA Modules:
  0.0 62.9 jit_solution(6797196858606943885)
XLA Ops:
  0.0 3.2 %attend.1 = (bf16[8,5888]{1,0:T(8,128)(2,1)S(1)}, bf16[8,8320]{1,0:T(8,128)(2,1)S(1)}) custom-call(s32[8]{0:T(128)} %length_hbm.1, s32[8]{0:T(128)} %adapter_hbm.1, s32[32]{0:T(128)} %slot_hbm.1, bf16[8,8192]{1,0:T(8,128)(2,1)} %query_hbm.1, bf16[8,2,1024]{2,1,0:T(2,128)(2,1)} %pair_hbm.1, bf16[8,2,128,1024]{3,2,1,0:T(8,128)(2,1)} %cache_hbm.1), custom_call_target="tpu_custom_call" | custom-call | flops 1000000000 | bytes 4194304 | tf_op jit(solution)/shard_map/attend/pallas_call | solution.py:143
  3.2 0.0 copy-start.1
  3.2 3.1 %collective-permute-start = (bf16[8,5888]{1,0:T(8,128)(2,1)S(1)}, bf16[8,5888]{1,0:T(8,128)(2,1)S(1)}, u32[]{:S(2)}, u32[]{:S(2)}) collective-permute-start(bf16[8,5888]{1,0:T(8,128)(2,1)S(1)} %get-tuple-element.12), channel_id=1, source_target_pairs={{0,4},{1,5},{2,6},{3,7},{4,0},{5,1},{6,2},{7,3},{8,12},{9,13},{10,... | collective-permute-start | bytes 282632 | tf_op jit(solution)/shard_map/ppermute | solution.py:247
  6.3 2.5 %collective-permute-start.2 = (bf16[8,5888]{1,0:T(8,128)(2,1)S(1)}, bf16[8,5888]{1,0:T(8,128)(2,1)S(1)}, u32[]{:S(2)}, u32[]{:S(2)}) collective-permute-start(bf16[8,5888]{1,0:T(8,128)(2,1)S(1)} %get-tuple-element.12), channel_id=1, source_target_pairs={{0,12},{1,13},{2,14},{3,15},{4,8},{5,9},{6,10},{7,11},{8,4},{9,5},... | collective-permute-start | bytes 282632 | tf_op jit(solution)/shard_map/ppermute | solution.py:247
  8.8 0.1 collective-permute-start.1
  8.9 1.5 %collective-permute-start.3 = (bf16[8,8320]{1,0:T(8,128)(2,1)S(1)}, bf16[8,8320]{1,0:T(8,128)(2,1)S(1)}, u32[]{:S(2)}, u32[]{:S(2)}) collective-permute-start(bf16[8,8320]{1,0:T(8,128)(2,1)S(1)} %get-tuple-element.11), channel_id=1, source_target_pairs={{0,2},{1,3},{2,0},{3,1},{4,6},{5,7},{6,4},{7,5},{8,10},{9,11},{10,... | collective-permute-start | bytes 399368 | tf_op jit(solution)/shard_map/ppermute | solution.py:247
  10.4 0.0 collective-permute-start.8
  10.4 0.0 collective-permute-done
  10.4 6.9 %collective-permute-done.1 = bf16[8,5888]{1,0:T(8,128)(2,1)S(1)} collective-permute-done((bf16[8,5888]{1,0:T(8,128)(2,1)S(1)}, bf16[8,5888]{1,0:T(8,128)(2,1)S(1)}, u32[]{:S(2)}, u32[]{:S(2)}) %collective-permute-start.1) | collective-permute-done | bytes 94240 | tf_op jit(solution)/shard_map/ppermute | solution.py:247
  17.4 0.0 collective-permute-done.3
  17.4 2.7 %collective-permute-start.6 = (bf16[16,2432]{1,0:T(8,128)(2,1)S(1)}, bf16[16,2432]{1,0:T(8,128)(2,1)S(1)}, u32[]{:S(2)}, u32[]{:S(2)}) collective-permute-start(bf16[16,2432]{1,0:T(8,128)(2,1)S(1)} %pad_maximum_fusion.1), channel_id=1, source_target_pairs={{0,12},{1,13},{2,14},{3,15},{4,8},{5,9},{6,10},{7,11},{8,4},{9,5},... | collective-permute-start | bytes 233480 | tf_op jit(solution)/shard_map/ppermute | solution.py:247
  20.1 0.0 collective-permute-start.5
  20.1 1.7 %collective-permute-start.4 = (bf16[16,2432]{1,0:T(8,128)(2,1)S(1)}, bf16[16,2432]{1,0:T(8,128)(2,1)S(1)}, u32[]{:S(2)}, u32[]{:S(2)}) collective-permute-start(bf16[16,2432]{1,0:T(8,128)(2,1)S(1)} %pad_maximum_fusion.1), channel_id=1, source_target_pairs={{0,4},{1,5},{2,6},{3,7},{4,0},{5,1},{6,2},{7,3},{8,12},{9,13},{10,... | collective-permute-start | bytes 233480 | tf_op jit(solution)/shard_map/ppermute | solution.py:247
  21.9 0.0 collective-permute-done.2
  21.9 1.6 %collective-permute-start.7 = (bf16[24,5888]{1,0:T(8,128)(2,1)S(1)}, bf16[24,5888]{1,0:T(8,128)(2,1)S(1)}, u32[]{:S(2)}, u32[]{:S(2)}) collective-permute-start(bf16[24,5888]{1,0:T(8,128)(2,1)S(1)} %constant_dynamic-update-slice_fusion), channel_id=1, source_target_pairs={{0,2},{1,3},{2,0},{3,1},{4,6},{5,7},{6,4},{7,5},{8,10},{9,11},{10,... | collective-permute-start | bytes 847880 | tf_op jit(solution)/shard_map/ppermute | solution.py:247
  23.5 1.0 %collective-permute-done.6 = bf16[16,2432]{1,0:T(8,128)(2,1)S(1)} collective-permute-done((bf16[16,2432]{1,0:T(8,128)(2,1)S(1)}, bf16[16,2432]{1,0:T(8,128)(2,1)S(1)}, u32[]{:S(2)}, u32[]{:S(2)}) %collective-permute-start.6) | collective-permute-done | bytes 77856 | tf_op jit(solution)/shard_map/ppermute | solution.py:247
  24.5 2.1 %collective-permute-done.5 = bf16[16,2432]{1,0:T(8,128)(2,1)S(1)} collective-permute-done((bf16[16,2432]{1,0:T(8,128)(2,1)S(1)}, bf16[16,2432]{1,0:T(8,128)(2,1)S(1)}, u32[]{:S(2)}, u32[]{:S(2)}) %collective-permute-start.5) | collective-permute-done | bytes 77856 | tf_op jit(solution)/shard_map/ppermute | solution.py:247
  26.5 0.0 collective-permute-done.4
  26.6 2.8 %collective-permute-done.7 = bf16[24,5888]{1,0:T(8,128)(2,1)S(1)} collective-permute-done((bf16[24,5888]{1,0:T(8,128)(2,1)S(1)}, bf16[24,5888]{1,0:T(8,128)(2,1)S(1)}, u32[]{:S(2)}, u32[]{:S(2)}) %collective-permute-start.7) | collective-permute-done | bytes 282656 | tf_op jit(solution)/shard_map/ppermute | solution.py:247
  29.4 0.0 copy-start
  29.4 0.1 maximum_maximum_fusion.rows_ref
  29.5 0.0 collective-permute-done.8.down_other_ref
  29.5 0.0 copy-done.1
  29.5 3.8 %shrink.1 = (bf16[64,640]{1,0:T(8,128)(2,1)S(1)}, bf16[64,640]{1,0:T(8,128)(2,1)S(1)}) custom-call(s32[1]{0:T(128)} %bitcast.device_ref, bf16[64,8320]{1,0:T(8,128)(2,1)S(1)} %maximum_maximum_fusion.rows_ref, bf16[2,64,8192]{2,1,0:T(8,128)(2,1)} %bitcast.10.down_ref, bf16[2,64,8192]{2,1,0:T(8,128)(2,1)} %collective-permute-done.8.down_other_ref, ...), custom_call_target="tpu_custom_call" | custom-call | flops 268435456 | bytes 4194304 | tf_op jit(solution)/shard_map/shrink/pallas_call | solution.py:196
  33.3 0.1 collective-permute-start.9
  33.4 1.3 %collective-permute-done.9.x_other_ref = bf16[64,640]{1,0:T(8,128)(2,1)S(1)} collective-permute-done((bf16[64,640]{1,0:T(8,128)(2,1)S(1)}, bf16[64,640]{1,0:T(8,128)(2,1)S(1)}, u32[]{:S(2)}, u32[]{:S(2)}) %collective-permute-start.9) | collective-permute-done | bytes 81952 | tf_op jit(solution)/shard_map/ppermute | solution.py:247
  34.6 0.0 copy-done
  34.6 1.8 %project.1 = (f32[64,8192]{1,0:T(8,128)S(1)}, bf16[64,8192]{1,0:T(8,128)(2,1)S(1)}) custom-call(bf16[64,640]{1,0:T(8,128)(2,1)S(1)} %get-tuple-element.13.x_ref, bf16[64,640]{1,0:T(8,128)(2,1)S(1)} %collective-permute-done.9.x_other_ref, bf16[512,8192]{1,0:T(8,128)(2,1)S(1)} %copy-done, bf16[2,64,8192]{2,1,0:T(8,128)(2,1)S(1)} %copy-done.1), custom_call_target="tpu_custom_call" | custom-call | flops 1342177280 | bytes 10485760 | tf_op jit(solution)/shard_map/project/pallas_call | solution.py:225
  36.5 0.2 collective-permute-start.10
  36.7 2.5 %collective-permute-done.10 = bf16[64,8192]{1,0:T(8,128)(2,1)S(1)} collective-permute-done((bf16[64,8192]{1,0:T(8,128)(2,1)S(1)}, bf16[64,8192]{1,0:T(8,128)(2,1)S(1)}, u32[]{:S(2)}, u32[]{:S(2)}) %collective-permute-start.10) | collective-permute-done | bytes 1048608 | tf_op jit(solution)/shard_map/ppermute | solution.py:247
  39.2 0.2 convert_add_fusion
  39.5 0.4 collective-permute-start.15
  39.8 2.1 %collective-permute-start.17 = (bf16[2,8,2304]{2,1,0:T(8,128)(2,1)S(1)}, bf16[2,8,2304]{2,1,0:T(8,128)(2,1)S(1)}, u32[]{:S(2)}, u32[]{:S(2)}) collective-permute-start(bf16[2,8,2304]{2,1,0:T(8,128)(2,1)S(1)} %get-tuple-element.18), channel_id=1, source_target_pairs={{0,12},{1,13},{2,14},{3,15},{4,8},{5,9},{6,10},{7,11},{8,4},{9,5},... | collective-permute-start | bytes 221192 | tf_op jit(solution)/shard_map/ppermute | solution.py:247
  41.9 1.1 %collective-permute-start.16 = (bf16[2,8,2304]{2,1,0:T(8,128)(2,1)S(1)}, bf16[2,8,2304]{2,1,0:T(8,128)(2,1)S(1)}, u32[]{:S(2)}, u32[]{:S(2)}) collective-permute-start(bf16[2,8,2304]{2,1,0:T(8,128)(2,1)S(1)} %get-tuple-element.19), channel_id=1, source_target_pairs={{0,8},{1,9},{2,10},{3,11},{4,12},{5,13},{6,14},{7,15},{8,0},{9,1},... | collective-permute-start | bytes 221192 | tf_op jit(solution)/shard_map/ppermute | solution.py:247
  43.0 1.6 %collective-permute-start.11 = (bf16[3,8,5888]{2,1,0:T(8,128)(2,1)S(1)}, bf16[3,8,5888]{2,1,0:T(8,128)(2,1)S(1)}, u32[]{:S(2)}, u32[]{:S(2)}) collective-permute-start(bf16[3,8,5888]{2,1,0:T(8,128)(2,1)S(1)} %slice_bitcast_fusion.1), channel_id=1, source_target_pairs={{0,2},{1,3},{2,0},{3,1},{4,6},{5,7},{6,4},{7,5},{8,10},{9,11},{10,... | collective-permute-start | bytes 847880 | tf_op jit(solution)/shard_map/ppermute | solution.py:247
  44.6 0.0 collective-permute-done.15
  44.6 2.0 %collective-permute-done.17 = bf16[2,8,2304]{2,1,0:T(8,128)(2,1)S(1)} collective-permute-done((bf16[2,8,2304]{2,1,0:T(8,128)(2,1)S(1)}, bf16[2,8,2304]{2,1,0:T(8,128)(2,1)S(1)}, u32[]{:S(2)}, u32[]{:S(2)}) %collective-permute-start.17) | collective-permute-done | bytes 73760 | tf_op jit(solution)/shard_map/ppermute | solution.py:247
  46.6 3.2 %collective-permute-done.16 = bf16[2,8,2304]{2,1,0:T(8,128)(2,1)S(1)} collective-permute-done((bf16[2,8,2304]{2,1,0:T(8,128)(2,1)S(1)}, bf16[2,8,2304]{2,1,0:T(8,128)(2,1)S(1)}, u32[]{:S(2)}, u32[]{:S(2)}) %collective-permute-start.16) | collective-permute-done | bytes 73760 | tf_op jit(solution)/shard_map/ppermute | solution.py:247
  49.9 1.2 %collective-permute-done.11 = bf16[3,8,5888]{2,1,0:T(8,128)(2,1)S(1)} collective-permute-done((bf16[3,8,5888]{2,1,0:T(8,128)(2,1)S(1)}, bf16[3,8,5888]{2,1,0:T(8,128)(2,1)S(1)}, u32[]{:S(2)}, u32[]{:S(2)}) %collective-permute-start.11) | collective-permute-done | bytes 282656 | tf_op jit(solution)/shard_map/ppermute | solution.py:247
  51.1 1.3 %collective-permute-start.12 = (bf16[8,5888]{1,0:T(8,128)(2,1)S(1)}, bf16[8,5888]{1,0:T(8,128)(2,1)S(1)}, u32[]{:S(2)}, u32[]{:S(2)}) collective-permute-start(bf16[8,5888]{1,0:T(8,128)(2,1)S(1)} %get-tuple-element.20), channel_id=1, source_target_pairs={{0,4},{1,5},{2,6},{3,7},{4,0},{5,1},{6,2},{7,3},{8,12},{9,13},{10,... | collective-permute-start | bytes 282632 | tf_op jit(solution)/shard_map/ppermute | solution.py:247
  52.5 2.1 %collective-permute-start.14 = (bf16[8,5888]{1,0:T(8,128)(2,1)S(1)}, bf16[8,5888]{1,0:T(8,128)(2,1)S(1)}, u32[]{:S(2)}, u32[]{:S(2)}) collective-permute-start(bf16[8,5888]{1,0:T(8,128)(2,1)S(1)} %get-tuple-element.21), channel_id=1, source_target_pairs={{0,12},{1,13},{2,14},{3,15},{4,8},{5,9},{6,10},{7,11},{8,4},{9,5},... | collective-permute-start | bytes 282632 | tf_op jit(solution)/shard_map/ppermute | solution.py:247
  54.6 0.1 collective-permute-start.13
  54.7 1.5 %collective-permute-start.18 = (bf16[8,8192]{1,0:T(8,128)(2,1)S(1)}, bf16[8,8192]{1,0:T(8,128)(2,1)S(1)}, u32[]{:S(2)}, u32[]{:S(2)}) collective-permute-start(bf16[8,8192]{1,0:T(8,128)(2,1)S(1)} %pad_maximum_fusion), channel_id=1, source_target_pairs={{0,2},{1,3},{2,0},{3,1},{4,6},{5,7},{6,4},{7,5},{8,10},{9,11},{10,... | collective-permute-start | bytes 393224 | tf_op jit(solution)/shard_map/ppermute | solution.py:247
  56.2 0.8 %collective-permute-done.12 = bf16[8,5888]{1,0:T(8,128)(2,1)S(1)} collective-permute-done((bf16[8,5888]{1,0:T(8,128)(2,1)S(1)}, bf16[8,5888]{1,0:T(8,128)(2,1)S(1)}, u32[]{:S(2)}, u32[]{:S(2)}) %collective-permute-start.12) | collective-permute-done | bytes 94240 | tf_op jit(solution)/shard_map/ppermute | solution.py:247
  57.0 2.1 %collective-permute-done.14 = bf16[8,5888]{1,0:T(8,128)(2,1)S(1)} collective-permute-done((bf16[8,5888]{1,0:T(8,128)(2,1)S(1)}, bf16[8,5888]{1,0:T(8,128)(2,1)S(1)}, u32[]{:S(2)}, u32[]{:S(2)}) %collective-permute-start.14) | collective-permute-done | bytes 94240 | tf_op jit(solution)/shard_map/ppermute | solution.py:247
  59.1 3.1 %collective-permute-done.13 = bf16[8,5888]{1,0:T(8,128)(2,1)S(1)} collective-permute-done((bf16[8,5888]{1,0:T(8,128)(2,1)S(1)}, bf16[8,5888]{1,0:T(8,128)(2,1)S(1)}, u32[]{:S(2)}, u32[]{:S(2)}) %collective-permute-start.13) | collective-permute-done | bytes 94240 | tf_op jit(solution)/shard_map/ppermute | solution.py:247
  62.2 0.0 collective-permute-done.18
  62.2 0.7 %fusion.2 = bf16[8,8192]{1,0:T(8,128)(2,1)} fusion(f32[8,2304]{1,0:T(8,128)S(1)} %slice_bitcast_fusion.10, f32[8,5888]{1,0:T(8,128)S(1)} %fusion.5, bf16[8,8192]{1,0:T(8,128)(2,1)S(1)} %collective-permute-done.18), kind=kLoop, calls=%fused_computation.7 | loop fusion | flops 262144 | bytes 524288 | tf_op jit(solution)/shard_map/convert_element_type | solution.py:288
  (18 shorter events, 0.3 us)
Async XLA Ops:
  3.2 26.3 %copy-start.1 = (bf16[2,64,8192]{2,1,0:T(8,128)(2,1)S(1)}, bf16[2,64,8192]{2,1,0:T(8,128)(2,1)}, u32[]{:S(2)}) copy-start(bf16[2,64,8192]{2,1,0:T(8,128)(2,1)} %up_ref.3) | copy-start | bytes 6291460
  3.2 7.2 %collective-permute-start = (bf16[8,5888]{1,0:T(8,128)(2,1)S(1)}, bf16[8,5888]{1,0:T(8,128)(2,1)S(1)}, u32[]{:S(2)}, u32[]{:S(2)}) collective-permute-start(bf16[8,5888]{1,0:T(8,128)(2,1)S(1)} %get-tuple-element.12), channel_id=1, source_target_pairs={{0,4},{1,5},{2,6},{3,7},{4,0},{5,1},{6,2},{7,3},{8,12},{9,13},{10,... | collective-permute-start | bytes 282632 | tf_op jit(solution)/shard_map/ppermute | solution.py:247
  6.3 15.6 %collective-permute-start.2 = (bf16[8,5888]{1,0:T(8,128)(2,1)S(1)}, bf16[8,5888]{1,0:T(8,128)(2,1)S(1)}, u32[]{:S(2)}, u32[]{:S(2)}) collective-permute-start(bf16[8,5888]{1,0:T(8,128)(2,1)S(1)} %get-tuple-element.12), channel_id=1, source_target_pairs={{0,12},{1,13},{2,14},{3,15},{4,8},{5,9},{6,10},{7,11},{8,4},{9,5},... | collective-permute-start | bytes 282632 | tf_op jit(solution)/shard_map/ppermute | solution.py:247
  8.8 8.6 %collective-permute-start.1 = (bf16[8,5888]{1,0:T(8,128)(2,1)S(1)}, bf16[8,5888]{1,0:T(8,128)(2,1)S(1)}, u32[]{:S(2)}, u32[]{:S(2)}) collective-permute-start(bf16[8,5888]{1,0:T(8,128)(2,1)S(1)} %get-tuple-element.12), channel_id=1, source_target_pairs={{0,8},{1,9},{2,10},{3,11},{4,12},{5,13},{6,14},{7,15},{8,0},{9,1},... | collective-permute-start | bytes 282632 | tf_op jit(solution)/shard_map/ppermute | solution.py:247
  8.9 8.5 %collective-permute-start.3 = (bf16[8,8320]{1,0:T(8,128)(2,1)S(1)}, bf16[8,8320]{1,0:T(8,128)(2,1)S(1)}, u32[]{:S(2)}, u32[]{:S(2)}) collective-permute-start(bf16[8,8320]{1,0:T(8,128)(2,1)S(1)} %get-tuple-element.11), channel_id=1, source_target_pairs={{0,2},{1,3},{2,0},{3,1},{4,6},{5,7},{6,4},{7,5},{8,10},{9,11},{10,... | collective-permute-start | bytes 399368 | tf_op jit(solution)/shard_map/ppermute | solution.py:247
  10.4 19.1 %collective-permute-start.8 = (bf16[2,64,8192]{2,1,0:T(8,128)(2,1)}, bf16[2,64,8192]{2,1,0:T(8,128)(2,1)}, u32[]{:S(2)}, u32[]{:S(2)}) collective-permute-start(bf16[2,64,8192]{2,1,0:T(8,128)(2,1)} %bitcast.10.down_ref), channel_id=1, source_target_pairs={{0,1},{1,0},{2,3},{3,2},{4,5},{5,4},{6,7},{7,6},{8,9},{9,8},{10,11... | collective-permute-start | bytes 6291464 | tf_op jit(solution)/shard_map/ppermute | solution.py:247
  17.4 7.1 %collective-permute-start.6 = (bf16[16,2432]{1,0:T(8,128)(2,1)S(1)}, bf16[16,2432]{1,0:T(8,128)(2,1)S(1)}, u32[]{:S(2)}, u32[]{:S(2)}) collective-permute-start(bf16[16,2432]{1,0:T(8,128)(2,1)S(1)} %pad_maximum_fusion.1), channel_id=1, source_target_pairs={{0,12},{1,13},{2,14},{3,15},{4,8},{5,9},{6,10},{7,11},{8,4},{9,5},... | collective-permute-start | bytes 233480 | tf_op jit(solution)/shard_map/ppermute | solution.py:247
  20.1 6.4 %collective-permute-start.5 = (bf16[16,2432]{1,0:T(8,128)(2,1)S(1)}, bf16[16,2432]{1,0:T(8,128)(2,1)S(1)}, u32[]{:S(2)}, u32[]{:S(2)}) collective-permute-start(bf16[16,2432]{1,0:T(8,128)(2,1)S(1)} %pad_maximum_fusion.1), channel_id=1, source_target_pairs={{0,8},{1,9},{2,10},{3,11},{4,12},{5,13},{6,14},{7,15},{8,0},{9,1},... | collective-permute-start | bytes 233480 | tf_op jit(solution)/shard_map/ppermute | solution.py:247
  20.1 6.4 %collective-permute-start.4 = (bf16[16,2432]{1,0:T(8,128)(2,1)S(1)}, bf16[16,2432]{1,0:T(8,128)(2,1)S(1)}, u32[]{:S(2)}, u32[]{:S(2)}) collective-permute-start(bf16[16,2432]{1,0:T(8,128)(2,1)S(1)} %pad_maximum_fusion.1), channel_id=1, source_target_pairs={{0,4},{1,5},{2,6},{3,7},{4,0},{5,1},{6,2},{7,3},{8,12},{9,13},{10,... | collective-permute-start | bytes 233480 | tf_op jit(solution)/shard_map/ppermute | solution.py:247
  21.9 7.5 %collective-permute-start.7 = (bf16[24,5888]{1,0:T(8,128)(2,1)S(1)}, bf16[24,5888]{1,0:T(8,128)(2,1)S(1)}, u32[]{:S(2)}, u32[]{:S(2)}) collective-permute-start(bf16[24,5888]{1,0:T(8,128)(2,1)S(1)} %constant_dynamic-update-slice_fusion), channel_id=1, source_target_pairs={{0,2},{1,3},{2,0},{3,1},{4,6},{5,7},{6,4},{7,5},{8,10},{9,11},{10,... | collective-permute-start | bytes 847880 | tf_op jit(solution)/shard_map/ppermute | solution.py:247
  29.4 5.2 %copy-start = (bf16[512,8192]{1,0:T(8,128)(2,1)S(1)}, bf16[512,8192]{1,0:T(8,128)(2,1)}, u32[]{:S(2)}) copy-start(bf16[512,8192]{1,0:T(8,128)(2,1)} %weight_ref.1) | copy-start | bytes 25165828
  33.3 1.3 %collective-permute-start.9 = (bf16[64,640]{1,0:T(8,128)(2,1)S(1)}, bf16[64,640]{1,0:T(8,128)(2,1)S(1)}, u32[]{:S(2)}, u32[]{:S(2)}) collective-permute-start(bf16[64,640]{1,0:T(8,128)(2,1)S(1)} %get-tuple-element.14), channel_id=1, source_target_pairs={{0,1},{1,0},{2,3},{3,2},{4,5},{5,4},{6,7},{7,6},{8,9},{9,8},{10,11... | collective-permute-start | bytes 245768 | tf_op jit(solution)/shard_map/ppermute | solution.py:247
  36.5 2.7 %collective-permute-start.10 = (bf16[64,8192]{1,0:T(8,128)(2,1)S(1)}, bf16[64,8192]{1,0:T(8,128)(2,1)S(1)}, u32[]{:S(2)}, u32[]{:S(2)}) collective-permute-start(bf16[64,8192]{1,0:T(8,128)(2,1)S(1)} %get-tuple-element.16), channel_id=1, source_target_pairs={{0,1},{1,0},{2,3},{3,2},{4,5},{5,4},{6,7},{7,6},{8,9},{9,8},{10,11... | collective-permute-start | bytes 3145736 | tf_op jit(solution)/shard_map/ppermute | solution.py:247
  39.5 5.2 %collective-permute-start.15 = (bf16[2,8,2304]{2,1,0:T(8,128)(2,1)S(1)}, bf16[2,8,2304]{2,1,0:T(8,128)(2,1)S(1)}, u32[]{:S(2)}, u32[]{:S(2)}) collective-permute-start(bf16[2,8,2304]{2,1,0:T(8,128)(2,1)S(1)} %get-tuple-element.17), channel_id=1, source_target_pairs={{0,4},{1,5},{2,6},{3,7},{4,0},{5,1},{6,2},{7,3},{8,12},{9,13},{10,... | collective-permute-start | bytes 221192 | tf_op jit(solution)/shard_map/ppermute | solution.py:247
  39.8 6.8 %collective-permute-start.17 = (bf16[2,8,2304]{2,1,0:T(8,128)(2,1)S(1)}, bf16[2,8,2304]{2,1,0:T(8,128)(2,1)S(1)}, u32[]{:S(2)}, u32[]{:S(2)}) collective-permute-start(bf16[2,8,2304]{2,1,0:T(8,128)(2,1)S(1)} %get-tuple-element.18), channel_id=1, source_target_pairs={{0,12},{1,13},{2,14},{3,15},{4,8},{5,9},{6,10},{7,11},{8,4},{9,5},... | collective-permute-start | bytes 221192 | tf_op jit(solution)/shard_map/ppermute | solution.py:247
  41.9 7.9 %collective-permute-start.16 = (bf16[2,8,2304]{2,1,0:T(8,128)(2,1)S(1)}, bf16[2,8,2304]{2,1,0:T(8,128)(2,1)S(1)}, u32[]{:S(2)}, u32[]{:S(2)}) collective-permute-start(bf16[2,8,2304]{2,1,0:T(8,128)(2,1)S(1)} %get-tuple-element.19), channel_id=1, source_target_pairs={{0,8},{1,9},{2,10},{3,11},{4,12},{5,13},{6,14},{7,15},{8,0},{9,1},... | collective-permute-start | bytes 221192 | tf_op jit(solution)/shard_map/ppermute | solution.py:247
  43.0 8.0 %collective-permute-start.11 = (bf16[3,8,5888]{2,1,0:T(8,128)(2,1)S(1)}, bf16[3,8,5888]{2,1,0:T(8,128)(2,1)S(1)}, u32[]{:S(2)}, u32[]{:S(2)}) collective-permute-start(bf16[3,8,5888]{2,1,0:T(8,128)(2,1)S(1)} %slice_bitcast_fusion.1), channel_id=1, source_target_pairs={{0,2},{1,3},{2,0},{3,1},{4,6},{5,7},{6,4},{7,5},{8,10},{9,11},{10,... | collective-permute-start | bytes 847880 | tf_op jit(solution)/shard_map/ppermute | solution.py:247
  51.1 5.8 %collective-permute-start.12 = (bf16[8,5888]{1,0:T(8,128)(2,1)S(1)}, bf16[8,5888]{1,0:T(8,128)(2,1)S(1)}, u32[]{:S(2)}, u32[]{:S(2)}) collective-permute-start(bf16[8,5888]{1,0:T(8,128)(2,1)S(1)} %get-tuple-element.20), channel_id=1, source_target_pairs={{0,4},{1,5},{2,6},{3,7},{4,0},{5,1},{6,2},{7,3},{8,12},{9,13},{10,... | collective-permute-start | bytes 282632 | tf_op jit(solution)/shard_map/ppermute | solution.py:247
  52.5 6.6 %collective-permute-start.14 = (bf16[8,5888]{1,0:T(8,128)(2,1)S(1)}, bf16[8,5888]{1,0:T(8,128)(2,1)S(1)}, u32[]{:S(2)}, u32[]{:S(2)}) collective-permute-start(bf16[8,5888]{1,0:T(8,128)(2,1)S(1)} %get-tuple-element.21), channel_id=1, source_target_pairs={{0,12},{1,13},{2,14},{3,15},{4,8},{5,9},{6,10},{7,11},{8,4},{9,5},... | collective-permute-start | bytes 282632 | tf_op jit(solution)/shard_map/ppermute | solution.py:247
  54.6 7.5 %collective-permute-start.13 = (bf16[8,5888]{1,0:T(8,128)(2,1)S(1)}, bf16[8,5888]{1,0:T(8,128)(2,1)S(1)}, u32[]{:S(2)}, u32[]{:S(2)}) collective-permute-start(bf16[8,5888]{1,0:T(8,128)(2,1)S(1)} %get-tuple-element.22), channel_id=1, source_target_pairs={{0,8},{1,9},{2,10},{3,11},{4,12},{5,13},{6,14},{7,15},{8,0},{9,1},... | collective-permute-start | bytes 282632 | tf_op jit(solution)/shard_map/ppermute | solution.py:247
  54.7 7.5 %collective-permute-start.18 = (bf16[8,8192]{1,0:T(8,128)(2,1)S(1)}, bf16[8,8192]{1,0:T(8,128)(2,1)S(1)}, u32[]{:S(2)}, u32[]{:S(2)}) collective-permute-start(bf16[8,8192]{1,0:T(8,128)(2,1)S(1)} %pad_maximum_fusion), channel_id=1, source_target_pairs={{0,2},{1,3},{2,0},{3,1},{4,6},{5,7},{6,4},{7,5},{8,10},{9,11},{10,... | collective-permute-start | bytes 393224 | tf_op jit(solution)/shard_map/ppermute | solution.py:247

commit v4 on v3

--- a/solution.py
+++ b/solution.py
@@ -163,22 +163,45 @@
     )(*(pltpu.with_memory_space_constraint(x, pltpu.HBM) for x in inputs))
 
 
-def shrink_kernel(device_ref, rows_ref, down_ref, down_other_ref, up_ref, own_ref, other_ref):
-    del up_ref
-    held, rank = down_ref.shape[0], down_ref.shape[1]
+def stage_kernel(down_ref, down_other_ref, out_ref, held, sems):
+    ranks = held.shape[1]
+    copies = [
+        pltpu.make_async_copy(ref, held.at[i], sems.at[i])
+        for i, ref in enumerate((down_ref, down_other_ref))
+    ]
+    for copy in copies:
+        copy.start()
+    for i, copy in enumerate(copies):
+        copy.wait()
+        for k in range(0, WIDTH, 1024):
+            out_ref[k : k + 1024, i * ranks : (i + 1) * ranks] = held[i, :, k : k + 1024].T
+
+
+def stage(down, down_other):
+    ranks = down.shape[0] * down.shape[1]
+    pair = [x.reshape(ranks, WIDTH) for x in (down, down_other)]
+    return pl.pallas_call(
+        stage_kernel,
+        out_shape=pltpu.VMEM((WIDTH, 2 * ranks), jnp.bfloat16),
+        in_specs=[HBM] * 2,
+        out_specs=VMEM,
+        scratch_shapes=[
+            pltpu.VMEM((2, ranks, WIDTH), jnp.bfloat16),
+            pltpu.SemaphoreType.DMA((2,)),
+        ],
+        compiler_params=pltpu.CompilerParams(vmem_limit_bytes=16 << 20),
+        cost_estimate=cost(10**8, 8 * ranks * WIDTH),
+        name="stage",
+    )(*(pltpu.with_memory_space_constraint(x, pltpu.HBM) for x in pair))
+
+
+def shrink_kernel(device_ref, rows_ref, factors_ref, up_ref, own_ref, other_ref):
+    held, rank = up_ref.shape[0], up_ref.shape[1]
     half = rows_ref.shape[0]
     ranks = held * rank
     head = own_ref.shape[1] - ranks
     me = device_ref[0]
-    terms = jnp.zeros((half, 2 * ranks), jnp.float32)
-    for k in range(0, WIDTH, 512):
-        at = slice(k, k + 512)
-        factors = jnp.concatenate(
-            [ref[:, :, at].reshape(ranks, 512) for ref in (down_ref, down_other_ref)], axis=0
-        )
-        terms += lax.dot_general(
-            rows_ref[:, at], factors, NT, preferred_element_type=jnp.float32
-        )
+    terms = jnp.dot(rows_ref[:, :WIDTH], factors_ref[...], preferred_element_type=jnp.float32)
     slot = rows_ref[:, WIDTH : WIDTH + LANES].astype(jnp.float32)[:, :1]
     column = lax.broadcasted_iota(jnp.int32, (half, ranks), 1)
     for i, (device, ref) in enumerate(((me, own_ref), (me ^ 1, other_ref))):
@@ -189,19 +212,19 @@
         ref[:, :head] = rows_ref[:, pl.ds(pl.multiple_of(device * head, head), head)]
 
 
-def shrink(device, rows, down, down_other, up, head):
+def shrink(device, rows, factors, up, head):
     half = rows.shape[0]
-    ranks = down.shape[0] * down.shape[1]
+    ranks = up.shape[0] * up.shape[1]
     out = jax.ShapeDtypeStruct((half, head + ranks), jnp.bfloat16)
     return pl.pallas_call(
         shrink_kernel,
         out_shape=(out, out),
-        in_specs=[SMEM] + [VMEM] * 4,
+        in_specs=[SMEM] + [VMEM] * 3,
         out_specs=(VMEM, VMEM),
         compiler_params=pltpu.CompilerParams(vmem_limit_bytes=16 << 20),
         cost_estimate=cost(4 * half * ranks * WIDTH, 4 * ranks * WIDTH),
         name="shrink",
-    )(device, rows, held_in_vmem(down), held_in_vmem(down_other), held_in_vmem(up))
+    )(device, rows, held_in_vmem(factors), held_in_vmem(up))
 
 
 def project_kernel(tile, x_ref, x_other_ref, weight_ref, up_ref, own_ref, other_ref):
@@ -247,29 +270,32 @@
         return lax.ppermute(x, "rep", [(i, i ^ mask) for i in range(members)])
 
     requests = queries.shape[0]
-    down = jnp.swapaxes(adapter_down, 1, 2)
-    down_other = swap(down, 1)
     a, own = attend(
         queries, incoming_pair, cache_key_value, cache_length, request_adapter, adapter_slot
     )
 
-    apart = range(1, depths)
+    down = jnp.swapaxes(adapter_down, 1, 2)
+    down_other, a, own = lax.optimization_barrier((swap(down, 1), a, own))
+    factors = stage(down, down_other)
+
+    apart = range(depths - 1, 0, -1)
     a_far = jnp.concatenate([swap(a, 4 * d) for d in apart], axis=0)
     side = swap(own, 2)
     b_sides = jnp.concatenate([own[:, CUT:], side[:, CUT:]], axis=0)
     b_far = jnp.stack([swap(b_sides, 4 * d) for d in apart], axis=0)
     b_far = jnp.swapaxes(b_far.reshape(depths - 1, 2, requests, -1), 0, 1)
     b_far = b_far.reshape(2, (depths - 1) * requests, -1)
+    a_side = swap(a_far, 2)
     rows = jnp.concatenate(
         [
             own, jnp.concatenate([a_far, b_far[0]], axis=1),
-            side, jnp.concatenate([swap(a_far, 2), b_far[1]], axis=1),
+            side, jnp.concatenate([a_side, b_far[1]], axis=1),
         ],
         axis=0,
     )
 
     device = lax.axis_index("rep").astype(jnp.int32).reshape(1)
-    x, x_send = shrink(device, rows, down, down_other, adapter_up, out_weight.shape[0])
+    x, x_send = shrink(device, rows, factors, adapter_up, out_weight.shape[0])
     x_other = swap(x_send, 1)
 
     mine, send = project(x, x_other, out_weight, adapter_up)
@@ -277,13 +303,15 @@
     a_sum, b_sum = sums[..., :CUT], sums[..., CUT:]
     a_part = a_sum[0, 1:] + swap(a_sum[1, 1:].astype(bf16), 2).astype(f32)
     b_send = b_sum.astype(bf16)
+    a_send = a_part.astype(bf16)
+    b_came = [swap(b_send[:, i], 4 * d) for i, d in enumerate(apart, 1)]
+    b_came, _ = lax.optimization_barrier((b_came, a_send))
     b_part = b_sum[:, 0]
-    for d in apart:
-        b_part = b_part + swap(b_send[:, d], 4 * d).astype(f32)
-    a_send = a_part.astype(bf16)
+    for came in b_came:
+        b_part = b_part + came.astype(f32)
     a_out = a_sum[0, 0]
-    for d in apart:
-        a_out = a_out + swap(a_send[d - 1], 4 * d).astype(f32)
+    for i, d in enumerate(apart):
+        a_out = a_out + swap(a_send[i], 4 * d).astype(f32)
     side = swap(jnp.concatenate([a_sum[1, 0], b_part[1]], axis=1).astype(bf16), 2)
     return (jnp.concatenate([a_out, b_part[0]], axis=1) + side.astype(f32)).astype(bf16)
 

time: 63 us -> 59.1 us (0.938)
  waiting for transfers between devices: 28.9 us -> 23 us
  starting transfers between devices: 23.7 us -> 25.5 us
    ppermute x19, waiting for transfers between devices: 28.9 us -> 23 us  [swap(): return lax.ppermute(x, 'rep', [(i, i ^ mask) for i in range(members)])]
    pallas_call x0 -> x1, Pallas kernels: none -> 2.98 us  [stage(): pl.pallas_call(stage_kernel, out_shape=pltpu.VMEM((WIDTH, 2 * ranks), jnp...]
    pallas_call x1, Pallas kernels: 3.75 us -> 0.84 us  [shrink(): pl.pallas_call(shrink_kernel, out_shape=(out, out), in_specs=[SMEM] + [VM...]
    ppermute x19, starting transfers between devices: 23.7 us -> 25.5 us  [swap(): return lax.ppermute(x, 'rep', [(i, i ^ mask) for i in range(members)])]
  transfers between devices with their start and end apart: 19 -> 19, of which waited for: 12 -> 11; matrix products, arithmetic and copies ran while one was open for 0% -> 0% of each run, Pallas kernels for 0% -> 10%
where the time goes in v4:
time: 59.1 us; the launch traced here: 58.9 us
  starting transfers between devices  25.5 us (43%)
  waiting for transfers between devices  23 us (39%)
  Pallas kernels  8.85 us (15%)
  other arithmetic  1.22 us (2%)
    ppermute x19, starting transfers between devices, swap(): return lax.ppermute(x, 'rep', [(i, i ^ mask) for i in range(members)])  25.5 us
    ppermute x19, waiting for transfers between devices, swap(): return lax.ppermute(x, 'rep', [(i, i ^ mask) for i in range(members)])  23 us
    pallas_call x1, Pallas kernels, attend(): pl.pallas_call(attend_kernel, out_shape=(pltpu.VMEM((requests, CUT), bf16...  3.18 us
    pallas_call x1, Pallas kernels, stage(): pl.pallas_call(stage_kernel, out_shape=pltpu.VMEM((WIDTH, 2 * ranks), jnp...  2.98 us
    pallas_call x1, Pallas kernels, project(): pl.pallas_call(functools.partial(project_kernel, 512), out_shape=(jax.Sha...  1.85 us
  transfers between devices with their start and end apart: 19, of which 11 were waited for; matrix products, arithmetic and copies ran while one was open for 0% of the time, Pallas kernels for 10%

profile of v4, /device:TPU:0, one launch (start us, length us, event | category | flops | bytes accessed | tf_op | source)
XLA Modules:
  0.0 58.9 jit_solution(18365764739826508244)
XLA Ops:
  0.0 0.5 collective-permute-start
  0.5 3.2 %attend.1 = (bf16[8,5888]{1,0:T(8,128)(2,1)S(1)}, bf16[8,8320]{1,0:T(8,128)(2,1)S(1)}) custom-call(s32[8]{0:T(128)} %length_hbm.1, s32[8]{0:T(128)} %adapter_hbm.1, s32[32]{0:T(128)} %slot_hbm.1, bf16[8,8192]{1,0:T(8,128)(2,1)} %query_hbm.1, bf16[8,2,1024]{2,1,0:T(2,128)(2,1)} %pair_hbm.1, bf16[8,2,128,1024]{3,2,1,0:T(8,128)(2,1)} %cache_hbm.1), custom_call_target="tpu_custom_call" | custom-call | flops 1000000000 | bytes 4194304 | tf_op jit(solution)/shard_map/attend/pallas_call | solution.py:143
  3.6 0.8 %collective-permute-done = bf16[2,64,8192]{2,1,0:T(8,128)(2,1)S(1)} collective-permute-done((bf16[2,64,8192]{2,1,0:T(8,128)(2,1)}, bf16[2,64,8192]{2,1,0:T(8,128)(2,1)S(1)}, u32[]{:S(2)}, u32[]{:S(2)}) %collective-permute-start) | collective-permute-done | bytes 2097184 | tf_op jit(solution)/shard_map/ppermute | solution.py:270
  4.5 0.0 copy-start.1
  4.5 5.0 %collective-permute-start.1 = (bf16[8,5888]{1,0:T(8,128)(2,1)S(1)}, bf16[8,5888]{1,0:T(8,128)(2,1)S(1)}, u32[]{:S(2)}, u32[]{:S(2)}) collective-permute-start(bf16[8,5888]{1,0:T(8,128)(2,1)S(1)} %get-tuple-element.20), channel_id=1, source_target_pairs={{0,12},{1,13},{2,14},{3,15},{4,8},{5,9},{6,10},{7,11},{8,4},{9,5},... | collective-permute-start | bytes 282632 | tf_op jit(solution)/shard_map/ppermute | solution.py:270
  9.4 1.5 %collective-permute-start.4 = (bf16[8,8320]{1,0:T(8,128)(2,1)S(1)}, bf16[8,8320]{1,0:T(8,128)(2,1)S(1)}, u32[]{:S(2)}, u32[]{:S(2)}) collective-permute-start(bf16[8,8320]{1,0:T(8,128)(2,1)S(1)} %get-tuple-element.19), channel_id=1, source_target_pairs={{0,2},{1,3},{2,0},{3,1},{4,6},{5,7},{6,4},{7,5},{8,10},{9,11},{10,... | collective-permute-start | bytes 399368 | tf_op jit(solution)/shard_map/ppermute | solution.py:270
  10.9 0.0 collective-permute-start.2
  11.0 0.8 %collective-permute-start.3 = (bf16[8,5888]{1,0:T(8,128)(2,1)S(1)}, bf16[8,5888]{1,0:T(8,128)(2,1)S(1)}, u32[]{:S(2)}, u32[]{:S(2)}) collective-permute-start(bf16[8,5888]{1,0:T(8,128)(2,1)S(1)} %get-tuple-element.20), channel_id=1, source_target_pairs={{0,4},{1,5},{2,6},{3,7},{4,0},{5,1},{6,2},{7,3},{8,12},{9,13},{10,... | collective-permute-start | bytes 282632 | tf_op jit(solution)/shard_map/ppermute | solution.py:270
  11.7 0.0 copy-done.1
  11.7 0.0 slice-start
  11.7 3.0 %stage.1.factors_ref = bf16[8192,256]{1,0:T(8,128)(2,1)S(1)} custom-call(bf16[128,8192]{1,0:T(8,128)(2,1)} %bitcast.72, bf16[128,8192]{1,0:T(8,128)(2,1)} %bitcast.73), custom_call_target="tpu_custom_call" | custom-call | flops 100000000 | bytes 8388608 | tf_op jit(solution)/shard_map/stage/pallas_call | solution.py:183
  14.7 0.0 copy-start
  14.7 0.0 collective-permute-done.1
  14.8 2.9 %collective-permute-done.2 = bf16[8,5888]{1,0:T(8,128)(2,1)S(1)} collective-permute-done((bf16[8,5888]{1,0:T(8,128)(2,1)S(1)}, bf16[8,5888]{1,0:T(8,128)(2,1)S(1)}, u32[]{:S(2)}, u32[]{:S(2)}) %collective-permute-start.2) | collective-permute-done | bytes 94240 | tf_op jit(solution)/shard_map/ppermute | solution.py:270
  17.7 0.0 collective-permute-done.4
  17.7 2.6 %collective-permute-start.5 = (bf16[16,2432]{1,0:T(8,128)(2,1)S(1)}, bf16[16,2432]{1,0:T(8,128)(2,1)S(1)}, u32[]{:S(2)}, u32[]{:S(2)}) collective-permute-start(bf16[16,2432]{1,0:T(8,128)(2,1)S(1)} %pad_maximum_fusion.1), channel_id=1, source_target_pairs={{0,12},{1,13},{2,14},{3,15},{4,8},{5,9},{6,10},{7,11},{8,4},{9,5},... | collective-permute-start | bytes 233480 | tf_op jit(solution)/shard_map/ppermute | solution.py:270
  20.3 0.0 collective-permute-start.6
  20.3 1.9 %collective-permute-start.7 = (bf16[16,2432]{1,0:T(8,128)(2,1)S(1)}, bf16[16,2432]{1,0:T(8,128)(2,1)S(1)}, u32[]{:S(2)}, u32[]{:S(2)}) collective-permute-start(bf16[16,2432]{1,0:T(8,128)(2,1)S(1)} %pad_maximum_fusion.1), channel_id=1, source_target_pairs={{0,4},{1,5},{2,6},{3,7},{4,0},{5,1},{6,2},{7,3},{8,12},{9,13},{10,... | collective-permute-start | bytes 233480 | tf_op jit(solution)/shard_map/ppermute | solution.py:270
  22.1 0.0 collective-permute-done.3
  22.2 1.6 %collective-permute-start.8 = (bf16[24,5888]{1,0:T(8,128)(2,1)S(1)}, bf16[24,5888]{1,0:T(8,128)(2,1)S(1)}, u32[]{:S(2)}, u32[]{:S(2)}) collective-permute-start(bf16[24,5888]{1,0:T(8,128)(2,1)S(1)} %constant_dynamic-update-slice_fusion), channel_id=1, source_target_pairs={{0,2},{1,3},{2,0},{3,1},{4,6},{5,7},{6,4},{7,5},{8,10},{9,11},{10,... | collective-permute-start | bytes 847880 | tf_op jit(solution)/shard_map/ppermute | solution.py:270
  23.7 0.7 %collective-permute-done.5 = bf16[16,2432]{1,0:T(8,128)(2,1)S(1)} collective-permute-done((bf16[16,2432]{1,0:T(8,128)(2,1)S(1)}, bf16[16,2432]{1,0:T(8,128)(2,1)S(1)}, u32[]{:S(2)}, u32[]{:S(2)}) %collective-permute-start.5) | collective-permute-done | bytes 77856 | tf_op jit(solution)/shard_map/ppermute | solution.py:270
  24.5 2.4 %collective-permute-done.6 = bf16[16,2432]{1,0:T(8,128)(2,1)S(1)} collective-permute-done((bf16[16,2432]{1,0:T(8,128)(2,1)S(1)}, bf16[16,2432]{1,0:T(8,128)(2,1)S(1)}, u32[]{:S(2)}, u32[]{:S(2)}) %collective-permute-start.6) | collective-permute-done | bytes 77856 | tf_op jit(solution)/shard_map/ppermute | solution.py:270
  26.8 0.0 collective-permute-done.7
  26.9 0.0 slice-start.1
  26.9 2.8 %collective-permute-done.8 = bf16[24,5888]{1,0:T(8,128)(2,1)S(1)} collective-permute-done((bf16[24,5888]{1,0:T(8,128)(2,1)S(1)}, bf16[24,5888]{1,0:T(8,128)(2,1)S(1)}, u32[]{:S(2)}, u32[]{:S(2)}) %collective-permute-start.8) | collective-permute-done | bytes 282656 | tf_op jit(solution)/shard_map/ppermute | solution.py:270
  29.7 0.1 maximum_maximum_fusion.rows_ref
  29.8 0.0 copy-done
  29.8 0.8 %shrink.1 = (bf16[64,640]{1,0:T(8,128)(2,1)S(1)}, bf16[64,640]{1,0:T(8,128)(2,1)S(1)}) custom-call(s32[1]{0:T(128)} %bitcast.device_ref, bf16[64,8320]{1,0:T(8,128)(2,1)S(1)} %maximum_maximum_fusion.rows_ref, bf16[8192,256]{1,0:T(8,128)(2,1)S(1)} %stage.1.factors_ref, bf16[2,64,8192]{2,1,0:T(8,128)(2,1)S(1)} %copy-done), custom_call_target="tpu_custom_call" | custom-call | flops 268435456 | bytes 4194304 | tf_op jit(solution)/shard_map/shrink/pallas_call | solution.py:219
  30.7 0.1 collective-permute-start.9
  30.8 1.3 %collective-permute-done.9.x_other_ref = bf16[64,640]{1,0:T(8,128)(2,1)S(1)} collective-permute-done((bf16[64,640]{1,0:T(8,128)(2,1)S(1)}, bf16[64,640]{1,0:T(8,128)(2,1)S(1)}, u32[]{:S(2)}, u32[]{:S(2)}) %collective-permute-start.9) | collective-permute-done | bytes 81952 | tf_op jit(solution)/shard_map/ppermute | solution.py:270
  32.0 0.0 slice-done
  32.0 0.0 slice-done.1
  32.0 1.8 %project.1 = (f32[64,8192]{1,0:T(8,128)S(1)}, bf16[64,8192]{1,0:T(8,128)(2,1)S(1)}) custom-call(bf16[64,640]{1,0:T(8,128)(2,1)S(1)} %get-tuple-element.22.x_ref, bf16[64,640]{1,0:T(8,128)(2,1)S(1)} %collective-permute-done.9.x_other_ref, bf16[512,8192]{1,0:T(8,128)(2,1)S(1)} %bitcast.64, bf16[2,64,8192]{2,1,0:T(8,128)(2,1)S(1)} %copy-done), custom_call_target="tpu_custom_call" | custom-call | flops 1342177280 | bytes 10485760 | tf_op jit(solution)/shard_map/project/pallas_call | solution.py:248
  33.9 0.2 collective-permute-start.10
  34.1 2.5 %collective-permute-done.10 = bf16[64,8192]{1,0:T(8,128)(2,1)S(1)} collective-permute-done((bf16[64,8192]{1,0:T(8,128)(2,1)S(1)}, bf16[64,8192]{1,0:T(8,128)(2,1)S(1)}, u32[]{:S(2)}, u32[]{:S(2)}) %collective-permute-start.10) | collective-permute-done | bytes 1048608 | tf_op jit(solution)/shard_map/ppermute | solution.py:270
  36.6 0.2 convert_add_fusion
  36.9 1.2 %collective-permute-start.11 = (bf16[3,8,5888]{2,1,0:T(8,128)(2,1)S(1)}, bf16[3,8,5888]{2,1,0:T(8,128)(2,1)S(1)}, u32[]{:S(2)}, u32[]{:S(2)}) collective-permute-start(bf16[3,8,5888]{2,1,0:T(8,128)(2,1)S(1)} %slice_bitcast_fusion.1), channel_id=1, source_target_pairs={{0,2},{1,3},{2,0},{3,1},{4,6},{5,7},{6,4},{7,5},{8,10},{9,11},{10,... | collective-permute-start | bytes 847880 | tf_op jit(solution)/shard_map/ppermute | solution.py:270
  38.2 2.6 %collective-permute-start.15 = (bf16[2,8,2304]{2,1,0:T(8,128)(2,1)S(1)}, bf16[2,8,2304]{2,1,0:T(8,128)(2,1)S(1)}, u32[]{:S(2)}, u32[]{:S(2)}) collective-permute-start(bf16[2,8,2304]{2,1,0:T(8,128)(2,1)S(1)} %get-tuple-element.31), channel_id=1, source_target_pairs={{0,12},{1,13},{2,14},{3,15},{4,8},{5,9},{6,10},{7,11},{8,4},{9,5},... | collective-permute-start | bytes 221192 | tf_op jit(solution)/shard_map/ppermute | solution.py:270
  40.7 0.0 collective-permute-start.16
  40.7 1.9 %collective-permute-start.17 = (bf16[2,8,2304]{2,1,0:T(8,128)(2,1)S(1)}, bf16[2,8,2304]{2,1,0:T(8,128)(2,1)S(1)}, u32[]{:S(2)}, u32[]{:S(2)}) collective-permute-start(bf16[2,8,2304]{2,1,0:T(8,128)(2,1)S(1)} %get-tuple-element.29), channel_id=1, source_target_pairs={{0,4},{1,5},{2,6},{3,7},{4,0},{5,1},{6,2},{7,3},{8,12},{9,13},{10,... | collective-permute-start | bytes 221192 | tf_op jit(solution)/shard_map/ppermute | solution.py:270
  42.6 3.2 %collective-permute-done.11 = bf16[3,8,5888]{2,1,0:T(8,128)(2,1)S(1)} collective-permute-done((bf16[3,8,5888]{2,1,0:T(8,128)(2,1)S(1)}, bf16[3,8,5888]{2,1,0:T(8,128)(2,1)S(1)}, u32[]{:S(2)}, u32[]{:S(2)}) %collective-permute-start.11) | collective-permute-done | bytes 282656 | tf_op jit(solution)/shard_map/ppermute | solution.py:270
  45.8 0.1 fusion.1
  45.9 0.0 collective-permute-done.15
  45.9 1.3 %collective-permute-done.16 = bf16[2,8,2304]{2,1,0:T(8,128)(2,1)S(1)} collective-permute-done((bf16[2,8,2304]{2,1,0:T(8,128)(2,1)S(1)}, bf16[2,8,2304]{2,1,0:T(8,128)(2,1)S(1)}, u32[]{:S(2)}, u32[]{:S(2)}) %collective-permute-start.16) | collective-permute-done | bytes 73760 | tf_op jit(solution)/shard_map/ppermute | solution.py:270
  47.2 0.0 collective-permute-done.17
  47.3 2.6 %collective-permute-start.12 = (bf16[8,5888]{1,0:T(8,128)(2,1)S(1)}, bf16[8,5888]{1,0:T(8,128)(2,1)S(1)}, u32[]{:S(2)}, u32[]{:S(2)}) collective-permute-start(bf16[8,5888]{1,0:T(8,128)(2,1)S(1)} %get-tuple-element.32), channel_id=1, source_target_pairs={{0,12},{1,13},{2,14},{3,15},{4,8},{5,9},{6,10},{7,11},{8,4},{9,5},... | collective-permute-start | bytes 282632 | tf_op jit(solution)/shard_map/ppermute | solution.py:270
  49.9 0.0 collective-permute-start.13
  49.9 1.9 %collective-permute-start.14 = (bf16[8,5888]{1,0:T(8,128)(2,1)S(1)}, bf16[8,5888]{1,0:T(8,128)(2,1)S(1)}, u32[]{:S(2)}, u32[]{:S(2)}) collective-permute-start(bf16[8,5888]{1,0:T(8,128)(2,1)S(1)} %get-tuple-element.33), channel_id=1, source_target_pairs={{0,4},{1,5},{2,6},{3,7},{4,0},{5,1},{6,2},{7,3},{8,12},{9,13},{10,... | collective-permute-start | bytes 282632 | tf_op jit(solution)/shard_map/ppermute | solution.py:270
  51.8 1.3 %collective-permute-start.18 = (bf16[8,8192]{1,0:T(8,128)(2,1)S(1)}, bf16[8,8192]{1,0:T(8,128)(2,1)S(1)}, u32[]{:S(2)}, u32[]{:S(2)}) collective-permute-start(bf16[8,8192]{1,0:T(8,128)(2,1)S(1)} %pad_maximum_fusion), channel_id=1, source_target_pairs={{0,2},{1,3},{2,0},{3,1},{4,6},{5,7},{6,4},{7,5},{8,10},{9,11},{10,... | collective-permute-start | bytes 393224 | tf_op jit(solution)/shard_map/ppermute | solution.py:270
  53.1 1.8 %collective-permute-done.12 = bf16[8,5888]{1,0:T(8,128)(2,1)S(1)} collective-permute-done((bf16[8,5888]{1,0:T(8,128)(2,1)S(1)}, bf16[8,5888]{1,0:T(8,128)(2,1)S(1)}, u32[]{:S(2)}, u32[]{:S(2)}) %collective-permute-start.12) | collective-permute-done | bytes 94240 | tf_op jit(solution)/shard_map/ppermute | solution.py:270
  54.8 3.4 %collective-permute-done.13 = bf16[8,5888]{1,0:T(8,128)(2,1)S(1)} collective-permute-done((bf16[8,5888]{1,0:T(8,128)(2,1)S(1)}, bf16[8,5888]{1,0:T(8,128)(2,1)S(1)}, u32[]{:S(2)}, u32[]{:S(2)}) %collective-permute-start.13) | collective-permute-done | bytes 94240 | tf_op jit(solution)/shard_map/ppermute | solution.py:270
  58.2 0.0 collective-permute-done.14
  58.2 0.0 collective-permute-done.18
  58.2 0.7 %fusion.2 = bf16[8,8192]{1,0:T(8,128)(2,1)} fusion(f32[8,2304]{1,0:T(8,128)S(1)} %slice_bitcast_fusion.10, f32[8,5888]{1,0:T(8,128)S(1)} %fusion.5, bf16[8,8192]{1,0:T(8,128)(2,1)S(1)} %collective-permute-done.18), kind=kLoop, calls=%fused_computation.7 | loop fusion | flops 262144 | bytes 524288 | tf_op jit(solution)/shard_map/convert_element_type | solution.py:316
  (18 shorter events, 0.3 us)
Async XLA Ops:
  0.0 4.5 %collective-permute-start = (bf16[2,64,8192]{2,1,0:T(8,128)(2,1)}, bf16[2,64,8192]{2,1,0:T(8,128)(2,1)S(1)}, u32[]{:S(2)}, u32[]{:S(2)}) collective-permute-start(bf16[2,64,8192]{2,1,0:T(8,128)(2,1)} %bitcast.71), channel_id=1, source_target_pairs={{0,1},{1,0},{2,3},{3,2},{4,5},{5,4},{6,7},{7,6},{8,9},{9,8},{10,11... | collective-permute-start | bytes 6291464 | tf_op jit(solution)/shard_map/ppermute | solution.py:270
  4.5 7.3 %copy-start.1 = (bf16[2,64,8192]{2,1,0:T(8,128)(2,1)}, bf16[2,64,8192]{2,1,0:T(8,128)(2,1)S(1)}, u32[]{:S(2)}) copy-start(bf16[2,64,8192]{2,1,0:T(8,128)(2,1)S(1)} %collective-permute-done) | copy-start | bytes 6291460
  4.5 10.3 %collective-permute-start.1 = (bf16[8,5888]{1,0:T(8,128)(2,1)S(1)}, bf16[8,5888]{1,0:T(8,128)(2,1)S(1)}, u32[]{:S(2)}, u32[]{:S(2)}) collective-permute-start(bf16[8,5888]{1,0:T(8,128)(2,1)S(1)} %get-tuple-element.20), channel_id=1, source_target_pairs={{0,12},{1,13},{2,14},{3,15},{4,8},{5,9},{6,10},{7,11},{8,4},{9,5},... | collective-permute-start | bytes 282632 | tf_op jit(solution)/shard_map/ppermute | solution.py:270
  9.4 8.2 %collective-permute-start.4 = (bf16[8,8320]{1,0:T(8,128)(2,1)S(1)}, bf16[8,8320]{1,0:T(8,128)(2,1)S(1)}, u32[]{:S(2)}, u32[]{:S(2)}) collective-permute-start(bf16[8,8320]{1,0:T(8,128)(2,1)S(1)} %get-tuple-element.19), channel_id=1, source_target_pairs={{0,2},{1,3},{2,0},{3,1},{4,6},{5,7},{6,4},{7,5},{8,10},{9,11},{10,... | collective-permute-start | bytes 399368 | tf_op jit(solution)/shard_map/ppermute | solution.py:270
  10.9 6.7 %collective-permute-start.2 = (bf16[8,5888]{1,0:T(8,128)(2,1)S(1)}, bf16[8,5888]{1,0:T(8,128)(2,1)S(1)}, u32[]{:S(2)}, u32[]{:S(2)}) collective-permute-start(bf16[8,5888]{1,0:T(8,128)(2,1)S(1)} %get-tuple-element.20), channel_id=1, source_target_pairs={{0,8},{1,9},{2,10},{3,11},{4,12},{5,13},{6,14},{7,15},{8,0},{9,1},... | collective-permute-start | bytes 282632 | tf_op jit(solution)/shard_map/ppermute | solution.py:270
  11.0 11.2 %collective-permute-start.3 = (bf16[8,5888]{1,0:T(8,128)(2,1)S(1)}, bf16[8,5888]{1,0:T(8,128)(2,1)S(1)}, u32[]{:S(2)}, u32[]{:S(2)}) collective-permute-start(bf16[8,5888]{1,0:T(8,128)(2,1)S(1)} %get-tuple-element.20), channel_id=1, source_target_pairs={{0,4},{1,5},{2,6},{3,7},{4,0},{5,1},{6,2},{7,3},{8,12},{9,13},{10,... | collective-permute-start | bytes 282632 | tf_op jit(solution)/shard_map/ppermute | solution.py:270
  11.7 20.3 %slice-start = ((s8[8388608]{0:T(1024)(128)(4,1)}), s8[4194304]{0:T(1024)(128)(4,1)S(1)}, s32[]{:S(2)}) async-start(s8[8388608]{0:T(1024)(128)(4,1)} %bitcast.63), calls=%async_computation | async-start | bytes 8388608
  14.7 15.1 %copy-start = (bf16[2,64,8192]{2,1,0:T(8,128)(2,1)S(1)}, bf16[2,64,8192]{2,1,0:T(8,128)(2,1)}, u32[]{:S(2)}) copy-start(bf16[2,64,8192]{2,1,0:T(8,128)(2,1)} %up_ref.3) | copy-start | bytes 6291460
  17.7 6.8 %collective-permute-start.5 = (bf16[16,2432]{1,0:T(8,128)(2,1)S(1)}, bf16[16,2432]{1,0:T(8,128)(2,1)S(1)}, u32[]{:S(2)}, u32[]{:S(2)}) collective-permute-start(bf16[16,2432]{1,0:T(8,128)(2,1)S(1)} %pad_maximum_fusion.1), channel_id=1, source_target_pairs={{0,12},{1,13},{2,14},{3,15},{4,8},{5,9},{6,10},{7,11},{8,4},{9,5},... | collective-permute-start | bytes 233480 | tf_op jit(solution)/shard_map/ppermute | solution.py:270
  20.3 6.5 %collective-permute-start.6 = (bf16[16,2432]{1,0:T(8,128)(2,1)S(1)}, bf16[16,2432]{1,0:T(8,128)(2,1)S(1)}, u32[]{:S(2)}, u32[]{:S(2)}) collective-permute-start(bf16[16,2432]{1,0:T(8,128)(2,1)S(1)} %pad_maximum_fusion.1), channel_id=1, source_target_pairs={{0,8},{1,9},{2,10},{3,11},{4,12},{5,13},{6,14},{7,15},{8,0},{9,1},... | collective-permute-start | bytes 233480 | tf_op jit(solution)/shard_map/ppermute | solution.py:270
  20.3 6.5 %collective-permute-start.7 = (bf16[16,2432]{1,0:T(8,128)(2,1)S(1)}, bf16[16,2432]{1,0:T(8,128)(2,1)S(1)}, u32[]{:S(2)}, u32[]{:S(2)}) collective-permute-start(bf16[16,2432]{1,0:T(8,128)(2,1)S(1)} %pad_maximum_fusion.1), channel_id=1, source_target_pairs={{0,4},{1,5},{2,6},{3,7},{4,0},{5,1},{6,2},{7,3},{8,12},{9,13},{10,... | collective-permute-start | bytes 233480 | tf_op jit(solution)/shard_map/ppermute | solution.py:270
  22.2 7.6 %collective-permute-start.8 = (bf16[24,5888]{1,0:T(8,128)(2,1)S(1)}, bf16[24,5888]{1,0:T(8,128)(2,1)S(1)}, u32[]{:S(2)}, u32[]{:S(2)}) collective-permute-start(bf16[24,5888]{1,0:T(8,128)(2,1)S(1)} %constant_dynamic-update-slice_fusion), channel_id=1, source_target_pairs={{0,2},{1,3},{2,0},{3,1},{4,6},{5,7},{6,4},{7,5},{8,10},{9,11},{10,... | collective-permute-start | bytes 847880 | tf_op jit(solution)/shard_map/ppermute | solution.py:270
  26.9 5.2 %slice-start.1 = ((s8[8388608]{0:T(1024)(128)(4,1)}), s8[4194304]{0:T(1024)(128)(4,1)S(1)}, s32[]{:S(2)}) async-start(s8[8388608]{0:T(1024)(128)(4,1)} %bitcast.63), calls=%async_computation.1 | async-start | bytes 8388608
  30.7 1.3 %collective-permute-start.9 = (bf16[64,640]{1,0:T(8,128)(2,1)S(1)}, bf16[64,640]{1,0:T(8,128)(2,1)S(1)}, u32[]{:S(2)}, u32[]{:S(2)}) collective-permute-start(bf16[64,640]{1,0:T(8,128)(2,1)S(1)} %get-tuple-element.23), channel_id=1, source_target_pairs={{0,1},{1,0},{2,3},{3,2},{4,5},{5,4},{6,7},{7,6},{8,9},{9,8},{10,11... | collective-permute-start | bytes 245768 | tf_op jit(solution)/shard_map/ppermute | solution.py:270
  33.9 2.7 %collective-permute-start.10 = (bf16[64,8192]{1,0:T(8,128)(2,1)S(1)}, bf16[64,8192]{1,0:T(8,128)(2,1)S(1)}, u32[]{:S(2)}, u32[]{:S(2)}) collective-permute-start(bf16[64,8192]{1,0:T(8,128)(2,1)S(1)} %get-tuple-element.25), channel_id=1, source_target_pairs={{0,1},{1,0},{2,3},{3,2},{4,5},{5,4},{6,7},{7,6},{8,9},{9,8},{10,11... | collective-permute-start | bytes 3145736 | tf_op jit(solution)/shard_map/ppermute | solution.py:270
  36.9 8.9 %collective-permute-start.11 = (bf16[3,8,5888]{2,1,0:T(8,128)(2,1)S(1)}, bf16[3,8,5888]{2,1,0:T(8,128)(2,1)S(1)}, u32[]{:S(2)}, u32[]{:S(2)}) collective-permute-start(bf16[3,8,5888]{2,1,0:T(8,128)(2,1)S(1)} %slice_bitcast_fusion.1), channel_id=1, source_target_pairs={{0,2},{1,3},{2,0},{3,1},{4,6},{5,7},{6,4},{7,5},{8,10},{9,11},{10,... | collective-permute-start | bytes 847880 | tf_op jit(solution)/shard_map/ppermute | solution.py:270
  38.2 7.7 %collective-permute-start.15 = (bf16[2,8,2304]{2,1,0:T(8,128)(2,1)S(1)}, bf16[2,8,2304]{2,1,0:T(8,128)(2,1)S(1)}, u32[]{:S(2)}, u32[]{:S(2)}) collective-permute-start(bf16[2,8,2304]{2,1,0:T(8,128)(2,1)S(1)} %get-tuple-element.31), channel_id=1, source_target_pairs={{0,12},{1,13},{2,14},{3,15},{4,8},{5,9},{6,10},{7,11},{8,4},{9,5},... | collective-permute-start | bytes 221192 | tf_op jit(solution)/shard_map/ppermute | solution.py:270
  40.7 6.5 %collective-permute-start.16 = (bf16[2,8,2304]{2,1,0:T(8,128)(2,1)S(1)}, bf16[2,8,2304]{2,1,0:T(8,128)(2,1)S(1)}, u32[]{:S(2)}, u32[]{:S(2)}) collective-permute-start(bf16[2,8,2304]{2,1,0:T(8,128)(2,1)S(1)} %get-tuple-element.30), channel_id=1, source_target_pairs={{0,8},{1,9},{2,10},{3,11},{4,12},{5,13},{6,14},{7,15},{8,0},{9,1},... | collective-permute-start | bytes 221192 | tf_op jit(solution)/shard_map/ppermute | solution.py:270
  40.7 6.5 %collective-permute-start.17 = (bf16[2,8,2304]{2,1,0:T(8,128)(2,1)S(1)}, bf16[2,8,2304]{2,1,0:T(8,128)(2,1)S(1)}, u32[]{:S(2)}, u32[]{:S(2)}) collective-permute-start(bf16[2,8,2304]{2,1,0:T(8,128)(2,1)S(1)} %get-tuple-element.29), channel_id=1, source_target_pairs={{0,4},{1,5},{2,6},{3,7},{4,0},{5,1},{6,2},{7,3},{8,12},{9,13},{10,... | collective-permute-start | bytes 221192 | tf_op jit(solution)/shard_map/ppermute | solution.py:270
  47.3 7.5 %collective-permute-start.12 = (bf16[8,5888]{1,0:T(8,128)(2,1)S(1)}, bf16[8,5888]{1,0:T(8,128)(2,1)S(1)}, u32[]{:S(2)}, u32[]{:S(2)}) collective-permute-start(bf16[8,5888]{1,0:T(8,128)(2,1)S(1)} %get-tuple-element.32), channel_id=1, source_target_pairs={{0,12},{1,13},{2,14},{3,15},{4,8},{5,9},{6,10},{7,11},{8,4},{9,5},... | collective-permute-start | bytes 282632 | tf_op jit(solution)/shard_map/ppermute | solution.py:270
  49.9 8.3 %collective-permute-start.13 = (bf16[8,5888]{1,0:T(8,128)(2,1)S(1)}, bf16[8,5888]{1,0:T(8,128)(2,1)S(1)}, u32[]{:S(2)}, u32[]{:S(2)}) collective-permute-start(bf16[8,5888]{1,0:T(8,128)(2,1)S(1)} %get-tuple-element.34), channel_id=1, source_target_pairs={{0,8},{1,9},{2,10},{3,11},{4,12},{5,13},{6,14},{7,15},{8,0},{9,1},... | collective-permute-start | bytes 282632 | tf_op jit(solution)/shard_map/ppermute | solution.py:270
  49.9 8.3 %collective-permute-start.14 = (bf16[8,5888]{1,0:T(8,128)(2,1)S(1)}, bf16[8,5888]{1,0:T(8,128)(2,1)S(1)}, u32[]{:S(2)}, u32[]{:S(2)}) collective-permute-start(bf16[8,5888]{1,0:T(8,128)(2,1)S(1)} %get-tuple-element.33), channel_id=1, source_target_pairs={{0,4},{1,5},{2,6},{3,7},{4,0},{5,1},{6,2},{7,3},{8,12},{9,13},{10,... | collective-permute-start | bytes 282632 | tf_op jit(solution)/shard_map/ppermute | solution.py:270
  51.8 6.5 %collective-permute-start.18 = (bf16[8,8192]{1,0:T(8,128)(2,1)S(1)}, bf16[8,8192]{1,0:T(8,128)(2,1)S(1)}, u32[]{:S(2)}, u32[]{:S(2)}) collective-permute-start(bf16[8,8192]{1,0:T(8,128)(2,1)S(1)} %pad_maximum_fusion), channel_id=1, source_target_pairs={{0,2},{1,3},{2,0},{3,1},{4,6},{5,7},{6,4},{7,5},{8,10},{9,11},{10,... | collective-permute-start | bytes 393224 | tf_op jit(solution)/shard_map/ppermute | solution.py:270

commit v5 on v4

--- a/solution.py
+++ b/solution.py
@@ -17,7 +17,8 @@
 ADAPTER_GAIN = 2.0
 MASKED_SCORE = -1e30
 
-CUT = 5888
+GATHER_CUT = 6144
+SCATTER_CUT = 6144
 
 NT = (((1,), (1,)), ((), ()))
 VMEM = pl.BlockSpec(memory_space=pltpu.VMEM)
@@ -143,7 +144,7 @@
     return pl.pallas_call(
         attend_kernel,
         out_shape=(
-            pltpu.VMEM((requests, CUT), bf16),
+            pltpu.VMEM((requests, GATHER_CUT), bf16),
             pltpu.VMEM((requests, WIDTH + LANES), bf16),
         ),
         in_specs=[HBM] * 6,
@@ -163,7 +164,8 @@
     )(*(pltpu.with_memory_space_constraint(x, pltpu.HBM) for x in inputs))
 
 
-def stage_kernel(down_ref, down_other_ref, out_ref, held, sems):
+def stage_kernel(down_ref, down_other_ref, up_ref, out_ref, held, sems):
+    del up_ref
     ranks = held.shape[1]
     copies = [
         pltpu.make_async_copy(ref, held.at[i], sems.at[i])
@@ -177,13 +179,13 @@
             out_ref[k : k + 1024, i * ranks : (i + 1) * ranks] = held[i, :, k : k + 1024].T
 
 
-def stage(down, down_other):
+def stage(down, down_other, up):
     ranks = down.shape[0] * down.shape[1]
     pair = [x.reshape(ranks, WIDTH) for x in (down, down_other)]
     return pl.pallas_call(
         stage_kernel,
         out_shape=pltpu.VMEM((WIDTH, 2 * ranks), jnp.bfloat16),
-        in_specs=[HBM] * 2,
+        in_specs=[HBM, HBM, VMEM],
         out_specs=VMEM,
         scratch_shapes=[
             pltpu.VMEM((2, ranks, WIDTH), jnp.bfloat16),
@@ -192,11 +194,11 @@
         compiler_params=pltpu.CompilerParams(vmem_limit_bytes=16 << 20),
         cost_estimate=cost(10**8, 8 * ranks * WIDTH),
         name="stage",
-    )(*(pltpu.with_memory_space_constraint(x, pltpu.HBM) for x in pair))
-
-
-def shrink_kernel(device_ref, rows_ref, factors_ref, up_ref, own_ref, other_ref):
-    held, rank = up_ref.shape[0], up_ref.shape[1]
+    )(*(pltpu.with_memory_space_constraint(x, pltpu.HBM) for x in pair), held_in_vmem(up))
+
+
+def shrink_kernel(held, rank, device_ref, rows_ref, factors_ref, weight_ref, own_ref, other_ref):
+    del weight_ref
     half = rows_ref.shape[0]
     ranks = held * rank
     head = own_ref.shape[1] - ranks
@@ -212,19 +214,19 @@
         ref[:, :head] = rows_ref[:, pl.ds(pl.multiple_of(device * head, head), head)]
 
 
-def shrink(device, rows, factors, up, head):
-    half = rows.shape[0]
+def shrink(device, rows, factors, up, weight):
+    half, head = rows.shape[0], weight.shape[0]
     ranks = up.shape[0] * up.shape[1]
     out = jax.ShapeDtypeStruct((half, head + ranks), jnp.bfloat16)
     return pl.pallas_call(
-        shrink_kernel,
+        functools.partial(shrink_kernel, up.shape[0], up.shape[1]),
         out_shape=(out, out),
         in_specs=[SMEM] + [VMEM] * 3,
         out_specs=(VMEM, VMEM),
         compiler_params=pltpu.CompilerParams(vmem_limit_bytes=16 << 20),
         cost_estimate=cost(4 * half * ranks * WIDTH, 4 * ranks * WIDTH),
         name="shrink",
-    )(device, rows, held_in_vmem(factors), held_in_vmem(up))
+    )(device, rows, held_in_vmem(factors), held_in_vmem(weight))
 
 
 def project_kernel(tile, x_ref, x_other_ref, weight_ref, up_ref, own_ref, other_ref):
@@ -276,16 +278,17 @@
 
     down = jnp.swapaxes(adapter_down, 1, 2)
     down_other, a, own = lax.optimization_barrier((swap(down, 1), a, own))
-    factors = stage(down, down_other)
+    factors = stage(down, down_other, adapter_up)
 
     apart = range(depths - 1, 0, -1)
     a_far = jnp.concatenate([swap(a, 4 * d) for d in apart], axis=0)
     side = swap(own, 2)
-    b_sides = jnp.concatenate([own[:, CUT:], side[:, CUT:]], axis=0)
-    b_far = jnp.stack([swap(b_sides, 4 * d) for d in apart], axis=0)
+    b_sides = jnp.concatenate([own[:, GATHER_CUT:], side[:, GATHER_CUT:]], axis=0)
+    a_side = swap(a_far, 2)
+    b_far, _ = lax.optimization_barrier(([swap(b_sides, 4 * d) for d in apart], a_side))
+    b_far = jnp.stack(b_far, axis=0)
     b_far = jnp.swapaxes(b_far.reshape(depths - 1, 2, requests, -1), 0, 1)
     b_far = b_far.reshape(2, (depths - 1) * requests, -1)
-    a_side = swap(a_far, 2)
     rows = jnp.concatenate(
         [
             own, jnp.concatenate([a_far, b_far[0]], axis=1),
@@ -295,12 +298,12 @@
     )
 
     device = lax.axis_index("rep").astype(jnp.int32).reshape(1)
-    x, x_send = shrink(device, rows, factors, adapter_up, out_weight.shape[0])
+    x, x_send = shrink(device, rows, factors, adapter_up, out_weight)
     x_other = swap(x_send, 1)
 
     mine, send = project(x, x_other, out_weight, adapter_up)
     sums = (mine + swap(send, 1).astype(f32)).reshape(2, depths, requests, WIDTH)
-    a_sum, b_sum = sums[..., :CUT], sums[..., CUT:]
+    a_sum, b_sum = sums[..., :SCATTER_CUT], sums[..., SCATTER_CUT:]
     a_part = a_sum[0, 1:] + swap(a_sum[1, 1:].astype(bf16), 2).astype(f32)
     b_send = b_sum.astype(bf16)
     a_send = a_part.astype(bf16)

time: 59.1 us -> 57 us (0.964)
  waiting for transfers between devices: 23 us -> 21.1 us
    ppermute x19, waiting for transfers between devices: 23 us -> 21.1 us  [swap(): return lax.ppermute(x, 'rep', [(i, i ^ mask) for i in range(members)])]
  transfers between devices with their start and end apart: 19 -> 19, of which waited for: 11 -> 9; matrix products, arithmetic and copies ran while one was open for 0% -> 0% of each run, Pallas kernels for 10% -> 11%
where the time goes in v5:
time: 57 us; the launch traced here: 56.8 us
  starting transfers between devices  25 us (44%)
  waiting for transfers between devices  21.1 us (37%)
  Pallas kernels  8.97 us (16%)
  other arithmetic  1.22 us (2%)
    ppermute x19, starting transfers between devices, swap(): return lax.ppermute(x, 'rep', [(i, i ^ mask) for i in range(members)])  25 us
    ppermute x19, waiting for transfers between devices, swap(): return lax.ppermute(x, 'rep', [(i, i ^ mask) for i in range(members)])  21.1 us
    pallas_call x1, Pallas kernels, attend(): pl.pallas_call(attend_kernel, out_shape=(pltpu.VMEM((requests, GATHER_CUT...  3.34 us
    pallas_call x1, Pallas kernels, stage(): pl.pallas_call(stage_kernel, out_shape=pltpu.VMEM((WIDTH, 2 * ranks), jnp...  2.98 us
    pallas_call x1, Pallas kernels, project(): pl.pallas_call(functools.partial(project_kernel, 512), out_shape=(jax.Sha...  1.8 us
  transfers between devices with their start and end apart: 19, of which 9 were waited for; matrix products, arithmetic and copies ran while one was open for 0% of the time, Pallas kernels for 11%

profile of v5, /device:TPU:0, one launch (start us, length us, event | category | flops | bytes accessed | tf_op | source)
XLA Modules:
  0.0 56.8 jit_solution(5153587838756752443)
XLA Ops:
  0.0 0.0 copy-start.1
  0.0 0.5 collective-permute-start
  0.5 3.3 %attend.1 = (bf16[8,6144]{1,0:T(8,128)(2,1)S(1)}, bf16[8,8320]{1,0:T(8,128)(2,1)S(1)}) custom-call(s32[8]{0:T(128)} %length_hbm.1, s32[8]{0:T(128)} %adapter_hbm.1, s32[32]{0:T(128)} %slot_hbm.1, bf16[8,8192]{1,0:T(8,128)(2,1)} %query_hbm.1, bf16[8,2,1024]{2,1,0:T(2,128)(2,1)} %pair_hbm.1, bf16[8,2,128,1024]{3,2,1,0:T(8,128)(2,1)} %cache_hbm.1), custom_call_target="tpu_custom_call" | custom-call | flops 1000000000 | bytes 4194304 | tf_op jit(solution)/shard_map/attend/pallas_call | solution.py:144
  3.8 0.6 %collective-permute-done = bf16[2,64,8192]{2,1,0:T(8,128)(2,1)S(1)} collective-permute-done((bf16[2,64,8192]{2,1,0:T(8,128)(2,1)}, bf16[2,64,8192]{2,1,0:T(8,128)(2,1)S(1)}, u32[]{:S(2)}, u32[]{:S(2)}) %collective-permute-start) | collective-permute-done | bytes 2097184 | tf_op jit(solution)/shard_map/ppermute | solution.py:272
  4.5 0.0 copy-start.2
  4.5 5.0 %collective-permute-start.1 = (bf16[8,6144]{1,0:T(8,128)(2,1)S(1)}, bf16[8,6144]{1,0:T(8,128)(2,1)S(1)}, u32[]{:S(2)}, u32[]{:S(2)}) collective-permute-start(bf16[8,6144]{1,0:T(8,128)(2,1)S(1)} %get-tuple-element.23), channel_id=1, source_target_pairs={{0,12},{1,13},{2,14},{3,15},{4,8},{5,9},{6,10},{7,11},{8,4},{9,5},... | collective-permute-start | bytes 294920 | tf_op jit(solution)/shard_map/ppermute | solution.py:272
  9.4 0.0 collective-permute-start.2
  9.4 0.6 collective-permute-start.3
  10.0 1.7 %collective-permute-start.4 = (bf16[8,8320]{1,0:T(8,128)(2,1)S(1)}, bf16[8,8320]{1,0:T(8,128)(2,1)S(1)}, u32[]{:S(2)}, u32[]{:S(2)}) collective-permute-start(bf16[8,8320]{1,0:T(8,128)(2,1)S(1)} %get-tuple-element.22), channel_id=1, source_target_pairs={{0,2},{1,3},{2,0},{3,1},{4,6},{5,7},{6,4},{7,5},{8,10},{9,11},{10,... | collective-permute-start | bytes 399368 | tf_op jit(solution)/shard_map/ppermute | solution.py:272
  11.7 1.4 %collective-permute-done.1 = bf16[8,6144]{1,0:T(8,128)(2,1)S(1)} collective-permute-done((bf16[8,6144]{1,0:T(8,128)(2,1)S(1)}, bf16[8,6144]{1,0:T(8,128)(2,1)S(1)}, u32[]{:S(2)}, u32[]{:S(2)}) %collective-permute-start.1) | collective-permute-done | bytes 98336 | tf_op jit(solution)/shard_map/ppermute | solution.py:272
  13.1 4.9 %collective-permute-done.2 = bf16[8,6144]{1,0:T(8,128)(2,1)S(1)} collective-permute-done((bf16[8,6144]{1,0:T(8,128)(2,1)S(1)}, bf16[8,6144]{1,0:T(8,128)(2,1)S(1)}, u32[]{:S(2)}, u32[]{:S(2)}) %collective-permute-start.2) | collective-permute-done | bytes 98336 | tf_op jit(solution)/shard_map/ppermute | solution.py:272
  18.0 0.0 collective-permute-done.3
  18.0 1.6 %collective-permute-start.8 = (bf16[24,6144]{1,0:T(8,128)(2,1)S(1)}, bf16[24,6144]{1,0:T(8,128)(2,1)S(1)}, u32[]{:S(2)}, u32[]{:S(2)}) collective-permute-start(bf16[24,6144]{1,0:T(8,128)(2,1)S(1)} %constant_dynamic-update-slice_fusion), channel_id=1, source_target_pairs={{0,2},{1,3},{2,0},{3,1},{4,6},{5,7},{6,4},{7,5},{8,10},{9,11},{10,... | collective-permute-start | bytes 884744 | tf_op jit(solution)/shard_map/ppermute | solution.py:272
  19.6 0.0 collective-permute-done.4
  19.6 0.0 copy-done.2
  19.6 2.5 %collective-permute-start.5 = (bf16[16,2176]{1,0:T(8,128)(2,1)S(1)}, bf16[16,2176]{1,0:T(8,128)(2,1)S(1)}, u32[]{:S(2)}, u32[]{:S(2)}) collective-permute-start(bf16[16,2176]{1,0:T(8,128)(2,1)S(1)} %pad_maximum_fusion.1), channel_id=1, source_target_pairs={{0,12},{1,13},{2,14},{3,15},{4,8},{5,9},{6,10},{7,11},{8,4},{9,5},... | collective-permute-start | bytes 208904 | tf_op jit(solution)/shard_map/ppermute | solution.py:272
  22.2 0.0 collective-permute-start.6
  22.2 1.9 %collective-permute-start.7 = (bf16[16,2176]{1,0:T(8,128)(2,1)S(1)}, bf16[16,2176]{1,0:T(8,128)(2,1)S(1)}, u32[]{:S(2)}, u32[]{:S(2)}) collective-permute-start(bf16[16,2176]{1,0:T(8,128)(2,1)S(1)} %pad_maximum_fusion.1), channel_id=1, source_target_pairs={{0,4},{1,5},{2,6},{3,7},{4,0},{5,1},{6,2},{7,3},{8,12},{9,13},{10,... | collective-permute-start | bytes 208904 | tf_op jit(solution)/shard_map/ppermute | solution.py:272
  24.1 0.0 copy-done.1
  24.1 0.0 copy-start
  24.1 3.0 %stage.1.factors_ref = bf16[8192,256]{1,0:T(8,128)(2,1)S(1)} custom-call(bf16[128,8192]{1,0:T(8,128)(2,1)} %bitcast.70, bf16[128,8192]{1,0:T(8,128)(2,1)} %bitcast.71, bf16[2,64,8192]{2,1,0:T(8,128)(2,1)S(1)} %copy-done.1), custom_call_target="tpu_custom_call" | custom-call | flops 100000000 | bytes 8388608 | tf_op jit(solution)/shard_map/stage/pallas_call | solution.py:185
  27.1 0.0 collective-permute-done.5
  27.1 1.2 %collective-permute-done.6 = bf16[16,2176]{1,0:T(8,128)(2,1)S(1)} collective-permute-done((bf16[16,2176]{1,0:T(8,128)(2,1)S(1)}, bf16[16,2176]{1,0:T(8,128)(2,1)S(1)}, u32[]{:S(2)}, u32[]{:S(2)}) %collective-permute-start.6) | collective-permute-done | bytes 69664 | tf_op jit(solution)/shard_map/ppermute | solution.py:272
  28.4 0.0 collective-permute-done.7
  28.4 0.0 collective-permute-done.8
  28.4 0.1 maximum_maximum_fusion.rows_ref
  28.5 0.2 copy-done
  28.7 0.8 %shrink.1 = (bf16[64,640]{1,0:T(8,128)(2,1)S(1)}, bf16[64,640]{1,0:T(8,128)(2,1)S(1)}) custom-call(s32[1]{0:T(128)} %bitcast.device_ref, bf16[64,8320]{1,0:T(8,128)(2,1)S(1)} %maximum_maximum_fusion.rows_ref, bf16[8192,256]{1,0:T(8,128)(2,1)S(1)} %stage.1.factors_ref, bf16[512,8192]{1,0:T(8,128)(2,1)S(1)} %copy-done), custom_call_target="tpu_custom_call" | custom-call | flops 268435456 | bytes 4194304 | tf_op jit(solution)/shard_map/shrink/pallas_call | solution.py:221
  29.6 0.1 collective-permute-start.9
  29.7 1.3 %collective-permute-done.9.x_other_ref = bf16[64,640]{1,0:T(8,128)(2,1)S(1)} collective-permute-done((bf16[64,640]{1,0:T(8,128)(2,1)S(1)}, bf16[64,640]{1,0:T(8,128)(2,1)S(1)}, u32[]{:S(2)}, u32[]{:S(2)}) %collective-permute-start.9) | collective-permute-done | bytes 81952 | tf_op jit(solution)/shard_map/ppermute | solution.py:272
  30.9 1.8 %project.1 = (f32[64,8192]{1,0:T(8,128)S(1)}, bf16[64,8192]{1,0:T(8,128)(2,1)S(1)}) custom-call(bf16[64,640]{1,0:T(8,128)(2,1)S(1)} %get-tuple-element.28.x_ref, bf16[64,640]{1,0:T(8,128)(2,1)S(1)} %collective-permute-done.9.x_other_ref, bf16[512,8192]{1,0:T(8,128)(2,1)S(1)} %copy-done, bf16[2,64,8192]{2,1,0:T(8,128)(2,1)S(1)} %copy-done.1), custom_call_target="tpu_custom_call" | custom-call | flops 1342177280 | bytes 10485760 | tf_op jit(solution)/shard_map/project/pallas_call | solution.py:250
  32.7 0.2 collective-permute-start.10
  33.0 2.5 %collective-permute-done.10 = bf16[64,8192]{1,0:T(8,128)(2,1)S(1)} collective-permute-done((bf16[64,8192]{1,0:T(8,128)(2,1)S(1)}, bf16[64,8192]{1,0:T(8,128)(2,1)S(1)}, u32[]{:S(2)}, u32[]{:S(2)}) %collective-permute-start.10) | collective-permute-done | bytes 1048608 | tf_op jit(solution)/shard_map/ppermute | solution.py:272
  35.5 0.2 convert_add_fusion
  35.8 0.6 %collective-permute-start.11 = (bf16[3,8,6144]{2,1,0:T(8,128)(2,1)S(1)}, bf16[3,8,6144]{2,1,0:T(8,128)(2,1)S(1)}, u32[]{:S(2)}, u32[]{:S(2)}) collective-permute-start(bf16[3,8,6144]{2,1,0:T(8,128)(2,1)S(1)} %slice_bitcast_fusion.1), channel_id=1, source_target_pairs={{0,2},{1,3},{2,0},{3,1},{4,6},{5,7},{6,4},{7,5},{8,10},{9,11},{10,... | collective-permute-start | bytes 884744 | tf_op jit(solution)/shard_map/ppermute | solution.py:272
  36.4 2.5 %collective-permute-start.15 = (bf16[2,8,2048]{2,1,0:T(8,128)(2,1)S(1)}, bf16[2,8,2048]{2,1,0:T(8,128)(2,1)S(1)}, u32[]{:S(2)}, u32[]{:S(2)}) collective-permute-start(bf16[2,8,2048]{2,1,0:T(8,128)(2,1)S(1)} %get-tuple-element.37), channel_id=1, source_target_pairs={{0,12},{1,13},{2,14},{3,15},{4,8},{5,9},{6,10},{7,11},{8,4},{9,5},... | collective-permute-start | bytes 196616 | tf_op jit(solution)/shard_map/ppermute | solution.py:272
  38.9 0.0 collective-permute-start.16
  38.9 1.9 %collective-permute-start.17 = (bf16[2,8,2048]{2,1,0:T(8,128)(2,1)S(1)}, bf16[2,8,2048]{2,1,0:T(8,128)(2,1)S(1)}, u32[]{:S(2)}, u32[]{:S(2)}) collective-permute-start(bf16[2,8,2048]{2,1,0:T(8,128)(2,1)S(1)} %get-tuple-element.35), channel_id=1, source_target_pairs={{0,4},{1,5},{2,6},{3,7},{4,0},{5,1},{6,2},{7,3},{8,12},{9,13},{10,... | collective-permute-start | bytes 196616 | tf_op jit(solution)/shard_map/ppermute | solution.py:272
  40.8 4.1 %collective-permute-done.11 = bf16[3,8,6144]{2,1,0:T(8,128)(2,1)S(1)} collective-permute-done((bf16[3,8,6144]{2,1,0:T(8,128)(2,1)S(1)}, bf16[3,8,6144]{2,1,0:T(8,128)(2,1)S(1)}, u32[]{:S(2)}, u32[]{:S(2)}) %collective-permute-start.11) | collective-permute-done | bytes 294944 | tf_op jit(solution)/shard_map/ppermute | solution.py:272
  44.9 0.1 fusion.1
  45.0 0.0 collective-permute-done.15
  45.0 0.0 collective-permute-done.16
  45.0 0.0 collective-permute-done.17
  45.1 2.5 %collective-permute-start.12 = (bf16[8,6144]{1,0:T(8,128)(2,1)S(1)}, bf16[8,6144]{1,0:T(8,128)(2,1)S(1)}, u32[]{:S(2)}, u32[]{:S(2)}) collective-permute-start(bf16[8,6144]{1,0:T(8,128)(2,1)S(1)} %get-tuple-element.38), channel_id=1, source_target_pairs={{0,12},{1,13},{2,14},{3,15},{4,8},{5,9},{6,10},{7,11},{8,4},{9,5},... | collective-permute-start | bytes 294920 | tf_op jit(solution)/shard_map/ppermute | solution.py:272
  47.6 0.0 collective-permute-start.13
  47.6 1.9 %collective-permute-start.14 = (bf16[8,6144]{1,0:T(8,128)(2,1)S(1)}, bf16[8,6144]{1,0:T(8,128)(2,1)S(1)}, u32[]{:S(2)}, u32[]{:S(2)}) collective-permute-start(bf16[8,6144]{1,0:T(8,128)(2,1)S(1)} %get-tuple-element.39), channel_id=1, source_target_pairs={{0,4},{1,5},{2,6},{3,7},{4,0},{5,1},{6,2},{7,3},{8,12},{9,13},{10,... | collective-permute-start | bytes 294920 | tf_op jit(solution)/shard_map/ppermute | solution.py:272
  49.6 1.5 %collective-permute-start.18 = (bf16[8,8192]{1,0:T(8,128)(2,1)S(1)}, bf16[8,8192]{1,0:T(8,128)(2,1)S(1)}, u32[]{:S(2)}, u32[]{:S(2)}) collective-permute-start(bf16[8,8192]{1,0:T(8,128)(2,1)S(1)} %pad_maximum_fusion), channel_id=1, source_target_pairs={{0,2},{1,3},{2,0},{3,1},{4,6},{5,7},{6,4},{7,5},{8,10},{9,11},{10,... | collective-permute-start | bytes 393224 | tf_op jit(solution)/shard_map/ppermute | solution.py:272
  51.0 1.7 %collective-permute-done.12 = bf16[8,6144]{1,0:T(8,128)(2,1)S(1)} collective-permute-done((bf16[8,6144]{1,0:T(8,128)(2,1)S(1)}, bf16[8,6144]{1,0:T(8,128)(2,1)S(1)}, u32[]{:S(2)}, u32[]{:S(2)}) %collective-permute-start.12) | collective-permute-done | bytes 98336 | tf_op jit(solution)/shard_map/ppermute | solution.py:272
  52.7 3.4 %collective-permute-done.13 = bf16[8,6144]{1,0:T(8,128)(2,1)S(1)} collective-permute-done((bf16[8,6144]{1,0:T(8,128)(2,1)S(1)}, bf16[8,6144]{1,0:T(8,128)(2,1)S(1)}, u32[]{:S(2)}, u32[]{:S(2)}) %collective-permute-start.13) | collective-permute-done | bytes 98336 | tf_op jit(solution)/shard_map/ppermute | solution.py:272
  56.1 0.0 collective-permute-done.14
  56.1 0.1 fusion.5
  56.1 0.0 collective-permute-done.18
  56.2 0.7 %fusion.2 = bf16[8,8192]{1,0:T(8,128)(2,1)} fusion(f32[8,2048]{1,0:T(8,128)S(1)} %slice_bitcast_fusion.10, f32[8,6144]{1,0:T(8,128)S(1)} %fusion.5, bf16[8,8192]{1,0:T(8,128)(2,1)S(1)} %collective-permute-done.18), kind=kLoop, calls=%fused_computation.7 | loop fusion | flops 262144 | bytes 524288 | tf_op jit(solution)/shard_map/convert_element_type | solution.py:319
  (16 shorter events, 0.2 us)
Async XLA Ops:
  0.0 24.1 %copy-start.1 = (bf16[2,64,8192]{2,1,0:T(8,128)(2,1)S(1)}, bf16[2,64,8192]{2,1,0:T(8,128)(2,1)}, u32[]{:S(2)}) copy-start(bf16[2,64,8192]{2,1,0:T(8,128)(2,1)} %up_ref.3) | copy-start | bytes 6291460
  0.0 4.5 %collective-permute-start = (bf16[2,64,8192]{2,1,0:T(8,128)(2,1)}, bf16[2,64,8192]{2,1,0:T(8,128)(2,1)S(1)}, u32[]{:S(2)}, u32[]{:S(2)}) collective-permute-start(bf16[2,64,8192]{2,1,0:T(8,128)(2,1)} %bitcast.69), channel_id=1, source_target_pairs={{0,1},{1,0},{2,3},{3,2},{4,5},{5,4},{6,7},{7,6},{8,9},{9,8},{10,11... | collective-permute-start | bytes 6291464 | tf_op jit(solution)/shard_map/ppermute | solution.py:272
  4.5 15.2 %copy-start.2 = (bf16[2,64,8192]{2,1,0:T(8,128)(2,1)}, bf16[2,64,8192]{2,1,0:T(8,128)(2,1)S(1)}, u32[]{:S(2)}) copy-start(bf16[2,64,8192]{2,1,0:T(8,128)(2,1)S(1)} %collective-permute-done) | copy-start | bytes 6291460
  4.5 8.6 %collective-permute-start.1 = (bf16[8,6144]{1,0:T(8,128)(2,1)S(1)}, bf16[8,6144]{1,0:T(8,128)(2,1)S(1)}, u32[]{:S(2)}, u32[]{:S(2)}) collective-permute-start(bf16[8,6144]{1,0:T(8,128)(2,1)S(1)} %get-tuple-element.23), channel_id=1, source_target_pairs={{0,12},{1,13},{2,14},{3,15},{4,8},{5,9},{6,10},{7,11},{8,4},{9,5},... | collective-permute-start | bytes 294920 | tf_op jit(solution)/shard_map/ppermute | solution.py:272
  9.4 8.6 %collective-permute-start.2 = (bf16[8,6144]{1,0:T(8,128)(2,1)S(1)}, bf16[8,6144]{1,0:T(8,128)(2,1)S(1)}, u32[]{:S(2)}, u32[]{:S(2)}) collective-permute-start(bf16[8,6144]{1,0:T(8,128)(2,1)S(1)} %get-tuple-element.23), channel_id=1, source_target_pairs={{0,8},{1,9},{2,10},{3,11},{4,12},{5,13},{6,14},{7,15},{8,0},{9,1},... | collective-permute-start | bytes 294920 | tf_op jit(solution)/shard_map/ppermute | solution.py:272
  9.4 8.6 %collective-permute-start.3 = (bf16[8,6144]{1,0:T(8,128)(2,1)S(1)}, bf16[8,6144]{1,0:T(8,128)(2,1)S(1)}, u32[]{:S(2)}, u32[]{:S(2)}) collective-permute-start(bf16[8,6144]{1,0:T(8,128)(2,1)S(1)} %get-tuple-element.23), channel_id=1, source_target_pairs={{0,4},{1,5},{2,6},{3,7},{4,0},{5,1},{6,2},{7,3},{8,12},{9,13},{10,... | collective-permute-start | bytes 294920 | tf_op jit(solution)/shard_map/ppermute | solution.py:272
  10.0 9.6 %collective-permute-start.4 = (bf16[8,8320]{1,0:T(8,128)(2,1)S(1)}, bf16[8,8320]{1,0:T(8,128)(2,1)S(1)}, u32[]{:S(2)}, u32[]{:S(2)}) collective-permute-start(bf16[8,8320]{1,0:T(8,128)(2,1)S(1)} %get-tuple-element.22), channel_id=1, source_target_pairs={{0,2},{1,3},{2,0},{3,1},{4,6},{5,7},{6,4},{7,5},{8,10},{9,11},{10,... | collective-permute-start | bytes 399368 | tf_op jit(solution)/shard_map/ppermute | solution.py:272
  18.0 10.3 %collective-permute-start.8 = (bf16[24,6144]{1,0:T(8,128)(2,1)S(1)}, bf16[24,6144]{1,0:T(8,128)(2,1)S(1)}, u32[]{:S(2)}, u32[]{:S(2)}) collective-permute-start(bf16[24,6144]{1,0:T(8,128)(2,1)S(1)} %constant_dynamic-update-slice_fusion), channel_id=1, source_target_pairs={{0,2},{1,3},{2,0},{3,1},{4,6},{5,7},{6,4},{7,5},{8,10},{9,11},{10,... | collective-permute-start | bytes 884744 | tf_op jit(solution)/shard_map/ppermute | solution.py:272
  19.6 7.5 %collective-permute-start.5 = (bf16[16,2176]{1,0:T(8,128)(2,1)S(1)}, bf16[16,2176]{1,0:T(8,128)(2,1)S(1)}, u32[]{:S(2)}, u32[]{:S(2)}) collective-permute-start(bf16[16,2176]{1,0:T(8,128)(2,1)S(1)} %pad_maximum_fusion.1), channel_id=1, source_target_pairs={{0,12},{1,13},{2,14},{3,15},{4,8},{5,9},{6,10},{7,11},{8,4},{9,5},... | collective-permute-start | bytes 208904 | tf_op jit(solution)/shard_map/ppermute | solution.py:272
  22.2 6.2 %collective-permute-start.6 = (bf16[16,2176]{1,0:T(8,128)(2,1)S(1)}, bf16[16,2176]{1,0:T(8,128)(2,1)S(1)}, u32[]{:S(2)}, u32[]{:S(2)}) collective-permute-start(bf16[16,2176]{1,0:T(8,128)(2,1)S(1)} %pad_maximum_fusion.1), channel_id=1, source_target_pairs={{0,8},{1,9},{2,10},{3,11},{4,12},{5,13},{6,14},{7,15},{8,0},{9,1},... | collective-permute-start | bytes 208904 | tf_op jit(solution)/shard_map/ppermute | solution.py:272
  22.2 6.2 %collective-permute-start.7 = (bf16[16,2176]{1,0:T(8,128)(2,1)S(1)}, bf16[16,2176]{1,0:T(8,128)(2,1)S(1)}, u32[]{:S(2)}, u32[]{:S(2)}) collective-permute-start(bf16[16,2176]{1,0:T(8,128)(2,1)S(1)} %pad_maximum_fusion.1), channel_id=1, source_target_pairs={{0,4},{1,5},{2,6},{3,7},{4,0},{5,1},{6,2},{7,3},{8,12},{9,13},{10,... | collective-permute-start | bytes 208904 | tf_op jit(solution)/shard_map/ppermute | solution.py:272
  24.1 4.6 %copy-start = (bf16[512,8192]{1,0:T(8,128)(2,1)S(1)}, bf16[512,8192]{1,0:T(8,128)(2,1)}, u32[]{:S(2)}) copy-start(bf16[512,8192]{1,0:T(8,128)(2,1)} %weight_ref.3) | copy-start | bytes 25165828
  29.6 1.3 %collective-permute-start.9 = (bf16[64,640]{1,0:T(8,128)(2,1)S(1)}, bf16[64,640]{1,0:T(8,128)(2,1)S(1)}, u32[]{:S(2)}, u32[]{:S(2)}) collective-permute-start(bf16[64,640]{1,0:T(8,128)(2,1)S(1)} %get-tuple-element.29), channel_id=1, source_target_pairs={{0,1},{1,0},{2,3},{3,2},{4,5},{5,4},{6,7},{7,6},{8,9},{9,8},{10,11... | collective-permute-start | bytes 245768 | tf_op jit(solution)/shard_map/ppermute | solution.py:272
  32.7 2.7 %collective-permute-start.10 = (bf16[64,8192]{1,0:T(8,128)(2,1)S(1)}, bf16[64,8192]{1,0:T(8,128)(2,1)S(1)}, u32[]{:S(2)}, u32[]{:S(2)}) collective-permute-start(bf16[64,8192]{1,0:T(8,128)(2,1)S(1)} %get-tuple-element.31), channel_id=1, source_target_pairs={{0,1},{1,0},{2,3},{3,2},{4,5},{5,4},{6,7},{7,6},{8,9},{9,8},{10,11... | collective-permute-start | bytes 3145736 | tf_op jit(solution)/shard_map/ppermute | solution.py:272
  35.8 9.1 %collective-permute-start.11 = (bf16[3,8,6144]{2,1,0:T(8,128)(2,1)S(1)}, bf16[3,8,6144]{2,1,0:T(8,128)(2,1)S(1)}, u32[]{:S(2)}, u32[]{:S(2)}) collective-permute-start(bf16[3,8,6144]{2,1,0:T(8,128)(2,1)S(1)} %slice_bitcast_fusion.1), channel_id=1, source_target_pairs={{0,2},{1,3},{2,0},{3,1},{4,6},{5,7},{6,4},{7,5},{8,10},{9,11},{10,... | collective-permute-start | bytes 884744 | tf_op jit(solution)/shard_map/ppermute | solution.py:272
  36.4 8.6 %collective-permute-start.15 = (bf16[2,8,2048]{2,1,0:T(8,128)(2,1)S(1)}, bf16[2,8,2048]{2,1,0:T(8,128)(2,1)S(1)}, u32[]{:S(2)}, u32[]{:S(2)}) collective-permute-start(bf16[2,8,2048]{2,1,0:T(8,128)(2,1)S(1)} %get-tuple-element.37), channel_id=1, source_target_pairs={{0,12},{1,13},{2,14},{3,15},{4,8},{5,9},{6,10},{7,11},{8,4},{9,5},... | collective-permute-start | bytes 196616 | tf_op jit(solution)/shard_map/ppermute | solution.py:272
  38.9 6.1 %collective-permute-start.16 = (bf16[2,8,2048]{2,1,0:T(8,128)(2,1)S(1)}, bf16[2,8,2048]{2,1,0:T(8,128)(2,1)S(1)}, u32[]{:S(2)}, u32[]{:S(2)}) collective-permute-start(bf16[2,8,2048]{2,1,0:T(8,128)(2,1)S(1)} %get-tuple-element.36), channel_id=1, source_target_pairs={{0,8},{1,9},{2,10},{3,11},{4,12},{5,13},{6,14},{7,15},{8,0},{9,1},... | collective-permute-start | bytes 196616 | tf_op jit(solution)/shard_map/ppermute | solution.py:272
  38.9 6.1 %collective-permute-start.17 = (bf16[2,8,2048]{2,1,0:T(8,128)(2,1)S(1)}, bf16[2,8,2048]{2,1,0:T(8,128)(2,1)S(1)}, u32[]{:S(2)}, u32[]{:S(2)}) collective-permute-start(bf16[2,8,2048]{2,1,0:T(8,128)(2,1)S(1)} %get-tuple-element.35), channel_id=1, source_target_pairs={{0,4},{1,5},{2,6},{3,7},{4,0},{5,1},{6,2},{7,3},{8,12},{9,13},{10,... | collective-permute-start | bytes 196616 | tf_op jit(solution)/shard_map/ppermute | solution.py:272
  45.1 7.6 %collective-permute-start.12 = (bf16[8,6144]{1,0:T(8,128)(2,1)S(1)}, bf16[8,6144]{1,0:T(8,128)(2,1)S(1)}, u32[]{:S(2)}, u32[]{:S(2)}) collective-permute-start(bf16[8,6144]{1,0:T(8,128)(2,1)S(1)} %get-tuple-element.38), channel_id=1, source_target_pairs={{0,12},{1,13},{2,14},{3,15},{4,8},{5,9},{6,10},{7,11},{8,4},{9,5},... | collective-permute-start | bytes 294920 | tf_op jit(solution)/shard_map/ppermute | solution.py:272
  47.6 8.4 %collective-permute-start.13 = (bf16[8,6144]{1,0:T(8,128)(2,1)S(1)}, bf16[8,6144]{1,0:T(8,128)(2,1)S(1)}, u32[]{:S(2)}, u32[]{:S(2)}) collective-permute-start(bf16[8,6144]{1,0:T(8,128)(2,1)S(1)} %get-tuple-element.40), channel_id=1, source_target_pairs={{0,8},{1,9},{2,10},{3,11},{4,12},{5,13},{6,14},{7,15},{8,0},{9,1},... | collective-permute-start | bytes 294920 | tf_op jit(solution)/shard_map/ppermute | solution.py:272
  47.6 8.4 %collective-permute-start.14 = (bf16[8,6144]{1,0:T(8,128)(2,1)S(1)}, bf16[8,6144]{1,0:T(8,128)(2,1)S(1)}, u32[]{:S(2)}, u32[]{:S(2)}) collective-permute-start(bf16[8,6144]{1,0:T(8,128)(2,1)S(1)} %get-tuple-element.39), channel_id=1, source_target_pairs={{0,4},{1,5},{2,6},{3,7},{4,0},{5,1},{6,2},{7,3},{8,12},{9,13},{10,... | collective-permute-start | bytes 294920 | tf_op jit(solution)/shard_map/ppermute | solution.py:272
  49.6 6.6 %collective-permute-start.18 = (bf16[8,8192]{1,0:T(8,128)(2,1)S(1)}, bf16[8,8192]{1,0:T(8,128)(2,1)S(1)}, u32[]{:S(2)}, u32[]{:S(2)}) collective-permute-start(bf16[8,8192]{1,0:T(8,128)(2,1)S(1)} %pad_maximum_fusion), channel_id=1, source_target_pairs={{0,2},{1,3},{2,0},{3,1},{4,6},{5,7},{6,4},{7,5},{8,10},{9,11},{10,... | collective-permute-start | bytes 393224 | tf_op jit(solution)/shard_map/ppermute | solution.py:272

commit v6 on v5

--- a/solution.py
+++ b/solution.py
@@ -17,7 +17,7 @@
 ADAPTER_GAIN = 2.0
 MASKED_SCORE = -1e30
 
-GATHER_CUT = 6144
+GATHER_CUT = 5888
 SCATTER_CUT = 6144
 
 NT = (((1,), (1,)), ((), ()))
@@ -229,26 +229,27 @@
     )(device, rows, held_in_vmem(factors), held_in_vmem(weight))
 
 
-def project_kernel(tile, x_ref, x_other_ref, weight_ref, up_ref, own_ref, other_ref):
+def project_kernel(first, tile, x_ref, x_other_ref, weight_ref, up_ref, own_ref, other_ref):
     half, columns = own_ref.shape
     held, rank, _ = up_ref.shape
     head = weight_ref.shape[0]
     x = jnp.concatenate([x_other_ref[...], x_ref[...]], axis=0)
     for start in range(0, columns, tile):
-        at = slice(start, start + tile)
-        out = jnp.dot(x[:, :head], weight_ref[:, at], preferred_element_type=jnp.float32)
+        at = slice(start, min(start + tile, columns))
+        there = slice(first + at.start, first + at.stop)
+        out = jnp.dot(x[:, :head], weight_ref[:, there], preferred_element_type=jnp.float32)
         out += jnp.dot(
-            x[:, head:], up_ref[:, :, at].reshape(held * rank, tile),
+            x[:, head:], up_ref[:, :, there].reshape(held * rank, -1),
             preferred_element_type=jnp.float32,
         )
         other_ref[:, at] = out[:half].astype(jnp.bfloat16)
         own_ref[:, at] = out[half:]
 
 
-def project(x, x_other, weight, up):
-    half, columns = x.shape[0], weight.shape[1]
+def project(x, x_other, weight, up, first, columns):
+    half = x.shape[0]
     return pl.pallas_call(
-        functools.partial(project_kernel, 512),
+        functools.partial(project_kernel, first, 512),
         out_shape=(
             jax.ShapeDtypeStruct((half, columns), jnp.float32),
             jax.ShapeDtypeStruct((half, columns), jnp.bfloat16),
@@ -301,9 +302,15 @@
     x, x_send = shrink(device, rows, factors, adapter_up, out_weight)
     x_other = swap(x_send, 1)
 
-    mine, send = project(x, x_other, out_weight, adapter_up)
-    sums = (mine + swap(send, 1).astype(f32)).reshape(2, depths, requests, WIDTH)
-    a_sum, b_sum = sums[..., :SCATTER_CUT], sums[..., SCATTER_CUT:]
+    def sums(mine, came):
+        return (mine + came.astype(f32)).reshape(2, depths, requests, -1)
+
+    mine, send = project(x, x_other, out_weight, adapter_up, 0, SCATTER_CUT)
+    came = swap(send, 1)
+    a_sum = sums(mine, came)
+    x, came = lax.optimization_barrier((x, came))
+    mine, send = project(x, x_other, out_weight, adapter_up, SCATTER_CUT, WIDTH - SCATTER_CUT)
+    b_sum = sums(mine, swap(send, 1))
     a_part = a_sum[0, 1:] + swap(a_sum[1, 1:].astype(bf16), 2).astype(f32)
     b_send = b_sum.astype(bf16)
     a_send = a_part.astype(bf16)

time: 57 us -> 56.5 us (level)
  starting transfers between devices: 25 us -> 24.3 us
    ppermute x19 -> x20, starting transfers between devices: 25 us -> 24.3 us  [swap(): return lax.ppermute(x, 'rep', [(i, i ^ mask) for i in range(members)])]
    pallas_call x1 -> x2, Pallas kernels: 1.8 us -> 2 us  [project(): pl.pallas_call(functools.partial(project_kernel, first, 512), out_shape=(...]
    ppermute x19 -> x20, waiting for transfers between devices: 21.1 us -> 21.2 us  [swap(): return lax.ppermute(x, 'rep', [(i, i ^ mask) for i in range(members)])]
  transfers between devices with their start and end apart: 19 -> 20, of which waited for: 9 -> 10; matrix products, arithmetic and copies ran while one was open for 0% -> 1% of each run, Pallas kernels for 11% -> 11%
where the time goes in v6:
time: 56.5 us; the launch traced here: 56.4 us
  starting transfers between devices  24.3 us (43%)
  waiting for transfers between devices  21.2 us (38%)
  Pallas kernels  9.17 us (16%)
  other arithmetic  1.27 us (2%)
    ppermute x20, starting transfers between devices, swap(): return lax.ppermute(x, 'rep', [(i, i ^ mask) for i in range(members)])  24.3 us
    ppermute x20, waiting for transfers between devices, swap(): return lax.ppermute(x, 'rep', [(i, i ^ mask) for i in range(members)])  21.2 us
    pallas_call x1, Pallas kernels, attend(): pl.pallas_call(attend_kernel, out_shape=(pltpu.VMEM((requests, GATHER_CUT...  3.34 us
    pallas_call x1, Pallas kernels, stage(): pl.pallas_call(stage_kernel, out_shape=pltpu.VMEM((WIDTH, 2 * ranks), jnp...  2.98 us
    pallas_call x2, Pallas kernels, project(): pl.pallas_call(functools.partial(project_kernel, first, 512), out_shape=(...  2 us
  transfers between devices with their start and end apart: 20, of which 10 were waited for; matrix products, arithmetic and copies ran while one was open for 1% of the time, Pallas kernels for 11%

profile of v6, /device:TPU:0, one launch (start us, length us, event | category | flops | bytes accessed | tf_op | source)
XLA Modules:
  0.0 56.4 jit_solution(7552894149258414957)
XLA Ops:
  0.0 0.0 copy-start.1
  0.0 0.5 collective-permute-start
  0.5 3.3 %attend.1 = (bf16[8,5888]{1,0:T(8,128)(2,1)S(1)}, bf16[8,8320]{1,0:T(8,128)(2,1)S(1)}) custom-call(s32[8]{0:T(128)} %length_hbm.1, s32[8]{0:T(128)} %adapter_hbm.1, s32[32]{0:T(128)} %slot_hbm.1, bf16[8,8192]{1,0:T(8,128)(2,1)} %query_hbm.1, bf16[8,2,1024]{2,1,0:T(2,128)(2,1)} %pair_hbm.1, bf16[8,2,128,1024]{3,2,1,0:T(8,128)(2,1)} %cache_hbm.1), custom_call_target="tpu_custom_call" | custom-call | flops 1000000000 | bytes 4194304 | tf_op jit(solution)/shard_map/attend/pallas_call | solution.py:144
  3.8 0.6 %collective-permute-done = bf16[2,64,8192]{2,1,0:T(8,128)(2,1)S(1)} collective-permute-done((bf16[2,64,8192]{2,1,0:T(8,128)(2,1)}, bf16[2,64,8192]{2,1,0:T(8,128)(2,1)S(1)}, u32[]{:S(2)}, u32[]{:S(2)}) %collective-permute-start) | collective-permute-done | bytes 2097184 | tf_op jit(solution)/shard_map/ppermute | solution.py:273
  4.5 0.0 copy-start.2
  4.5 5.0 %collective-permute-start.1 = (bf16[8,5888]{1,0:T(8,128)(2,1)S(1)}, bf16[8,5888]{1,0:T(8,128)(2,1)S(1)}, u32[]{:S(2)}, u32[]{:S(2)}) collective-permute-start(bf16[8,5888]{1,0:T(8,128)(2,1)S(1)} %get-tuple-element.26), channel_id=1, source_target_pairs={{0,12},{1,13},{2,14},{3,15},{4,8},{5,9},{6,10},{7,11},{8,4},{9,5},... | collective-permute-start | bytes 282632 | tf_op jit(solution)/shard_map/ppermute | solution.py:273
  9.4 0.0 collective-permute-start.2
  9.4 0.6 %collective-permute-start.3 = (bf16[8,5888]{1,0:T(8,128)(2,1)S(1)}, bf16[8,5888]{1,0:T(8,128)(2,1)S(1)}, u32[]{:S(2)}, u32[]{:S(2)}) collective-permute-start(bf16[8,5888]{1,0:T(8,128)(2,1)S(1)} %get-tuple-element.26), channel_id=1, source_target_pairs={{0,4},{1,5},{2,6},{3,7},{4,0},{5,1},{6,2},{7,3},{8,12},{9,13},{10,... | collective-permute-start | bytes 282632 | tf_op jit(solution)/shard_map/ppermute | solution.py:273
  10.0 1.7 %collective-permute-start.4 = (bf16[8,8320]{1,0:T(8,128)(2,1)S(1)}, bf16[8,8320]{1,0:T(8,128)(2,1)S(1)}, u32[]{:S(2)}, u32[]{:S(2)}) collective-permute-start(bf16[8,8320]{1,0:T(8,128)(2,1)S(1)} %get-tuple-element.25), channel_id=1, source_target_pairs={{0,2},{1,3},{2,0},{3,1},{4,6},{5,7},{6,4},{7,5},{8,10},{9,11},{10,... | collective-permute-start | bytes 399368 | tf_op jit(solution)/shard_map/ppermute | solution.py:273
  11.7 1.3 %collective-permute-done.1 = bf16[8,5888]{1,0:T(8,128)(2,1)S(1)} collective-permute-done((bf16[8,5888]{1,0:T(8,128)(2,1)S(1)}, bf16[8,5888]{1,0:T(8,128)(2,1)S(1)}, u32[]{:S(2)}, u32[]{:S(2)}) %collective-permute-start.1) | collective-permute-done | bytes 94240 | tf_op jit(solution)/shard_map/ppermute | solution.py:273
  13.0 4.6 %collective-permute-done.2 = bf16[8,5888]{1,0:T(8,128)(2,1)S(1)} collective-permute-done((bf16[8,5888]{1,0:T(8,128)(2,1)S(1)}, bf16[8,5888]{1,0:T(8,128)(2,1)S(1)}, u32[]{:S(2)}, u32[]{:S(2)}) %collective-permute-start.2) | collective-permute-done | bytes 94240 | tf_op jit(solution)/shard_map/ppermute | solution.py:273
  17.7 0.0 collective-permute-done.3
  17.7 1.6 %collective-permute-start.8 = (bf16[24,5888]{1,0:T(8,128)(2,1)S(1)}, bf16[24,5888]{1,0:T(8,128)(2,1)S(1)}, u32[]{:S(2)}, u32[]{:S(2)}) collective-permute-start(bf16[24,5888]{1,0:T(8,128)(2,1)S(1)} %constant_dynamic-update-slice_fusion), channel_id=1, source_target_pairs={{0,2},{1,3},{2,0},{3,1},{4,6},{5,7},{6,4},{7,5},{8,10},{9,11},{10,... | collective-permute-start | bytes 847880 | tf_op jit(solution)/shard_map/ppermute | solution.py:273
  19.3 0.0 collective-permute-done.4
  19.3 0.0 copy-done.2
  19.3 2.5 %collective-permute-start.5 = (bf16[16,2432]{1,0:T(8,128)(2,1)S(1)}, bf16[16,2432]{1,0:T(8,128)(2,1)S(1)}, u32[]{:S(2)}, u32[]{:S(2)}) collective-permute-start(bf16[16,2432]{1,0:T(8,128)(2,1)S(1)} %pad_maximum_fusion.1), channel_id=1, source_target_pairs={{0,12},{1,13},{2,14},{3,15},{4,8},{5,9},{6,10},{7,11},{8,4},{9,5},... | collective-permute-start | bytes 233480 | tf_op jit(solution)/shard_map/ppermute | solution.py:273
  21.8 0.0 collective-permute-start.6
  21.8 1.9 %collective-permute-start.7 = (bf16[16,2432]{1,0:T(8,128)(2,1)S(1)}, bf16[16,2432]{1,0:T(8,128)(2,1)S(1)}, u32[]{:S(2)}, u32[]{:S(2)}) collective-permute-start(bf16[16,2432]{1,0:T(8,128)(2,1)S(1)} %pad_maximum_fusion.1), channel_id=1, source_target_pairs={{0,4},{1,5},{2,6},{3,7},{4,0},{5,1},{6,2},{7,3},{8,12},{9,13},{10,... | collective-permute-start | bytes 233480 | tf_op jit(solution)/shard_map/ppermute | solution.py:273
  23.7 0.0 copy-done.1
  23.8 0.0 copy-start
  23.8 3.0 %stage.1.factors_ref = bf16[8192,256]{1,0:T(8,128)(2,1)S(1)} custom-call(bf16[128,8192]{1,0:T(8,128)(2,1)} %bitcast.68, bf16[128,8192]{1,0:T(8,128)(2,1)} %bitcast.69, bf16[2,64,8192]{2,1,0:T(8,128)(2,1)S(1)} %copy-done.1), custom_call_target="tpu_custom_call" | custom-call | flops 100000000 | bytes 8388608 | tf_op jit(solution)/shard_map/stage/pallas_call | solution.py:185
  26.7 0.0 collective-permute-done.5
  26.8 1.9 %collective-permute-done.6 = bf16[16,2432]{1,0:T(8,128)(2,1)S(1)} collective-permute-done((bf16[16,2432]{1,0:T(8,128)(2,1)S(1)}, bf16[16,2432]{1,0:T(8,128)(2,1)S(1)}, u32[]{:S(2)}, u32[]{:S(2)}) %collective-permute-start.6) | collective-permute-done | bytes 77856 | tf_op jit(solution)/shard_map/ppermute | solution.py:273
  28.6 0.0 collective-permute-done.7
  28.6 0.0 collective-permute-done.8
  28.7 0.1 maximum_maximum_fusion.rows_ref
  28.8 0.0 copy-done
  28.8 0.8 %shrink.1 = (bf16[64,640]{1,0:T(8,128)(2,1)S(1)}, bf16[64,640]{1,0:T(8,128)(2,1)S(1)}) custom-call(s32[1]{0:T(128)} %bitcast.device_ref, bf16[64,8320]{1,0:T(8,128)(2,1)S(1)} %maximum_maximum_fusion.rows_ref, bf16[8192,256]{1,0:T(8,128)(2,1)S(1)} %stage.1.factors_ref, bf16[512,8192]{1,0:T(8,128)(2,1)S(1)} %copy-done), custom_call_target="tpu_custom_call" | custom-call | flops 268435456 | bytes 4194304 | tf_op jit(solution)/shard_map/shrink/pallas_call | solution.py:221
  29.6 0.1 collective-permute-start.9
  29.7 1.3 %collective-permute-done.9.x_other_ref = bf16[64,640]{1,0:T(8,128)(2,1)S(1)} collective-permute-done((bf16[64,640]{1,0:T(8,128)(2,1)S(1)}, bf16[64,640]{1,0:T(8,128)(2,1)S(1)}, u32[]{:S(2)}, u32[]{:S(2)}) %collective-permute-start.9) | collective-permute-done | bytes 81952 | tf_op jit(solution)/shard_map/ppermute | solution.py:273
  31.0 1.4 %project.2 = (f32[64,6144]{1,0:T(8,128)S(1)}, bf16[64,6144]{1,0:T(8,128)(2,1)S(1)}) custom-call(bf16[64,640]{1,0:T(8,128)(2,1)S(1)} %get-tuple-element.35.x_ref, bf16[64,640]{1,0:T(8,128)(2,1)S(1)} %collective-permute-done.9.x_other_ref, bf16[512,8192]{1,0:T(8,128)(2,1)S(1)} %copy-done, bf16[2,64,8192]{2,1,0:T(8,128)(2,1)S(1)} %copy-done.1), custom_call_target="tpu_custom_call" | custom-call | flops 1006632960 | bytes 7864320 | tf_op jit(solution)/shard_map/project/pallas_call | solution.py:251
  32.4 0.2 collective-permute-start.10
  32.6 2.1 %collective-permute-done.10 = bf16[64,6144]{1,0:T(8,128)(2,1)S(1)} collective-permute-done((bf16[64,6144]{1,0:T(8,128)(2,1)S(1)}, bf16[64,6144]{1,0:T(8,128)(2,1)S(1)}, u32[]{:S(2)}, u32[]{:S(2)}) %collective-permute-start.10) | collective-permute-done | bytes 786464 | tf_op jit(solution)/shard_map/ppermute | solution.py:273
  34.8 0.2 convert_add_fusion
  34.9 0.1 convert.11
  35.1 0.6 %project.3 = (f32[64,2048]{1,0:T(8,128)S(1)}, bf16[64,2048]{1,0:T(8,128)(2,1)S(1)}) custom-call(bf16[64,640]{1,0:T(8,128)(2,1)S(1)} %get-tuple-element.35.x_ref, bf16[64,640]{1,0:T(8,128)(2,1)S(1)} %collective-permute-done.9.x_other_ref, bf16[512,8192]{1,0:T(8,128)(2,1)S(1)} %copy-done, bf16[2,64,8192]{2,1,0:T(8,128)(2,1)S(1)} %copy-done.1), custom_call_target="tpu_custom_call" | custom-call | flops 335544320 | bytes 2621440 | tf_op jit(solution)/shard_map/project/pallas_call | solution.py:251
  35.6 0.2 collective-permute-start.15
  35.9 0.6 %collective-permute-start.11 = (bf16[3,8,6144]{2,1,0:T(8,128)(2,1)S(1)}, bf16[3,8,6144]{2,1,0:T(8,128)(2,1)S(1)}, u32[]{:S(2)}, u32[]{:S(2)}) collective-permute-start(bf16[3,8,6144]{2,1,0:T(8,128)(2,1)S(1)} %slice_bitcast_fusion.1), channel_id=1, source_target_pairs={{0,2},{1,3},{2,0},{3,1},{4,6},{5,7},{6,4},{7,5},{8,10},{9,11},{10,... | collective-permute-start | bytes 884744 | tf_op jit(solution)/shard_map/ppermute | solution.py:273
  36.4 0.8 %collective-permute-done.15 = bf16[64,2048]{1,0:T(8,128)(2,1)S(1)} collective-permute-done((bf16[64,2048]{1,0:T(8,128)(2,1)S(1)}, bf16[64,2048]{1,0:T(8,128)(2,1)S(1)}, u32[]{:S(2)}, u32[]{:S(2)}) %collective-permute-start.15) | collective-permute-done | bytes 262176 | tf_op jit(solution)/shard_map/ppermute | solution.py:273
  37.3 2.2 %collective-permute-start.16 = (bf16[2,8,2048]{2,1,0:T(8,128)(2,1)S(1)}, bf16[2,8,2048]{2,1,0:T(8,128)(2,1)S(1)}, u32[]{:S(2)}, u32[]{:S(2)}) collective-permute-start(bf16[2,8,2048]{2,1,0:T(8,128)(2,1)S(1)} %get-tuple-element.46), channel_id=1, source_target_pairs={{0,12},{1,13},{2,14},{3,15},{4,8},{5,9},{6,10},{7,11},{8,4},{9,5},... | collective-permute-start | bytes 196616 | tf_op jit(solution)/shard_map/ppermute | solution.py:273
  39.5 0.0 collective-permute-start.17
  39.5 2.3 %collective-permute-start.18 = (bf16[2,8,2048]{2,1,0:T(8,128)(2,1)S(1)}, bf16[2,8,2048]{2,1,0:T(8,128)(2,1)S(1)}, u32[]{:S(2)}, u32[]{:S(2)}) collective-permute-start(bf16[2,8,2048]{2,1,0:T(8,128)(2,1)S(1)} %get-tuple-element.44), channel_id=1, source_target_pairs={{0,4},{1,5},{2,6},{3,7},{4,0},{5,1},{6,2},{7,3},{8,12},{9,13},{10,... | collective-permute-start | bytes 196616 | tf_op jit(solution)/shard_map/ppermute | solution.py:273
  41.8 3.4 %collective-permute-done.11 = bf16[3,8,6144]{2,1,0:T(8,128)(2,1)S(1)} collective-permute-done((bf16[3,8,6144]{2,1,0:T(8,128)(2,1)S(1)}, bf16[3,8,6144]{2,1,0:T(8,128)(2,1)S(1)}, u32[]{:S(2)}, u32[]{:S(2)}) %collective-permute-start.11) | collective-permute-done | bytes 294944 | tf_op jit(solution)/shard_map/ppermute | solution.py:273
  45.2 0.1 fusion.1
  45.3 2.2 %collective-permute-start.12 = (bf16[8,6144]{1,0:T(8,128)(2,1)S(1)}, bf16[8,6144]{1,0:T(8,128)(2,1)S(1)}, u32[]{:S(2)}, u32[]{:S(2)}) collective-permute-start(bf16[8,6144]{1,0:T(8,128)(2,1)S(1)} %get-tuple-element.41), channel_id=1, source_target_pairs={{0,12},{1,13},{2,14},{3,15},{4,8},{5,9},{6,10},{7,11},{8,4},{9,5},... | collective-permute-start | bytes 294920 | tf_op jit(solution)/shard_map/ppermute | solution.py:273
  47.5 0.0 collective-permute-start.13
  47.5 0.0 collective-permute-done.16
  47.5 2.3 %collective-permute-start.14 = (bf16[8,6144]{1,0:T(8,128)(2,1)S(1)}, bf16[8,6144]{1,0:T(8,128)(2,1)S(1)}, u32[]{:S(2)}, u32[]{:S(2)}) collective-permute-start(bf16[8,6144]{1,0:T(8,128)(2,1)S(1)} %get-tuple-element.42), channel_id=1, source_target_pairs={{0,4},{1,5},{2,6},{3,7},{4,0},{5,1},{6,2},{7,3},{8,12},{9,13},{10,... | collective-permute-start | bytes 294920 | tf_op jit(solution)/shard_map/ppermute | solution.py:273
  49.8 0.0 collective-permute-done.17
  49.8 0.0 collective-permute-done.18
  49.9 0.6 %collective-permute-start.19 = (bf16[8,8192]{1,0:T(8,128)(2,1)S(1)}, bf16[8,8192]{1,0:T(8,128)(2,1)S(1)}, u32[]{:S(2)}, u32[]{:S(2)}) collective-permute-start(bf16[8,8192]{1,0:T(8,128)(2,1)S(1)} %pad_maximum_fusion), channel_id=1, source_target_pairs={{0,2},{1,3},{2,0},{3,1},{4,6},{5,7},{6,4},{7,5},{8,10},{9,11},{10,... | collective-permute-start | bytes 393224 | tf_op jit(solution)/shard_map/ppermute | solution.py:273
  50.4 2.5 %collective-permute-done.12 = bf16[8,6144]{1,0:T(8,128)(2,1)S(1)} collective-permute-done((bf16[8,6144]{1,0:T(8,128)(2,1)S(1)}, bf16[8,6144]{1,0:T(8,128)(2,1)S(1)}, u32[]{:S(2)}, u32[]{:S(2)}) %collective-permute-start.12) | collective-permute-done | bytes 98336 | tf_op jit(solution)/shard_map/ppermute | solution.py:273
  53.0 2.6 %collective-permute-done.13 = bf16[8,6144]{1,0:T(8,128)(2,1)S(1)} collective-permute-done((bf16[8,6144]{1,0:T(8,128)(2,1)S(1)}, bf16[8,6144]{1,0:T(8,128)(2,1)S(1)}, u32[]{:S(2)}, u32[]{:S(2)}) %collective-permute-start.13) | collective-permute-done | bytes 98336 | tf_op jit(solution)/shard_map/ppermute | solution.py:273
  55.6 0.0 collective-permute-done.14
  55.7 0.0 collective-permute-done.19
  55.7 0.7 %fusion.2 = bf16[8,8192]{1,0:T(8,128)(2,1)} fusion(f32[8,2048]{1,0:T(8,128)S(1)} %slice_bitcast_fusion.10, f32[8,6144]{1,0:T(8,128)S(1)} %fusion.5, bf16[8,8192]{1,0:T(8,128)(2,1)S(1)} %collective-permute-done.19), kind=kLoop, calls=%fused_computation.8 | loop fusion | flops 262144 | bytes 524288 | tf_op jit(solution)/shard_map/convert_element_type | solution.py:326
  (18 shorter events, 0.3 us)
Async XLA Ops:
  0.0 23.7 %copy-start.1 = (bf16[2,64,8192]{2,1,0:T(8,128)(2,1)S(1)}, bf16[2,64,8192]{2,1,0:T(8,128)(2,1)}, u32[]{:S(2)}) copy-start(bf16[2,64,8192]{2,1,0:T(8,128)(2,1)} %up_ref.5) | copy-start | bytes 6291460
  0.0 4.5 %collective-permute-start = (bf16[2,64,8192]{2,1,0:T(8,128)(2,1)}, bf16[2,64,8192]{2,1,0:T(8,128)(2,1)S(1)}, u32[]{:S(2)}, u32[]{:S(2)}) collective-permute-start(bf16[2,64,8192]{2,1,0:T(8,128)(2,1)} %bitcast.67), channel_id=1, source_target_pairs={{0,1},{1,0},{2,3},{3,2},{4,5},{5,4},{6,7},{7,6},{8,9},{9,8},{10,11... | collective-permute-start | bytes 6291464 | tf_op jit(solution)/shard_map/ppermute | solution.py:273
  4.5 14.8 %copy-start.2 = (bf16[2,64,8192]{2,1,0:T(8,128)(2,1)}, bf16[2,64,8192]{2,1,0:T(8,128)(2,1)S(1)}, u32[]{:S(2)}) copy-start(bf16[2,64,8192]{2,1,0:T(8,128)(2,1)S(1)} %collective-permute-done) | copy-start | bytes 6291460
  4.5 8.6 %collective-permute-start.1 = (bf16[8,5888]{1,0:T(8,128)(2,1)S(1)}, bf16[8,5888]{1,0:T(8,128)(2,1)S(1)}, u32[]{:S(2)}, u32[]{:S(2)}) collective-permute-start(bf16[8,5888]{1,0:T(8,128)(2,1)S(1)} %get-tuple-element.26), channel_id=1, source_target_pairs={{0,12},{1,13},{2,14},{3,15},{4,8},{5,9},{6,10},{7,11},{8,4},{9,5},... | collective-permute-start | bytes 282632 | tf_op jit(solution)/shard_map/ppermute | solution.py:273
  9.4 8.2 %collective-permute-start.2 = (bf16[8,5888]{1,0:T(8,128)(2,1)S(1)}, bf16[8,5888]{1,0:T(8,128)(2,1)S(1)}, u32[]{:S(2)}, u32[]{:S(2)}) collective-permute-start(bf16[8,5888]{1,0:T(8,128)(2,1)S(1)} %get-tuple-element.26), channel_id=1, source_target_pairs={{0,8},{1,9},{2,10},{3,11},{4,12},{5,13},{6,14},{7,15},{8,0},{9,1},... | collective-permute-start | bytes 282632 | tf_op jit(solution)/shard_map/ppermute | solution.py:273
  9.4 8.2 %collective-permute-start.3 = (bf16[8,5888]{1,0:T(8,128)(2,1)S(1)}, bf16[8,5888]{1,0:T(8,128)(2,1)S(1)}, u32[]{:S(2)}, u32[]{:S(2)}) collective-permute-start(bf16[8,5888]{1,0:T(8,128)(2,1)S(1)} %get-tuple-element.26), channel_id=1, source_target_pairs={{0,4},{1,5},{2,6},{3,7},{4,0},{5,1},{6,2},{7,3},{8,12},{9,13},{10,... | collective-permute-start | bytes 282632 | tf_op jit(solution)/shard_map/ppermute | solution.py:273
  10.0 9.3 %collective-permute-start.4 = (bf16[8,8320]{1,0:T(8,128)(2,1)S(1)}, bf16[8,8320]{1,0:T(8,128)(2,1)S(1)}, u32[]{:S(2)}, u32[]{:S(2)}) collective-permute-start(bf16[8,8320]{1,0:T(8,128)(2,1)S(1)} %get-tuple-element.25), channel_id=1, source_target_pairs={{0,2},{1,3},{2,0},{3,1},{4,6},{5,7},{6,4},{7,5},{8,10},{9,11},{10,... | collective-permute-start | bytes 399368 | tf_op jit(solution)/shard_map/ppermute | solution.py:273
  17.7 10.9 %collective-permute-start.8 = (bf16[24,5888]{1,0:T(8,128)(2,1)S(1)}, bf16[24,5888]{1,0:T(8,128)(2,1)S(1)}, u32[]{:S(2)}, u32[]{:S(2)}) collective-permute-start(bf16[24,5888]{1,0:T(8,128)(2,1)S(1)} %constant_dynamic-update-slice_fusion), channel_id=1, source_target_pairs={{0,2},{1,3},{2,0},{3,1},{4,6},{5,7},{6,4},{7,5},{8,10},{9,11},{10,... | collective-permute-start | bytes 847880 | tf_op jit(solution)/shard_map/ppermute | solution.py:273
  19.3 7.5 %collective-permute-start.5 = (bf16[16,2432]{1,0:T(8,128)(2,1)S(1)}, bf16[16,2432]{1,0:T(8,128)(2,1)S(1)}, u32[]{:S(2)}, u32[]{:S(2)}) collective-permute-start(bf16[16,2432]{1,0:T(8,128)(2,1)S(1)} %pad_maximum_fusion.1), channel_id=1, source_target_pairs={{0,12},{1,13},{2,14},{3,15},{4,8},{5,9},{6,10},{7,11},{8,4},{9,5},... | collective-permute-start | bytes 233480 | tf_op jit(solution)/shard_map/ppermute | solution.py:273
  21.8 6.8 %collective-permute-start.6 = (bf16[16,2432]{1,0:T(8,128)(2,1)S(1)}, bf16[16,2432]{1,0:T(8,128)(2,1)S(1)}, u32[]{:S(2)}, u32[]{:S(2)}) collective-permute-start(bf16[16,2432]{1,0:T(8,128)(2,1)S(1)} %pad_maximum_fusion.1), channel_id=1, source_target_pairs={{0,8},{1,9},{2,10},{3,11},{4,12},{5,13},{6,14},{7,15},{8,0},{9,1},... | collective-permute-start | bytes 233480 | tf_op jit(solution)/shard_map/ppermute | solution.py:273
  21.8 6.8 %collective-permute-start.7 = (bf16[16,2432]{1,0:T(8,128)(2,1)S(1)}, bf16[16,2432]{1,0:T(8,128)(2,1)S(1)}, u32[]{:S(2)}, u32[]{:S(2)}) collective-permute-start(bf16[16,2432]{1,0:T(8,128)(2,1)S(1)} %pad_maximum_fusion.1), channel_id=1, source_target_pairs={{0,4},{1,5},{2,6},{3,7},{4,0},{5,1},{6,2},{7,3},{8,12},{9,13},{10,... | collective-permute-start | bytes 233480 | tf_op jit(solution)/shard_map/ppermute | solution.py:273
  23.8 5.0 %copy-start = (bf16[512,8192]{1,0:T(8,128)(2,1)S(1)}, bf16[512,8192]{1,0:T(8,128)(2,1)}, u32[]{:S(2)}) copy-start(bf16[512,8192]{1,0:T(8,128)(2,1)} %weight_ref.5) | copy-start | bytes 25165828
  29.6 1.3 %collective-permute-start.9 = (bf16[64,640]{1,0:T(8,128)(2,1)S(1)}, bf16[64,640]{1,0:T(8,128)(2,1)S(1)}, u32[]{:S(2)}, u32[]{:S(2)}) collective-permute-start(bf16[64,640]{1,0:T(8,128)(2,1)S(1)} %get-tuple-element.32), channel_id=1, source_target_pairs={{0,1},{1,0},{2,3},{3,2},{4,5},{5,4},{6,7},{7,6},{8,9},{9,8},{10,11... | collective-permute-start | bytes 245768 | tf_op jit(solution)/shard_map/ppermute | solution.py:273
  32.4 2.4 %collective-permute-start.10 = (bf16[64,6144]{1,0:T(8,128)(2,1)S(1)}, bf16[64,6144]{1,0:T(8,128)(2,1)S(1)}, u32[]{:S(2)}, u32[]{:S(2)}) collective-permute-start(bf16[64,6144]{1,0:T(8,128)(2,1)S(1)} %get-tuple-element.34), channel_id=1, source_target_pairs={{0,1},{1,0},{2,3},{3,2},{4,5},{5,4},{6,7},{7,6},{8,9},{9,8},{10,11... | collective-permute-start | bytes 2359304 | tf_op jit(solution)/shard_map/ppermute | solution.py:273
  35.6 1.6 %collective-permute-start.15 = (bf16[64,2048]{1,0:T(8,128)(2,1)S(1)}, bf16[64,2048]{1,0:T(8,128)(2,1)S(1)}, u32[]{:S(2)}, u32[]{:S(2)}) collective-permute-start(bf16[64,2048]{1,0:T(8,128)(2,1)S(1)} %get-tuple-element.37), channel_id=1, source_target_pairs={{0,1},{1,0},{2,3},{3,2},{4,5},{5,4},{6,7},{7,6},{8,9},{9,8},{10,11... | collective-permute-start | bytes 786440 | tf_op jit(solution)/shard_map/ppermute | solution.py:273
  35.9 9.3 %collective-permute-start.11 = (bf16[3,8,6144]{2,1,0:T(8,128)(2,1)S(1)}, bf16[3,8,6144]{2,1,0:T(8,128)(2,1)S(1)}, u32[]{:S(2)}, u32[]{:S(2)}) collective-permute-start(bf16[3,8,6144]{2,1,0:T(8,128)(2,1)S(1)} %slice_bitcast_fusion.1), channel_id=1, source_target_pairs={{0,2},{1,3},{2,0},{3,1},{4,6},{5,7},{6,4},{7,5},{8,10},{9,11},{10,... | collective-permute-start | bytes 884744 | tf_op jit(solution)/shard_map/ppermute | solution.py:273
  37.3 10.1 %collective-permute-start.16 = (bf16[2,8,2048]{2,1,0:T(8,128)(2,1)S(1)}, bf16[2,8,2048]{2,1,0:T(8,128)(2,1)S(1)}, u32[]{:S(2)}, u32[]{:S(2)}) collective-permute-start(bf16[2,8,2048]{2,1,0:T(8,128)(2,1)S(1)} %get-tuple-element.46), channel_id=1, source_target_pairs={{0,12},{1,13},{2,14},{3,15},{4,8},{5,9},{6,10},{7,11},{8,4},{9,5},... | collective-permute-start | bytes 196616 | tf_op jit(solution)/shard_map/ppermute | solution.py:273
  39.5 10.3 %collective-permute-start.17 = (bf16[2,8,2048]{2,1,0:T(8,128)(2,1)S(1)}, bf16[2,8,2048]{2,1,0:T(8,128)(2,1)S(1)}, u32[]{:S(2)}, u32[]{:S(2)}) collective-permute-start(bf16[2,8,2048]{2,1,0:T(8,128)(2,1)S(1)} %get-tuple-element.45), channel_id=1, source_target_pairs={{0,8},{1,9},{2,10},{3,11},{4,12},{5,13},{6,14},{7,15},{8,0},{9,1},... | collective-permute-start | bytes 196616 | tf_op jit(solution)/shard_map/ppermute | solution.py:273
  39.5 10.3 %collective-permute-start.18 = (bf16[2,8,2048]{2,1,0:T(8,128)(2,1)S(1)}, bf16[2,8,2048]{2,1,0:T(8,128)(2,1)S(1)}, u32[]{:S(2)}, u32[]{:S(2)}) collective-permute-start(bf16[2,8,2048]{2,1,0:T(8,128)(2,1)S(1)} %get-tuple-element.44), channel_id=1, source_target_pairs={{0,4},{1,5},{2,6},{3,7},{4,0},{5,1},{6,2},{7,3},{8,12},{9,13},{10,... | collective-permute-start | bytes 196616 | tf_op jit(solution)/shard_map/ppermute | solution.py:273
  45.3 7.7 %collective-permute-start.12 = (bf16[8,6144]{1,0:T(8,128)(2,1)S(1)}, bf16[8,6144]{1,0:T(8,128)(2,1)S(1)}, u32[]{:S(2)}, u32[]{:S(2)}) collective-permute-start(bf16[8,6144]{1,0:T(8,128)(2,1)S(1)} %get-tuple-element.41), channel_id=1, source_target_pairs={{0,12},{1,13},{2,14},{3,15},{4,8},{5,9},{6,10},{7,11},{8,4},{9,5},... | collective-permute-start | bytes 294920 | tf_op jit(solution)/shard_map/ppermute | solution.py:273
  47.5 8.2 %collective-permute-start.13 = (bf16[8,6144]{1,0:T(8,128)(2,1)S(1)}, bf16[8,6144]{1,0:T(8,128)(2,1)S(1)}, u32[]{:S(2)}, u32[]{:S(2)}) collective-permute-start(bf16[8,6144]{1,0:T(8,128)(2,1)S(1)} %get-tuple-element.43), channel_id=1, source_target_pairs={{0,8},{1,9},{2,10},{3,11},{4,12},{5,13},{6,14},{7,15},{8,0},{9,1},... | collective-permute-start | bytes 294920 | tf_op jit(solution)/shard_map/ppermute | solution.py:273
  47.5 8.2 %collective-permute-start.14 = (bf16[8,6144]{1,0:T(8,128)(2,1)S(1)}, bf16[8,6144]{1,0:T(8,128)(2,1)S(1)}, u32[]{:S(2)}, u32[]{:S(2)}) collective-permute-start(bf16[8,6144]{1,0:T(8,128)(2,1)S(1)} %get-tuple-element.42), channel_id=1, source_target_pairs={{0,4},{1,5},{2,6},{3,7},{4,0},{5,1},{6,2},{7,3},{8,12},{9,13},{10,... | collective-permute-start | bytes 294920 | tf_op jit(solution)/shard_map/ppermute | solution.py:273
  49.9 5.8 %collective-permute-start.19 = (bf16[8,8192]{1,0:T(8,128)(2,1)S(1)}, bf16[8,8192]{1,0:T(8,128)(2,1)S(1)}, u32[]{:S(2)}, u32[]{:S(2)}) collective-permute-start(bf16[8,8192]{1,0:T(8,128)(2,1)S(1)} %pad_maximum_fusion), channel_id=1, source_target_pairs={{0,2},{1,3},{2,0},{3,1},{4,6},{5,7},{6,4},{7,5},{8,10},{9,11},{10,... | collective-permute-start | bytes 393224 | tf_op jit(solution)/shard_map/ppermute | solution.py:273

commit v7 on v6

--- a/solution.py
+++ b/solution.py
@@ -277,13 +277,12 @@
         queries, incoming_pair, cache_key_value, cache_length, request_adapter, adapter_slot
     )
 
-    down = jnp.swapaxes(adapter_down, 1, 2)
-    down_other, a, own = lax.optimization_barrier((swap(down, 1), a, own))
-    factors = stage(down, down_other, adapter_up)
-
     apart = range(depths - 1, 0, -1)
     a_far = jnp.concatenate([swap(a, 4 * d) for d in apart], axis=0)
     side = swap(own, 2)
+    down = jnp.swapaxes(adapter_down, 1, 2)
+    down_other, a_far, side = lax.optimization_barrier((swap(down, 1), a_far, side))
+    factors = stage(down, down_other, adapter_up)
     b_sides = jnp.concatenate([own[:, GATHER_CUT:], side[:, GATHER_CUT:]], axis=0)
     a_side = swap(a_far, 2)
     b_far, _ = lax.optimization_barrier(([swap(b_sides, 4 * d) for d in apart], a_side))

time: 56.5 us -> 55.9 us (0.989)
  transfers between devices with their start and end apart: 20 -> 20, of which waited for: 10 -> 9; matrix products, arithmetic and copies ran while one was open for 1% -> 1% of each run, Pallas kernels for 11% -> 11%
where the time goes in v7:
time: 55.9 us; the launch traced here: 55.8 us
  starting transfers between devices  23.9 us (43%)
  waiting for transfers between devices  21.1 us (38%)
  Pallas kernels  9.19 us (16%)
  other arithmetic  1.29 us (2%)
    ppermute x20, starting transfers between devices, swap(): return lax.ppermute(x, 'rep', [(i, i ^ mask) for i in range(members)])  23.9 us
    ppermute x20, waiting for transfers between devices, swap(): return lax.ppermute(x, 'rep', [(i, i ^ mask) for i in range(members)])  21.1 us
    pallas_call x1, Pallas kernels, attend(): pl.pallas_call(attend_kernel, out_shape=(pltpu.VMEM((requests, GATHER_CUT...  3.34 us
    pallas_call x1, Pallas kernels, stage(): pl.pallas_call(stage_kernel, out_shape=pltpu.VMEM((WIDTH, 2 * ranks), jnp...  2.98 us
    pallas_call x2, Pallas kernels, project(): pl.pallas_call(functools.partial(project_kernel, first, 512), out_shape=(...  2.02 us
  transfers between devices with their start and end apart: 20, of which 9 were waited for; matrix products, arithmetic and copies ran while one was open for 1% of the time, Pallas kernels for 11%

profile of v7, /device:TPU:0, one launch (start us, length us, event | category | flops | bytes accessed | tf_op | source)
XLA Modules:
  0.0 55.8 jit_solution(13851709789823999242)
XLA Ops:
  0.0 0.0 copy-start.1
  0.0 0.5 collective-permute-start
  0.5 3.3 %attend.1 = (bf16[8,5888]{1,0:T(8,128)(2,1)S(1)}, bf16[8,8320]{1,0:T(8,128)(2,1)S(1)}) custom-call(s32[8]{0:T(128)} %length_hbm.1, s32[8]{0:T(128)} %adapter_hbm.1, s32[32]{0:T(128)} %slot_hbm.1, bf16[8,8192]{1,0:T(8,128)(2,1)} %query_hbm.1, bf16[8,2,1024]{2,1,0:T(2,128)(2,1)} %pair_hbm.1, bf16[8,2,128,1024]{3,2,1,0:T(8,128)(2,1)} %cache_hbm.1), custom_call_target="tpu_custom_call" | custom-call | flops 1000000000 | bytes 4194304 | tf_op jit(solution)/shard_map/attend/pallas_call | solution.py:144
  3.8 4.7 %collective-permute-start.1 = (bf16[8,5888]{1,0:T(8,128)(2,1)S(1)}, bf16[8,5888]{1,0:T(8,128)(2,1)S(1)}, u32[]{:S(2)}, u32[]{:S(2)}) collective-permute-start(bf16[8,5888]{1,0:T(8,128)(2,1)S(1)} %get-tuple-element.24), channel_id=1, source_target_pairs={{0,12},{1,13},{2,14},{3,15},{4,8},{5,9},{6,10},{7,11},{8,4},{9,5},... | collective-permute-start | bytes 282632 | tf_op jit(solution)/shard_map/ppermute | solution.py:273
  8.5 0.0 collective-permute-start.2
  8.5 0.6 %collective-permute-start.3 = (bf16[8,5888]{1,0:T(8,128)(2,1)S(1)}, bf16[8,5888]{1,0:T(8,128)(2,1)S(1)}, u32[]{:S(2)}, u32[]{:S(2)}) collective-permute-start(bf16[8,5888]{1,0:T(8,128)(2,1)S(1)} %get-tuple-element.24), channel_id=1, source_target_pairs={{0,4},{1,5},{2,6},{3,7},{4,0},{5,1},{6,2},{7,3},{8,12},{9,13},{10,... | collective-permute-start | bytes 282632 | tf_op jit(solution)/shard_map/ppermute | solution.py:273
  9.1 1.7 %collective-permute-start.4 = (bf16[8,8320]{1,0:T(8,128)(2,1)S(1)}, bf16[8,8320]{1,0:T(8,128)(2,1)S(1)}, u32[]{:S(2)}, u32[]{:S(2)}) collective-permute-start(bf16[8,8320]{1,0:T(8,128)(2,1)S(1)} %get-tuple-element.23), channel_id=1, source_target_pairs={{0,2},{1,3},{2,0},{3,1},{4,6},{5,7},{6,4},{7,5},{8,10},{9,11},{10,... | collective-permute-start | bytes 399368 | tf_op jit(solution)/shard_map/ppermute | solution.py:273
  10.8 1.3 %collective-permute-done.1 = bf16[8,5888]{1,0:T(8,128)(2,1)S(1)} collective-permute-done((bf16[8,5888]{1,0:T(8,128)(2,1)S(1)}, bf16[8,5888]{1,0:T(8,128)(2,1)S(1)}, u32[]{:S(2)}, u32[]{:S(2)}) %collective-permute-start.1) | collective-permute-done | bytes 94240 | tf_op jit(solution)/shard_map/ppermute | solution.py:273
  12.1 4.8 %collective-permute-done.2 = bf16[8,5888]{1,0:T(8,128)(2,1)S(1)} collective-permute-done((bf16[8,5888]{1,0:T(8,128)(2,1)S(1)}, bf16[8,5888]{1,0:T(8,128)(2,1)S(1)}, u32[]{:S(2)}, u32[]{:S(2)}) %collective-permute-start.2) | collective-permute-done | bytes 94240 | tf_op jit(solution)/shard_map/ppermute | solution.py:273
  16.9 0.0 collective-permute-done.3
  16.9 0.0 collective-permute-done.4
  16.9 0.0 collective-permute-done
  17.0 1.6 %collective-permute-start.8 = (bf16[24,5888]{1,0:T(8,128)(2,1)S(1)}, bf16[24,5888]{1,0:T(8,128)(2,1)S(1)}, u32[]{:S(2)}, u32[]{:S(2)}) collective-permute-start(bf16[24,5888]{1,0:T(8,128)(2,1)S(1)} %pad_maximum_fusion), channel_id=1, source_target_pairs={{0,2},{1,3},{2,0},{3,1},{4,6},{5,7},{6,4},{7,5},{8,10},{9,11},{10,... | collective-permute-start | bytes 847880 | tf_op jit(solution)/shard_map/ppermute | solution.py:273
  18.5 2.5 %collective-permute-start.5 = (bf16[16,2432]{1,0:T(8,128)(2,1)S(1)}, bf16[16,2432]{1,0:T(8,128)(2,1)S(1)}, u32[]{:S(2)}, u32[]{:S(2)}) collective-permute-start(bf16[16,2432]{1,0:T(8,128)(2,1)S(1)} %pad_maximum_fusion.2), channel_id=1, source_target_pairs={{0,12},{1,13},{2,14},{3,15},{4,8},{5,9},{6,10},{7,11},{8,4},{9,5},... | collective-permute-start | bytes 233480 | tf_op jit(solution)/shard_map/ppermute | solution.py:273
  21.0 0.0 collective-permute-start.6
  21.0 1.9 %collective-permute-start.7 = (bf16[16,2432]{1,0:T(8,128)(2,1)S(1)}, bf16[16,2432]{1,0:T(8,128)(2,1)S(1)}, u32[]{:S(2)}, u32[]{:S(2)}) collective-permute-start(bf16[16,2432]{1,0:T(8,128)(2,1)S(1)} %pad_maximum_fusion.2), channel_id=1, source_target_pairs={{0,4},{1,5},{2,6},{3,7},{4,0},{5,1},{6,2},{7,3},{8,12},{9,13},{10,... | collective-permute-start | bytes 233480 | tf_op jit(solution)/shard_map/ppermute | solution.py:273
  22.9 0.0 copy-done.1
  22.9 0.0 copy-start
  22.9 3.0 %stage.1.factors_ref = bf16[8192,256]{1,0:T(8,128)(2,1)S(1)} custom-call(bf16[128,8192]{1,0:T(8,128)(2,1)} %bitcast.68, bf16[128,8192]{1,0:T(8,128)(2,1)} %bitcast.12.down_other_ref, bf16[2,64,8192]{2,1,0:T(8,128)(2,1)S(1)} %copy-done.1), custom_call_target="tpu_custom_call" | custom-call | flops 100000000 | bytes 8388608 | tf_op jit(solution)/shard_map/stage/pallas_call | solution.py:185
  25.9 0.0 collective-permute-done.5
  25.9 2.1 %collective-permute-done.6 = bf16[16,2432]{1,0:T(8,128)(2,1)S(1)} collective-permute-done((bf16[16,2432]{1,0:T(8,128)(2,1)S(1)}, bf16[16,2432]{1,0:T(8,128)(2,1)S(1)}, u32[]{:S(2)}, u32[]{:S(2)}) %collective-permute-start.6) | collective-permute-done | bytes 77856 | tf_op jit(solution)/shard_map/ppermute | solution.py:273
  28.0 0.0 collective-permute-done.7
  28.0 0.0 collective-permute-done.8
  28.1 0.1 maximum_maximum_fusion.rows_ref
  28.2 0.0 copy-done
  28.2 0.8 %shrink.1 = (bf16[64,640]{1,0:T(8,128)(2,1)S(1)}, bf16[64,640]{1,0:T(8,128)(2,1)S(1)}) custom-call(s32[1]{0:T(128)} %bitcast.device_ref, bf16[64,8320]{1,0:T(8,128)(2,1)S(1)} %maximum_maximum_fusion.rows_ref, bf16[8192,256]{1,0:T(8,128)(2,1)S(1)} %stage.1.factors_ref, bf16[512,8192]{1,0:T(8,128)(2,1)S(1)} %copy-done), custom_call_target="tpu_custom_call" | custom-call | flops 268435456 | bytes 4194304 | tf_op jit(solution)/shard_map/shrink/pallas_call | solution.py:221
  29.0 0.1 collective-permute-start.9
  29.1 1.3 %collective-permute-done.9.x_other_ref = bf16[64,640]{1,0:T(8,128)(2,1)S(1)} collective-permute-done((bf16[64,640]{1,0:T(8,128)(2,1)S(1)}, bf16[64,640]{1,0:T(8,128)(2,1)S(1)}, u32[]{:S(2)}, u32[]{:S(2)}) %collective-permute-start.9) | collective-permute-done | bytes 81952 | tf_op jit(solution)/shard_map/ppermute | solution.py:273
  30.4 1.4 %project.2 = (f32[64,6144]{1,0:T(8,128)S(1)}, bf16[64,6144]{1,0:T(8,128)(2,1)S(1)}) custom-call(bf16[64,640]{1,0:T(8,128)(2,1)S(1)} %get-tuple-element.35.x_ref, bf16[64,640]{1,0:T(8,128)(2,1)S(1)} %collective-permute-done.9.x_other_ref, bf16[512,8192]{1,0:T(8,128)(2,1)S(1)} %copy-done, bf16[2,64,8192]{2,1,0:T(8,128)(2,1)S(1)} %copy-done.1), custom_call_target="tpu_custom_call" | custom-call | flops 1006632960 | bytes 7864320 | tf_op jit(solution)/shard_map/project/pallas_call | solution.py:251
  31.8 0.2 collective-permute-start.10
  32.0 2.1 %collective-permute-done.10 = bf16[64,6144]{1,0:T(8,128)(2,1)S(1)} collective-permute-done((bf16[64,6144]{1,0:T(8,128)(2,1)S(1)}, bf16[64,6144]{1,0:T(8,128)(2,1)S(1)}, u32[]{:S(2)}, u32[]{:S(2)}) %collective-permute-start.10) | collective-permute-done | bytes 786464 | tf_op jit(solution)/shard_map/ppermute | solution.py:273
  34.2 0.2 convert_add_fusion
  34.3 0.1 convert.11
  34.4 0.6 %project.3 = (f32[64,2048]{1,0:T(8,128)S(1)}, bf16[64,2048]{1,0:T(8,128)(2,1)S(1)}) custom-call(bf16[64,640]{1,0:T(8,128)(2,1)S(1)} %get-tuple-element.35.x_ref, bf16[64,640]{1,0:T(8,128)(2,1)S(1)} %collective-permute-done.9.x_other_ref, bf16[512,8192]{1,0:T(8,128)(2,1)S(1)} %copy-done, bf16[2,64,8192]{2,1,0:T(8,128)(2,1)S(1)} %copy-done.1), custom_call_target="tpu_custom_call" | custom-call | flops 335544320 | bytes 2621440 | tf_op jit(solution)/shard_map/project/pallas_call | solution.py:251
  35.0 0.2 collective-permute-start.15
  35.2 0.6 %collective-permute-start.11 = (bf16[3,8,6144]{2,1,0:T(8,128)(2,1)S(1)}, bf16[3,8,6144]{2,1,0:T(8,128)(2,1)S(1)}, u32[]{:S(2)}, u32[]{:S(2)}) collective-permute-start(bf16[3,8,6144]{2,1,0:T(8,128)(2,1)S(1)} %slice_bitcast_fusion.1), channel_id=1, source_target_pairs={{0,2},{1,3},{2,0},{3,1},{4,6},{5,7},{6,4},{7,5},{8,10},{9,11},{10,... | collective-permute-start | bytes 884744 | tf_op jit(solution)/shard_map/ppermute | solution.py:273
  35.8 0.8 %collective-permute-done.15 = bf16[64,2048]{1,0:T(8,128)(2,1)S(1)} collective-permute-done((bf16[64,2048]{1,0:T(8,128)(2,1)S(1)}, bf16[64,2048]{1,0:T(8,128)(2,1)S(1)}, u32[]{:S(2)}, u32[]{:S(2)}) %collective-permute-start.15) | collective-permute-done | bytes 262176 | tf_op jit(solution)/shard_map/ppermute | solution.py:273
  36.7 1.9 %collective-permute-start.16 = (bf16[2,8,2048]{2,1,0:T(8,128)(2,1)S(1)}, bf16[2,8,2048]{2,1,0:T(8,128)(2,1)S(1)}, u32[]{:S(2)}, u32[]{:S(2)}) collective-permute-start(bf16[2,8,2048]{2,1,0:T(8,128)(2,1)S(1)} %get-tuple-element.46), channel_id=1, source_target_pairs={{0,12},{1,13},{2,14},{3,15},{4,8},{5,9},{6,10},{7,11},{8,4},{9,5},... | collective-permute-start | bytes 196616 | tf_op jit(solution)/shard_map/ppermute | solution.py:273
  38.7 0.0 collective-permute-start.17
  38.7 2.5 %collective-permute-start.18 = (bf16[2,8,2048]{2,1,0:T(8,128)(2,1)S(1)}, bf16[2,8,2048]{2,1,0:T(8,128)(2,1)S(1)}, u32[]{:S(2)}, u32[]{:S(2)}) collective-permute-start(bf16[2,8,2048]{2,1,0:T(8,128)(2,1)S(1)} %get-tuple-element.44), channel_id=1, source_target_pairs={{0,4},{1,5},{2,6},{3,7},{4,0},{5,1},{6,2},{7,3},{8,12},{9,13},{10,... | collective-permute-start | bytes 196616 | tf_op jit(solution)/shard_map/ppermute | solution.py:273
  41.2 3.4 %collective-permute-done.11 = bf16[3,8,6144]{2,1,0:T(8,128)(2,1)S(1)} collective-permute-done((bf16[3,8,6144]{2,1,0:T(8,128)(2,1)S(1)}, bf16[3,8,6144]{2,1,0:T(8,128)(2,1)S(1)}, u32[]{:S(2)}, u32[]{:S(2)}) %collective-permute-start.11) | collective-permute-done | bytes 294944 | tf_op jit(solution)/shard_map/ppermute | solution.py:273
  44.6 0.1 fusion.1
  44.7 1.9 %collective-permute-start.12 = (bf16[8,6144]{1,0:T(8,128)(2,1)S(1)}, bf16[8,6144]{1,0:T(8,128)(2,1)S(1)}, u32[]{:S(2)}, u32[]{:S(2)}) collective-permute-start(bf16[8,6144]{1,0:T(8,128)(2,1)S(1)} %get-tuple-element.41), channel_id=1, source_target_pairs={{0,12},{1,13},{2,14},{3,15},{4,8},{5,9},{6,10},{7,11},{8,4},{9,5},... | collective-permute-start | bytes 294920 | tf_op jit(solution)/shard_map/ppermute | solution.py:273
  46.6 0.0 collective-permute-start.13
  46.6 0.0 collective-permute-done.16
  46.6 2.5 %collective-permute-start.14 = (bf16[8,6144]{1,0:T(8,128)(2,1)S(1)}, bf16[8,6144]{1,0:T(8,128)(2,1)S(1)}, u32[]{:S(2)}, u32[]{:S(2)}) collective-permute-start(bf16[8,6144]{1,0:T(8,128)(2,1)S(1)} %get-tuple-element.42), channel_id=1, source_target_pairs={{0,4},{1,5},{2,6},{3,7},{4,0},{5,1},{6,2},{7,3},{8,12},{9,13},{10,... | collective-permute-start | bytes 294920 | tf_op jit(solution)/shard_map/ppermute | solution.py:273
  49.2 0.0 collective-permute-done.17
  49.2 0.0 collective-permute-done.18
  49.3 0.6 collective-permute-start.19
  49.8 2.6 %collective-permute-done.12 = bf16[8,6144]{1,0:T(8,128)(2,1)S(1)} collective-permute-done((bf16[8,6144]{1,0:T(8,128)(2,1)S(1)}, bf16[8,6144]{1,0:T(8,128)(2,1)S(1)}, u32[]{:S(2)}, u32[]{:S(2)}) %collective-permute-start.12) | collective-permute-done | bytes 98336 | tf_op jit(solution)/shard_map/ppermute | solution.py:273
  52.4 2.6 %collective-permute-done.13 = bf16[8,6144]{1,0:T(8,128)(2,1)S(1)} collective-permute-done((bf16[8,6144]{1,0:T(8,128)(2,1)S(1)}, bf16[8,6144]{1,0:T(8,128)(2,1)S(1)}, u32[]{:S(2)}, u32[]{:S(2)}) %collective-permute-start.13) | collective-permute-done | bytes 98336 | tf_op jit(solution)/shard_map/ppermute | solution.py:273
  55.0 0.0 collective-permute-done.14
  55.1 0.0 collective-permute-done.19
  55.1 0.7 %fusion.2 = bf16[8,8192]{1,0:T(8,128)(2,1)} fusion(f32[8,2048]{1,0:T(8,128)S(1)} %slice_bitcast_fusion.10, f32[8,6144]{1,0:T(8,128)S(1)} %fusion.5, bf16[8,8192]{1,0:T(8,128)(2,1)S(1)} %collective-permute-done.19), kind=kLoop, calls=%fused_computation.9 | loop fusion | flops 262144 | bytes 524288 | tf_op jit(solution)/shard_map/convert_element_type | solution.py:325
  (16 shorter events, 0.3 us)
Async XLA Ops:
  0.0 22.9 %copy-start.1 = (bf16[2,64,8192]{2,1,0:T(8,128)(2,1)S(1)}, bf16[2,64,8192]{2,1,0:T(8,128)(2,1)}, u32[]{:S(2)}) copy-start(bf16[2,64,8192]{2,1,0:T(8,128)(2,1)} %up_ref.5) | copy-start | bytes 6291460
  0.0 16.9 %collective-permute-start = (bf16[2,64,8192]{2,1,0:T(8,128)(2,1)}, bf16[2,64,8192]{2,1,0:T(8,128)(2,1)}, u32[]{:S(2)}, u32[]{:S(2)}) collective-permute-start(bf16[2,64,8192]{2,1,0:T(8,128)(2,1)} %bitcast.67), channel_id=1, source_target_pairs={{0,1},{1,0},{2,3},{3,2},{4,5},{5,4},{6,7},{7,6},{8,9},{9,8},{10,11... | collective-permute-start | bytes 6291464 | tf_op jit(solution)/shard_map/ppermute | solution.py:273
  3.8 8.3 %collective-permute-start.1 = (bf16[8,5888]{1,0:T(8,128)(2,1)S(1)}, bf16[8,5888]{1,0:T(8,128)(2,1)S(1)}, u32[]{:S(2)}, u32[]{:S(2)}) collective-permute-start(bf16[8,5888]{1,0:T(8,128)(2,1)S(1)} %get-tuple-element.24), channel_id=1, source_target_pairs={{0,12},{1,13},{2,14},{3,15},{4,8},{5,9},{6,10},{7,11},{8,4},{9,5},... | collective-permute-start | bytes 282632 | tf_op jit(solution)/shard_map/ppermute | solution.py:273
  8.5 8.4 %collective-permute-start.2 = (bf16[8,5888]{1,0:T(8,128)(2,1)S(1)}, bf16[8,5888]{1,0:T(8,128)(2,1)S(1)}, u32[]{:S(2)}, u32[]{:S(2)}) collective-permute-start(bf16[8,5888]{1,0:T(8,128)(2,1)S(1)} %get-tuple-element.24), channel_id=1, source_target_pairs={{0,8},{1,9},{2,10},{3,11},{4,12},{5,13},{6,14},{7,15},{8,0},{9,1},... | collective-permute-start | bytes 282632 | tf_op jit(solution)/shard_map/ppermute | solution.py:273
  8.5 8.4 %collective-permute-start.3 = (bf16[8,5888]{1,0:T(8,128)(2,1)S(1)}, bf16[8,5888]{1,0:T(8,128)(2,1)S(1)}, u32[]{:S(2)}, u32[]{:S(2)}) collective-permute-start(bf16[8,5888]{1,0:T(8,128)(2,1)S(1)} %get-tuple-element.24), channel_id=1, source_target_pairs={{0,4},{1,5},{2,6},{3,7},{4,0},{5,1},{6,2},{7,3},{8,12},{9,13},{10,... | collective-permute-start | bytes 282632 | tf_op jit(solution)/shard_map/ppermute | solution.py:273
  9.1 7.8 %collective-permute-start.4 = (bf16[8,8320]{1,0:T(8,128)(2,1)S(1)}, bf16[8,8320]{1,0:T(8,128)(2,1)S(1)}, u32[]{:S(2)}, u32[]{:S(2)}) collective-permute-start(bf16[8,8320]{1,0:T(8,128)(2,1)S(1)} %get-tuple-element.23), channel_id=1, source_target_pairs={{0,2},{1,3},{2,0},{3,1},{4,6},{5,7},{6,4},{7,5},{8,10},{9,11},{10,... | collective-permute-start | bytes 399368 | tf_op jit(solution)/shard_map/ppermute | solution.py:273
  17.0 11.0 %collective-permute-start.8 = (bf16[24,5888]{1,0:T(8,128)(2,1)S(1)}, bf16[24,5888]{1,0:T(8,128)(2,1)S(1)}, u32[]{:S(2)}, u32[]{:S(2)}) collective-permute-start(bf16[24,5888]{1,0:T(8,128)(2,1)S(1)} %pad_maximum_fusion), channel_id=1, source_target_pairs={{0,2},{1,3},{2,0},{3,1},{4,6},{5,7},{6,4},{7,5},{8,10},{9,11},{10,... | collective-permute-start | bytes 847880 | tf_op jit(solution)/shard_map/ppermute | solution.py:273
  18.5 7.4 %collective-permute-start.5 = (bf16[16,2432]{1,0:T(8,128)(2,1)S(1)}, bf16[16,2432]{1,0:T(8,128)(2,1)S(1)}, u32[]{:S(2)}, u32[]{:S(2)}) collective-permute-start(bf16[16,2432]{1,0:T(8,128)(2,1)S(1)} %pad_maximum_fusion.2), channel_id=1, source_target_pairs={{0,12},{1,13},{2,14},{3,15},{4,8},{5,9},{6,10},{7,11},{8,4},{9,5},... | collective-permute-start | bytes 233480 | tf_op jit(solution)/shard_map/ppermute | solution.py:273
  21.0 7.0 %collective-permute-start.6 = (bf16[16,2432]{1,0:T(8,128)(2,1)S(1)}, bf16[16,2432]{1,0:T(8,128)(2,1)S(1)}, u32[]{:S(2)}, u32[]{:S(2)}) collective-permute-start(bf16[16,2432]{1,0:T(8,128)(2,1)S(1)} %pad_maximum_fusion.2), channel_id=1, source_target_pairs={{0,8},{1,9},{2,10},{3,11},{4,12},{5,13},{6,14},{7,15},{8,0},{9,1},... | collective-permute-start | bytes 233480 | tf_op jit(solution)/shard_map/ppermute | solution.py:273
  21.0 7.0 %collective-permute-start.7 = (bf16[16,2432]{1,0:T(8,128)(2,1)S(1)}, bf16[16,2432]{1,0:T(8,128)(2,1)S(1)}, u32[]{:S(2)}, u32[]{:S(2)}) collective-permute-start(bf16[16,2432]{1,0:T(8,128)(2,1)S(1)} %pad_maximum_fusion.2), channel_id=1, source_target_pairs={{0,4},{1,5},{2,6},{3,7},{4,0},{5,1},{6,2},{7,3},{8,12},{9,13},{10,... | collective-permute-start | bytes 233480 | tf_op jit(solution)/shard_map/ppermute | solution.py:273
  22.9 5.2 %copy-start = (bf16[512,8192]{1,0:T(8,128)(2,1)S(1)}, bf16[512,8192]{1,0:T(8,128)(2,1)}, u32[]{:S(2)}) copy-start(bf16[512,8192]{1,0:T(8,128)(2,1)} %weight_ref.5) | copy-start | bytes 25165828
  29.0 1.3 %collective-permute-start.9 = (bf16[64,640]{1,0:T(8,128)(2,1)S(1)}, bf16[64,640]{1,0:T(8,128)(2,1)S(1)}, u32[]{:S(2)}, u32[]{:S(2)}) collective-permute-start(bf16[64,640]{1,0:T(8,128)(2,1)S(1)} %get-tuple-element.32), channel_id=1, source_target_pairs={{0,1},{1,0},{2,3},{3,2},{4,5},{5,4},{6,7},{7,6},{8,9},{9,8},{10,11... | collective-permute-start | bytes 245768 | tf_op jit(solution)/shard_map/ppermute | solution.py:273
  31.8 2.4 %collective-permute-start.10 = (bf16[64,6144]{1,0:T(8,128)(2,1)S(1)}, bf16[64,6144]{1,0:T(8,128)(2,1)S(1)}, u32[]{:S(2)}, u32[]{:S(2)}) collective-permute-start(bf16[64,6144]{1,0:T(8,128)(2,1)S(1)} %get-tuple-element.34), channel_id=1, source_target_pairs={{0,1},{1,0},{2,3},{3,2},{4,5},{5,4},{6,7},{7,6},{8,9},{9,8},{10,11... | collective-permute-start | bytes 2359304 | tf_op jit(solution)/shard_map/ppermute | solution.py:273
  35.0 1.6 %collective-permute-start.15 = (bf16[64,2048]{1,0:T(8,128)(2,1)S(1)}, bf16[64,2048]{1,0:T(8,128)(2,1)S(1)}, u32[]{:S(2)}, u32[]{:S(2)}) collective-permute-start(bf16[64,2048]{1,0:T(8,128)(2,1)S(1)} %get-tuple-element.37), channel_id=1, source_target_pairs={{0,1},{1,0},{2,3},{3,2},{4,5},{5,4},{6,7},{7,6},{8,9},{9,8},{10,11... | collective-permute-start | bytes 786440 | tf_op jit(solution)/shard_map/ppermute | solution.py:273
  35.2 9.3 %collective-permute-start.11 = (bf16[3,8,6144]{2,1,0:T(8,128)(2,1)S(1)}, bf16[3,8,6144]{2,1,0:T(8,128)(2,1)S(1)}, u32[]{:S(2)}, u32[]{:S(2)}) collective-permute-start(bf16[3,8,6144]{2,1,0:T(8,128)(2,1)S(1)} %slice_bitcast_fusion.1), channel_id=1, source_target_pairs={{0,2},{1,3},{2,0},{3,1},{4,6},{5,7},{6,4},{7,5},{8,10},{9,11},{10,... | collective-permute-start | bytes 884744 | tf_op jit(solution)/shard_map/ppermute | solution.py:273
  36.7 9.9 %collective-permute-start.16 = (bf16[2,8,2048]{2,1,0:T(8,128)(2,1)S(1)}, bf16[2,8,2048]{2,1,0:T(8,128)(2,1)S(1)}, u32[]{:S(2)}, u32[]{:S(2)}) collective-permute-start(bf16[2,8,2048]{2,1,0:T(8,128)(2,1)S(1)} %get-tuple-element.46), channel_id=1, source_target_pairs={{0,12},{1,13},{2,14},{3,15},{4,8},{5,9},{6,10},{7,11},{8,4},{9,5},... | collective-permute-start | bytes 196616 | tf_op jit(solution)/shard_map/ppermute | solution.py:273
  38.7 10.5 %collective-permute-start.17 = (bf16[2,8,2048]{2,1,0:T(8,128)(2,1)S(1)}, bf16[2,8,2048]{2,1,0:T(8,128)(2,1)S(1)}, u32[]{:S(2)}, u32[]{:S(2)}) collective-permute-start(bf16[2,8,2048]{2,1,0:T(8,128)(2,1)S(1)} %get-tuple-element.45), channel_id=1, source_target_pairs={{0,8},{1,9},{2,10},{3,11},{4,12},{5,13},{6,14},{7,15},{8,0},{9,1},... | collective-permute-start | bytes 196616 | tf_op jit(solution)/shard_map/ppermute | solution.py:273
  38.7 10.5 %collective-permute-start.18 = (bf16[2,8,2048]{2,1,0:T(8,128)(2,1)S(1)}, bf16[2,8,2048]{2,1,0:T(8,128)(2,1)S(1)}, u32[]{:S(2)}, u32[]{:S(2)}) collective-permute-start(bf16[2,8,2048]{2,1,0:T(8,128)(2,1)S(1)} %get-tuple-element.44), channel_id=1, source_target_pairs={{0,4},{1,5},{2,6},{3,7},{4,0},{5,1},{6,2},{7,3},{8,12},{9,13},{10,... | collective-permute-start | bytes 196616 | tf_op jit(solution)/shard_map/ppermute | solution.py:273
  44.7 7.7 %collective-permute-start.12 = (bf16[8,6144]{1,0:T(8,128)(2,1)S(1)}, bf16[8,6144]{1,0:T(8,128)(2,1)S(1)}, u32[]{:S(2)}, u32[]{:S(2)}) collective-permute-start(bf16[8,6144]{1,0:T(8,128)(2,1)S(1)} %get-tuple-element.41), channel_id=1, source_target_pairs={{0,12},{1,13},{2,14},{3,15},{4,8},{5,9},{6,10},{7,11},{8,4},{9,5},... | collective-permute-start | bytes 294920 | tf_op jit(solution)/shard_map/ppermute | solution.py:273
  46.6 8.4 %collective-permute-start.13 = (bf16[8,6144]{1,0:T(8,128)(2,1)S(1)}, bf16[8,6144]{1,0:T(8,128)(2,1)S(1)}, u32[]{:S(2)}, u32[]{:S(2)}) collective-permute-start(bf16[8,6144]{1,0:T(8,128)(2,1)S(1)} %get-tuple-element.43), channel_id=1, source_target_pairs={{0,8},{1,9},{2,10},{3,11},{4,12},{5,13},{6,14},{7,15},{8,0},{9,1},... | collective-permute-start | bytes 294920 | tf_op jit(solution)/shard_map/ppermute | solution.py:273
  46.6 8.4 %collective-permute-start.14 = (bf16[8,6144]{1,0:T(8,128)(2,1)S(1)}, bf16[8,6144]{1,0:T(8,128)(2,1)S(1)}, u32[]{:S(2)}, u32[]{:S(2)}) collective-permute-start(bf16[8,6144]{1,0:T(8,128)(2,1)S(1)} %get-tuple-element.42), channel_id=1, source_target_pairs={{0,4},{1,5},{2,6},{3,7},{4,0},{5,1},{6,2},{7,3},{8,12},{9,13},{10,... | collective-permute-start | bytes 294920 | tf_op jit(solution)/shard_map/ppermute | solution.py:273
  49.3 5.8 %collective-permute-start.19 = (bf16[8,8192]{1,0:T(8,128)(2,1)S(1)}, bf16[8,8192]{1,0:T(8,128)(2,1)S(1)}, u32[]{:S(2)}, u32[]{:S(2)}) collective-permute-start(bf16[8,8192]{1,0:T(8,128)(2,1)S(1)} %pad_maximum_fusion.1), channel_id=1, source_target_pairs={{0,2},{1,3},{2,0},{3,1},{4,6},{5,7},{6,4},{7,5},{8,10},{9,11},{10,... | collective-permute-start | bytes 393224 | tf_op jit(solution)/shard_map/ppermute | solution.py:273

commit v8 on v7

--- a/solution.py
+++ b/solution.py
@@ -13,11 +13,11 @@
 GROUP = QUERY_HEADS // KEY_VALUE_HEADS
 WIDTH = QUERY_HEADS * HEAD_SIZE
 LANES = 128
-BATCH = 4
+FIRST = 3
 ADAPTER_GAIN = 2.0
 MASKED_SCORE = -1e30
 
-GATHER_CUT = 5888
+GATHER_CUT = 6144
 SCATTER_CUT = 6144
 
 NT = (((1,), (1,)), ((), ()))
@@ -77,8 +77,7 @@
     position = lax.broadcasted_iota(jnp.int32, (QUERY_HEADS, slots), 1)
     blank = jnp.zeros((GROUP, HEAD_SIZE), jnp.float32)
     pairs = KEY_VALUE_HEADS // 2
-    for r in range(0, requests, BATCH):
-        batch = range(r, r + BATCH)
+    for batch in (range(FIRST), range(FIRST, requests)):
         for t in batch:
             fetch(t).wait()
         scores = []

time: 55.9 us -> 55.9 us (level)
  no operation moved by 1% of the time
where the time goes in v8:
time: 55.9 us; the launch traced here: 55.8 us
  starting transfers between devices  23.9 us (43%)
  waiting for transfers between devices  20.9 us (37%)
  Pallas kernels  9.18 us (16%)
  other arithmetic  1.29 us (2%)
    ppermute x20, starting transfers between devices, swap(): return lax.ppermute(x, 'rep', [(i, i ^ mask) for i in range(members)])  23.9 us
    ppermute x20, waiting for transfers between devices, swap(): return lax.ppermute(x, 'rep', [(i, i ^ mask) for i in range(members)])  20.9 us
    pallas_call x1, Pallas kernels, attend(): pl.pallas_call(attend_kernel, out_shape=(pltpu.VMEM((requests, GATHER_CUT...  3.36 us
    pallas_call x1, Pallas kernels, stage(): pl.pallas_call(stage_kernel, out_shape=pltpu.VMEM((WIDTH, 2 * ranks), jnp...  2.98 us
    pallas_call x2, Pallas kernels, project(): pl.pallas_call(functools.partial(project_kernel, first, 512), out_shape=(...  2 us
  transfers between devices with their start and end apart: 20, of which 9 were waited for; matrix products, arithmetic and copies ran while one was open for 1% of the time, Pallas kernels for 11%

profile of v8, /device:TPU:0, one launch (start us, length us, event | category | flops | bytes accessed | tf_op | source)
XLA Modules:
  0.0 55.8 jit_solution(16613386050198685269)
XLA Ops:
  0.0 0.0 copy-start.1
  0.0 0.5 collective-permute-start
  0.5 3.4 %attend.1 = (bf16[8,6144]{1,0:T(8,128)(2,1)S(1)}, bf16[8,8320]{1,0:T(8,128)(2,1)S(1)}) custom-call(s32[8]{0:T(128)} %length_hbm.1, s32[8]{0:T(128)} %adapter_hbm.1, s32[32]{0:T(128)} %slot_hbm.1, bf16[8,8192]{1,0:T(8,128)(2,1)} %query_hbm.1, bf16[8,2,1024]{2,1,0:T(2,128)(2,1)} %pair_hbm.1, bf16[8,2,128,1024]{3,2,1,0:T(8,128)(2,1)} %cache_hbm.1), custom_call_target="tpu_custom_call" | custom-call | flops 1000000000 | bytes 4194304 | tf_op jit(solution)/shard_map/attend/pallas_call | solution.py:143
  3.8 4.7 %collective-permute-start.1 = (bf16[8,6144]{1,0:T(8,128)(2,1)S(1)}, bf16[8,6144]{1,0:T(8,128)(2,1)S(1)}, u32[]{:S(2)}, u32[]{:S(2)}) collective-permute-start(bf16[8,6144]{1,0:T(8,128)(2,1)S(1)} %get-tuple-element.24), channel_id=1, source_target_pairs={{0,12},{1,13},{2,14},{3,15},{4,8},{5,9},{6,10},{7,11},{8,4},{9,5},... | collective-permute-start | bytes 294920 | tf_op jit(solution)/shard_map/ppermute | solution.py:272
  8.5 0.0 collective-permute-start.2
  8.5 0.6 %collective-permute-start.3 = (bf16[8,6144]{1,0:T(8,128)(2,1)S(1)}, bf16[8,6144]{1,0:T(8,128)(2,1)S(1)}, u32[]{:S(2)}, u32[]{:S(2)}) collective-permute-start(bf16[8,6144]{1,0:T(8,128)(2,1)S(1)} %get-tuple-element.24), channel_id=1, source_target_pairs={{0,4},{1,5},{2,6},{3,7},{4,0},{5,1},{6,2},{7,3},{8,12},{9,13},{10,... | collective-permute-start | bytes 294920 | tf_op jit(solution)/shard_map/ppermute | solution.py:272
  9.1 1.7 %collective-permute-start.4 = (bf16[8,8320]{1,0:T(8,128)(2,1)S(1)}, bf16[8,8320]{1,0:T(8,128)(2,1)S(1)}, u32[]{:S(2)}, u32[]{:S(2)}) collective-permute-start(bf16[8,8320]{1,0:T(8,128)(2,1)S(1)} %get-tuple-element.23), channel_id=1, source_target_pairs={{0,2},{1,3},{2,0},{3,1},{4,6},{5,7},{6,4},{7,5},{8,10},{9,11},{10,... | collective-permute-start | bytes 399368 | tf_op jit(solution)/shard_map/ppermute | solution.py:272
  10.8 1.4 %collective-permute-done.1 = bf16[8,6144]{1,0:T(8,128)(2,1)S(1)} collective-permute-done((bf16[8,6144]{1,0:T(8,128)(2,1)S(1)}, bf16[8,6144]{1,0:T(8,128)(2,1)S(1)}, u32[]{:S(2)}, u32[]{:S(2)}) %collective-permute-start.1) | collective-permute-done | bytes 98336 | tf_op jit(solution)/shard_map/ppermute | solution.py:272
  12.2 5.1 %collective-permute-done.2 = bf16[8,6144]{1,0:T(8,128)(2,1)S(1)} collective-permute-done((bf16[8,6144]{1,0:T(8,128)(2,1)S(1)}, bf16[8,6144]{1,0:T(8,128)(2,1)S(1)}, u32[]{:S(2)}, u32[]{:S(2)}) %collective-permute-start.2) | collective-permute-done | bytes 98336 | tf_op jit(solution)/shard_map/ppermute | solution.py:272
  17.3 0.0 collective-permute-done.3
  17.3 0.0 collective-permute-done.4
  17.3 0.0 collective-permute-done
  17.3 1.6 %collective-permute-start.8 = (bf16[24,6144]{1,0:T(8,128)(2,1)S(1)}, bf16[24,6144]{1,0:T(8,128)(2,1)S(1)}, u32[]{:S(2)}, u32[]{:S(2)}) collective-permute-start(bf16[24,6144]{1,0:T(8,128)(2,1)S(1)} %pad_maximum_fusion), channel_id=1, source_target_pairs={{0,2},{1,3},{2,0},{3,1},{4,6},{5,7},{6,4},{7,5},{8,10},{9,11},{10,... | collective-permute-start | bytes 884744 | tf_op jit(solution)/shard_map/ppermute | solution.py:272
  18.9 2.5 %collective-permute-start.5 = (bf16[16,2176]{1,0:T(8,128)(2,1)S(1)}, bf16[16,2176]{1,0:T(8,128)(2,1)S(1)}, u32[]{:S(2)}, u32[]{:S(2)}) collective-permute-start(bf16[16,2176]{1,0:T(8,128)(2,1)S(1)} %pad_maximum_fusion.2), channel_id=1, source_target_pairs={{0,12},{1,13},{2,14},{3,15},{4,8},{5,9},{6,10},{7,11},{8,4},{9,5},... | collective-permute-start | bytes 208904 | tf_op jit(solution)/shard_map/ppermute | solution.py:272
  21.4 0.0 collective-permute-start.6
  21.4 1.9 %collective-permute-start.7 = (bf16[16,2176]{1,0:T(8,128)(2,1)S(1)}, bf16[16,2176]{1,0:T(8,128)(2,1)S(1)}, u32[]{:S(2)}, u32[]{:S(2)}) collective-permute-start(bf16[16,2176]{1,0:T(8,128)(2,1)S(1)} %pad_maximum_fusion.2), channel_id=1, source_target_pairs={{0,4},{1,5},{2,6},{3,7},{4,0},{5,1},{6,2},{7,3},{8,12},{9,13},{10,... | collective-permute-start | bytes 208904 | tf_op jit(solution)/shard_map/ppermute | solution.py:272
  23.3 0.0 copy-done.1
  23.3 0.0 copy-start
  23.3 3.0 %stage.1.factors_ref = bf16[8192,256]{1,0:T(8,128)(2,1)S(1)} custom-call(bf16[128,8192]{1,0:T(8,128)(2,1)} %bitcast.68, bf16[128,8192]{1,0:T(8,128)(2,1)} %bitcast.12.down_other_ref, bf16[2,64,8192]{2,1,0:T(8,128)(2,1)S(1)} %copy-done.1), custom_call_target="tpu_custom_call" | custom-call | flops 100000000 | bytes 8388608 | tf_op jit(solution)/shard_map/stage/pallas_call | solution.py:184
  26.3 0.0 collective-permute-done.5
  26.3 1.4 %collective-permute-done.6 = bf16[16,2176]{1,0:T(8,128)(2,1)S(1)} collective-permute-done((bf16[16,2176]{1,0:T(8,128)(2,1)S(1)}, bf16[16,2176]{1,0:T(8,128)(2,1)S(1)}, u32[]{:S(2)}, u32[]{:S(2)}) %collective-permute-start.6) | collective-permute-done | bytes 69664 | tf_op jit(solution)/shard_map/ppermute | solution.py:272
  27.7 0.0 collective-permute-done.7
  27.7 0.0 collective-permute-done.8
  27.7 0.1 maximum_maximum_fusion.rows_ref
  27.8 0.1 copy-done
  28.0 0.8 %shrink.1 = (bf16[64,640]{1,0:T(8,128)(2,1)S(1)}, bf16[64,640]{1,0:T(8,128)(2,1)S(1)}) custom-call(s32[1]{0:T(128)} %bitcast.device_ref, bf16[64,8320]{1,0:T(8,128)(2,1)S(1)} %maximum_maximum_fusion.rows_ref, bf16[8192,256]{1,0:T(8,128)(2,1)S(1)} %stage.1.factors_ref, bf16[512,8192]{1,0:T(8,128)(2,1)S(1)} %copy-done), custom_call_target="tpu_custom_call" | custom-call | flops 268435456 | bytes 4194304 | tf_op jit(solution)/shard_map/shrink/pallas_call | solution.py:220
  28.8 0.1 collective-permute-start.9
  28.9 1.3 %collective-permute-done.9.x_other_ref = bf16[64,640]{1,0:T(8,128)(2,1)S(1)} collective-permute-done((bf16[64,640]{1,0:T(8,128)(2,1)S(1)}, bf16[64,640]{1,0:T(8,128)(2,1)S(1)}, u32[]{:S(2)}, u32[]{:S(2)}) %collective-permute-start.9) | collective-permute-done | bytes 81952 | tf_op jit(solution)/shard_map/ppermute | solution.py:272
  30.1 1.4 %project.2 = (f32[64,6144]{1,0:T(8,128)S(1)}, bf16[64,6144]{1,0:T(8,128)(2,1)S(1)}) custom-call(bf16[64,640]{1,0:T(8,128)(2,1)S(1)} %get-tuple-element.35.x_ref, bf16[64,640]{1,0:T(8,128)(2,1)S(1)} %collective-permute-done.9.x_other_ref, bf16[512,8192]{1,0:T(8,128)(2,1)S(1)} %copy-done, bf16[2,64,8192]{2,1,0:T(8,128)(2,1)S(1)} %copy-done.1), custom_call_target="tpu_custom_call" | custom-call | flops 1006632960 | bytes 7864320 | tf_op jit(solution)/shard_map/project/pallas_call | solution.py:250
  31.6 0.2 collective-permute-start.10
  31.8 2.1 %collective-permute-done.10 = bf16[64,6144]{1,0:T(8,128)(2,1)S(1)} collective-permute-done((bf16[64,6144]{1,0:T(8,128)(2,1)S(1)}, bf16[64,6144]{1,0:T(8,128)(2,1)S(1)}, u32[]{:S(2)}, u32[]{:S(2)}) %collective-permute-start.10) | collective-permute-done | bytes 786464 | tf_op jit(solution)/shard_map/ppermute | solution.py:272
  33.9 0.2 convert_add_fusion
  34.1 0.1 convert.11
  34.2 0.6 %project.3 = (f32[64,2048]{1,0:T(8,128)S(1)}, bf16[64,2048]{1,0:T(8,128)(2,1)S(1)}) custom-call(bf16[64,640]{1,0:T(8,128)(2,1)S(1)} %get-tuple-element.35.x_ref, bf16[64,640]{1,0:T(8,128)(2,1)S(1)} %collective-permute-done.9.x_other_ref, bf16[512,8192]{1,0:T(8,128)(2,1)S(1)} %copy-done, bf16[2,64,8192]{2,1,0:T(8,128)(2,1)S(1)} %copy-done.1), custom_call_target="tpu_custom_call" | custom-call | flops 335544320 | bytes 2621440 | tf_op jit(solution)/shard_map/project/pallas_call | solution.py:250
  34.8 0.2 collective-permute-start.15
  35.0 0.6 %collective-permute-start.11 = (bf16[3,8,6144]{2,1,0:T(8,128)(2,1)S(1)}, bf16[3,8,6144]{2,1,0:T(8,128)(2,1)S(1)}, u32[]{:S(2)}, u32[]{:S(2)}) collective-permute-start(bf16[3,8,6144]{2,1,0:T(8,128)(2,1)S(1)} %slice_bitcast_fusion.1), channel_id=1, source_target_pairs={{0,2},{1,3},{2,0},{3,1},{4,6},{5,7},{6,4},{7,5},{8,10},{9,11},{10,... | collective-permute-start | bytes 884744 | tf_op jit(solution)/shard_map/ppermute | solution.py:272
  35.6 0.8 %collective-permute-done.15 = bf16[64,2048]{1,0:T(8,128)(2,1)S(1)} collective-permute-done((bf16[64,2048]{1,0:T(8,128)(2,1)S(1)}, bf16[64,2048]{1,0:T(8,128)(2,1)S(1)}, u32[]{:S(2)}, u32[]{:S(2)}) %collective-permute-start.15) | collective-permute-done | bytes 262176 | tf_op jit(solution)/shard_map/ppermute | solution.py:272
  36.5 2.5 %collective-permute-start.16 = (bf16[2,8,2048]{2,1,0:T(8,128)(2,1)S(1)}, bf16[2,8,2048]{2,1,0:T(8,128)(2,1)S(1)}, u32[]{:S(2)}, u32[]{:S(2)}) collective-permute-start(bf16[2,8,2048]{2,1,0:T(8,128)(2,1)S(1)} %get-tuple-element.46), channel_id=1, source_target_pairs={{0,12},{1,13},{2,14},{3,15},{4,8},{5,9},{6,10},{7,11},{8,4},{9,5},... | collective-permute-start | bytes 196616 | tf_op jit(solution)/shard_map/ppermute | solution.py:272
  39.0 0.0 collective-permute-start.17
  39.0 1.9 %collective-permute-start.18 = (bf16[2,8,2048]{2,1,0:T(8,128)(2,1)S(1)}, bf16[2,8,2048]{2,1,0:T(8,128)(2,1)S(1)}, u32[]{:S(2)}, u32[]{:S(2)}) collective-permute-start(bf16[2,8,2048]{2,1,0:T(8,128)(2,1)S(1)} %get-tuple-element.44), channel_id=1, source_target_pairs={{0,4},{1,5},{2,6},{3,7},{4,0},{5,1},{6,2},{7,3},{8,12},{9,13},{10,... | collective-permute-start | bytes 196616 | tf_op jit(solution)/shard_map/ppermute | solution.py:272
  40.9 3.4 %collective-permute-done.11 = bf16[3,8,6144]{2,1,0:T(8,128)(2,1)S(1)} collective-permute-done((bf16[3,8,6144]{2,1,0:T(8,128)(2,1)S(1)}, bf16[3,8,6144]{2,1,0:T(8,128)(2,1)S(1)}, u32[]{:S(2)}, u32[]{:S(2)}) %collective-permute-start.11) | collective-permute-done | bytes 294944 | tf_op jit(solution)/shard_map/ppermute | solution.py:272
  44.4 0.1 fusion.1
  44.5 2.5 %collective-permute-start.12 = (bf16[8,6144]{1,0:T(8,128)(2,1)S(1)}, bf16[8,6144]{1,0:T(8,128)(2,1)S(1)}, u32[]{:S(2)}, u32[]{:S(2)}) collective-permute-start(bf16[8,6144]{1,0:T(8,128)(2,1)S(1)} %get-tuple-element.41), channel_id=1, source_target_pairs={{0,12},{1,13},{2,14},{3,15},{4,8},{5,9},{6,10},{7,11},{8,4},{9,5},... | collective-permute-start | bytes 294920 | tf_op jit(solution)/shard_map/ppermute | solution.py:272
  47.0 0.0 collective-permute-start.13
  47.0 0.0 collective-permute-done.16
  47.0 1.9 %collective-permute-start.14 = (bf16[8,6144]{1,0:T(8,128)(2,1)S(1)}, bf16[8,6144]{1,0:T(8,128)(2,1)S(1)}, u32[]{:S(2)}, u32[]{:S(2)}) collective-permute-start(bf16[8,6144]{1,0:T(8,128)(2,1)S(1)} %get-tuple-element.42), channel_id=1, source_target_pairs={{0,4},{1,5},{2,6},{3,7},{4,0},{5,1},{6,2},{7,3},{8,12},{9,13},{10,... | collective-permute-start | bytes 294920 | tf_op jit(solution)/shard_map/ppermute | solution.py:272
  48.9 0.0 collective-permute-done.17
  48.9 0.0 collective-permute-done.18
  49.0 0.6 %collective-permute-start.19 = (bf16[8,8192]{1,0:T(8,128)(2,1)S(1)}, bf16[8,8192]{1,0:T(8,128)(2,1)S(1)}, u32[]{:S(2)}, u32[]{:S(2)}) collective-permute-start(bf16[8,8192]{1,0:T(8,128)(2,1)S(1)} %pad_maximum_fusion.1), channel_id=1, source_target_pairs={{0,2},{1,3},{2,0},{3,1},{4,6},{5,7},{6,4},{7,5},{8,10},{9,11},{10,... | collective-permute-start | bytes 393224 | tf_op jit(solution)/shard_map/ppermute | solution.py:272
  49.6 2.5 %collective-permute-done.12 = bf16[8,6144]{1,0:T(8,128)(2,1)S(1)} collective-permute-done((bf16[8,6144]{1,0:T(8,128)(2,1)S(1)}, bf16[8,6144]{1,0:T(8,128)(2,1)S(1)}, u32[]{:S(2)}, u32[]{:S(2)}) %collective-permute-start.12) | collective-permute-done | bytes 98336 | tf_op jit(solution)/shard_map/ppermute | solution.py:272
  52.1 2.9 %collective-permute-done.13 = bf16[8,6144]{1,0:T(8,128)(2,1)S(1)} collective-permute-done((bf16[8,6144]{1,0:T(8,128)(2,1)S(1)}, bf16[8,6144]{1,0:T(8,128)(2,1)S(1)}, u32[]{:S(2)}, u32[]{:S(2)}) %collective-permute-start.13) | collective-permute-done | bytes 98336 | tf_op jit(solution)/shard_map/ppermute | solution.py:272
  55.0 0.0 collective-permute-done.14
  55.1 0.0 collective-permute-done.19
  55.1 0.7 %fusion.2 = bf16[8,8192]{1,0:T(8,128)(2,1)} fusion(f32[8,2048]{1,0:T(8,128)S(1)} %slice_bitcast_fusion.10, f32[8,6144]{1,0:T(8,128)S(1)} %fusion.5, bf16[8,8192]{1,0:T(8,128)(2,1)S(1)} %collective-permute-done.19), kind=kLoop, calls=%fused_computation.9 | loop fusion | flops 262144 | bytes 524288 | tf_op jit(solution)/shard_map/convert_element_type | solution.py:324
  (16 shorter events, 0.3 us)
Async XLA Ops:
  0.0 23.3 %copy-start.1 = (bf16[2,64,8192]{2,1,0:T(8,128)(2,1)S(1)}, bf16[2,64,8192]{2,1,0:T(8,128)(2,1)}, u32[]{:S(2)}) copy-start(bf16[2,64,8192]{2,1,0:T(8,128)(2,1)} %up_ref.5) | copy-start | bytes 6291460
  0.0 17.3 %collective-permute-start = (bf16[2,64,8192]{2,1,0:T(8,128)(2,1)}, bf16[2,64,8192]{2,1,0:T(8,128)(2,1)}, u32[]{:S(2)}, u32[]{:S(2)}) collective-permute-start(bf16[2,64,8192]{2,1,0:T(8,128)(2,1)} %bitcast.67), channel_id=1, source_target_pairs={{0,1},{1,0},{2,3},{3,2},{4,5},{5,4},{6,7},{7,6},{8,9},{9,8},{10,11... | collective-permute-start | bytes 6291464 | tf_op jit(solution)/shard_map/ppermute | solution.py:272
  3.8 8.4 %collective-permute-start.1 = (bf16[8,6144]{1,0:T(8,128)(2,1)S(1)}, bf16[8,6144]{1,0:T(8,128)(2,1)S(1)}, u32[]{:S(2)}, u32[]{:S(2)}) collective-permute-start(bf16[8,6144]{1,0:T(8,128)(2,1)S(1)} %get-tuple-element.24), channel_id=1, source_target_pairs={{0,12},{1,13},{2,14},{3,15},{4,8},{5,9},{6,10},{7,11},{8,4},{9,5},... | collective-permute-start | bytes 294920 | tf_op jit(solution)/shard_map/ppermute | solution.py:272
  8.5 8.8 %collective-permute-start.2 = (bf16[8,6144]{1,0:T(8,128)(2,1)S(1)}, bf16[8,6144]{1,0:T(8,128)(2,1)S(1)}, u32[]{:S(2)}, u32[]{:S(2)}) collective-permute-start(bf16[8,6144]{1,0:T(8,128)(2,1)S(1)} %get-tuple-element.24), channel_id=1, source_target_pairs={{0,8},{1,9},{2,10},{3,11},{4,12},{5,13},{6,14},{7,15},{8,0},{9,1},... | collective-permute-start | bytes 294920 | tf_op jit(solution)/shard_map/ppermute | solution.py:272
  8.5 8.8 %collective-permute-start.3 = (bf16[8,6144]{1,0:T(8,128)(2,1)S(1)}, bf16[8,6144]{1,0:T(8,128)(2,1)S(1)}, u32[]{:S(2)}, u32[]{:S(2)}) collective-permute-start(bf16[8,6144]{1,0:T(8,128)(2,1)S(1)} %get-tuple-element.24), channel_id=1, source_target_pairs={{0,4},{1,5},{2,6},{3,7},{4,0},{5,1},{6,2},{7,3},{8,12},{9,13},{10,... | collective-permute-start | bytes 294920 | tf_op jit(solution)/shard_map/ppermute | solution.py:272
  9.1 8.2 %collective-permute-start.4 = (bf16[8,8320]{1,0:T(8,128)(2,1)S(1)}, bf16[8,8320]{1,0:T(8,128)(2,1)S(1)}, u32[]{:S(2)}, u32[]{:S(2)}) collective-permute-start(bf16[8,8320]{1,0:T(8,128)(2,1)S(1)} %get-tuple-element.23), channel_id=1, source_target_pairs={{0,2},{1,3},{2,0},{3,1},{4,6},{5,7},{6,4},{7,5},{8,10},{9,11},{10,... | collective-permute-start | bytes 399368 | tf_op jit(solution)/shard_map/ppermute | solution.py:272
  17.3 10.3 %collective-permute-start.8 = (bf16[24,6144]{1,0:T(8,128)(2,1)S(1)}, bf16[24,6144]{1,0:T(8,128)(2,1)S(1)}, u32[]{:S(2)}, u32[]{:S(2)}) collective-permute-start(bf16[24,6144]{1,0:T(8,128)(2,1)S(1)} %pad_maximum_fusion), channel_id=1, source_target_pairs={{0,2},{1,3},{2,0},{3,1},{4,6},{5,7},{6,4},{7,5},{8,10},{9,11},{10,... | collective-permute-start | bytes 884744 | tf_op jit(solution)/shard_map/ppermute | solution.py:272
  18.9 7.4 %collective-permute-start.5 = (bf16[16,2176]{1,0:T(8,128)(2,1)S(1)}, bf16[16,2176]{1,0:T(8,128)(2,1)S(1)}, u32[]{:S(2)}, u32[]{:S(2)}) collective-permute-start(bf16[16,2176]{1,0:T(8,128)(2,1)S(1)} %pad_maximum_fusion.2), channel_id=1, source_target_pairs={{0,12},{1,13},{2,14},{3,15},{4,8},{5,9},{6,10},{7,11},{8,4},{9,5},... | collective-permute-start | bytes 208904 | tf_op jit(solution)/shard_map/ppermute | solution.py:272
  21.4 6.3 %collective-permute-start.6 = (bf16[16,2176]{1,0:T(8,128)(2,1)S(1)}, bf16[16,2176]{1,0:T(8,128)(2,1)S(1)}, u32[]{:S(2)}, u32[]{:S(2)}) collective-permute-start(bf16[16,2176]{1,0:T(8,128)(2,1)S(1)} %pad_maximum_fusion.2), channel_id=1, source_target_pairs={{0,8},{1,9},{2,10},{3,11},{4,12},{5,13},{6,14},{7,15},{8,0},{9,1},... | collective-permute-start | bytes 208904 | tf_op jit(solution)/shard_map/ppermute | solution.py:272
  21.4 6.3 %collective-permute-start.7 = (bf16[16,2176]{1,0:T(8,128)(2,1)S(1)}, bf16[16,2176]{1,0:T(8,128)(2,1)S(1)}, u32[]{:S(2)}, u32[]{:S(2)}) collective-permute-start(bf16[16,2176]{1,0:T(8,128)(2,1)S(1)} %pad_maximum_fusion.2), channel_id=1, source_target_pairs={{0,4},{1,5},{2,6},{3,7},{4,0},{5,1},{6,2},{7,3},{8,12},{9,13},{10,... | collective-permute-start | bytes 208904 | tf_op jit(solution)/shard_map/ppermute | solution.py:272
  23.3 4.6 %copy-start = (bf16[512,8192]{1,0:T(8,128)(2,1)S(1)}, bf16[512,8192]{1,0:T(8,128)(2,1)}, u32[]{:S(2)}) copy-start(bf16[512,8192]{1,0:T(8,128)(2,1)} %weight_ref.5) | copy-start | bytes 25165828
  28.8 1.3 %collective-permute-start.9 = (bf16[64,640]{1,0:T(8,128)(2,1)S(1)}, bf16[64,640]{1,0:T(8,128)(2,1)S(1)}, u32[]{:S(2)}, u32[]{:S(2)}) collective-permute-start(bf16[64,640]{1,0:T(8,128)(2,1)S(1)} %get-tuple-element.32), channel_id=1, source_target_pairs={{0,1},{1,0},{2,3},{3,2},{4,5},{5,4},{6,7},{7,6},{8,9},{9,8},{10,11... | collective-permute-start | bytes 245768 | tf_op jit(solution)/shard_map/ppermute | solution.py:272
  31.6 2.4 %collective-permute-start.10 = (bf16[64,6144]{1,0:T(8,128)(2,1)S(1)}, bf16[64,6144]{1,0:T(8,128)(2,1)S(1)}, u32[]{:S(2)}, u32[]{:S(2)}) collective-permute-start(bf16[64,6144]{1,0:T(8,128)(2,1)S(1)} %get-tuple-element.34), channel_id=1, source_target_pairs={{0,1},{1,0},{2,3},{3,2},{4,5},{5,4},{6,7},{7,6},{8,9},{9,8},{10,11... | collective-permute-start | bytes 2359304 | tf_op jit(solution)/shard_map/ppermute | solution.py:272
  34.8 1.6 %collective-permute-start.15 = (bf16[64,2048]{1,0:T(8,128)(2,1)S(1)}, bf16[64,2048]{1,0:T(8,128)(2,1)S(1)}, u32[]{:S(2)}, u32[]{:S(2)}) collective-permute-start(bf16[64,2048]{1,0:T(8,128)(2,1)S(1)} %get-tuple-element.37), channel_id=1, source_target_pairs={{0,1},{1,0},{2,3},{3,2},{4,5},{5,4},{6,7},{7,6},{8,9},{9,8},{10,11... | collective-permute-start | bytes 786440 | tf_op jit(solution)/shard_map/ppermute | solution.py:272
  35.0 9.3 %collective-permute-start.11 = (bf16[3,8,6144]{2,1,0:T(8,128)(2,1)S(1)}, bf16[3,8,6144]{2,1,0:T(8,128)(2,1)S(1)}, u32[]{:S(2)}, u32[]{:S(2)}) collective-permute-start(bf16[3,8,6144]{2,1,0:T(8,128)(2,1)S(1)} %slice_bitcast_fusion.1), channel_id=1, source_target_pairs={{0,2},{1,3},{2,0},{3,1},{4,6},{5,7},{6,4},{7,5},{8,10},{9,11},{10,... | collective-permute-start | bytes 884744 | tf_op jit(solution)/shard_map/ppermute | solution.py:272
  36.5 10.5 %collective-permute-start.16 = (bf16[2,8,2048]{2,1,0:T(8,128)(2,1)S(1)}, bf16[2,8,2048]{2,1,0:T(8,128)(2,1)S(1)}, u32[]{:S(2)}, u32[]{:S(2)}) collective-permute-start(bf16[2,8,2048]{2,1,0:T(8,128)(2,1)S(1)} %get-tuple-element.46), channel_id=1, source_target_pairs={{0,12},{1,13},{2,14},{3,15},{4,8},{5,9},{6,10},{7,11},{8,4},{9,5},... | collective-permute-start | bytes 196616 | tf_op jit(solution)/shard_map/ppermute | solution.py:272
  39.0 9.9 %collective-permute-start.17 = (bf16[2,8,2048]{2,1,0:T(8,128)(2,1)S(1)}, bf16[2,8,2048]{2,1,0:T(8,128)(2,1)S(1)}, u32[]{:S(2)}, u32[]{:S(2)}) collective-permute-start(bf16[2,8,2048]{2,1,0:T(8,128)(2,1)S(1)} %get-tuple-element.45), channel_id=1, source_target_pairs={{0,8},{1,9},{2,10},{3,11},{4,12},{5,13},{6,14},{7,15},{8,0},{9,1},... | collective-permute-start | bytes 196616 | tf_op jit(solution)/shard_map/ppermute | solution.py:272
  39.0 9.9 %collective-permute-start.18 = (bf16[2,8,2048]{2,1,0:T(8,128)(2,1)S(1)}, bf16[2,8,2048]{2,1,0:T(8,128)(2,1)S(1)}, u32[]{:S(2)}, u32[]{:S(2)}) collective-permute-start(bf16[2,8,2048]{2,1,0:T(8,128)(2,1)S(1)} %get-tuple-element.44), channel_id=1, source_target_pairs={{0,4},{1,5},{2,6},{3,7},{4,0},{5,1},{6,2},{7,3},{8,12},{9,13},{10,... | collective-permute-start | bytes 196616 | tf_op jit(solution)/shard_map/ppermute | solution.py:272
  44.5 7.6 %collective-permute-start.12 = (bf16[8,6144]{1,0:T(8,128)(2,1)S(1)}, bf16[8,6144]{1,0:T(8,128)(2,1)S(1)}, u32[]{:S(2)}, u32[]{:S(2)}) collective-permute-start(bf16[8,6144]{1,0:T(8,128)(2,1)S(1)} %get-tuple-element.41), channel_id=1, source_target_pairs={{0,12},{1,13},{2,14},{3,15},{4,8},{5,9},{6,10},{7,11},{8,4},{9,5},... | collective-permute-start | bytes 294920 | tf_op jit(solution)/shard_map/ppermute | solution.py:272
  47.0 8.0 %collective-permute-start.13 = (bf16[8,6144]{1,0:T(8,128)(2,1)S(1)}, bf16[8,6144]{1,0:T(8,128)(2,1)S(1)}, u32[]{:S(2)}, u32[]{:S(2)}) collective-permute-start(bf16[8,6144]{1,0:T(8,128)(2,1)S(1)} %get-tuple-element.43), channel_id=1, source_target_pairs={{0,8},{1,9},{2,10},{3,11},{4,12},{5,13},{6,14},{7,15},{8,0},{9,1},... | collective-permute-start | bytes 294920 | tf_op jit(solution)/shard_map/ppermute | solution.py:272
  47.0 8.0 %collective-permute-start.14 = (bf16[8,6144]{1,0:T(8,128)(2,1)S(1)}, bf16[8,6144]{1,0:T(8,128)(2,1)S(1)}, u32[]{:S(2)}, u32[]{:S(2)}) collective-permute-start(bf16[8,6144]{1,0:T(8,128)(2,1)S(1)} %get-tuple-element.42), channel_id=1, source_target_pairs={{0,4},{1,5},{2,6},{3,7},{4,0},{5,1},{6,2},{7,3},{8,12},{9,13},{10,... | collective-permute-start | bytes 294920 | tf_op jit(solution)/shard_map/ppermute | solution.py:272
  49.0 6.1 %collective-permute-start.19 = (bf16[8,8192]{1,0:T(8,128)(2,1)S(1)}, bf16[8,8192]{1,0:T(8,128)(2,1)S(1)}, u32[]{:S(2)}, u32[]{:S(2)}) collective-permute-start(bf16[8,8192]{1,0:T(8,128)(2,1)S(1)} %pad_maximum_fusion.1), channel_id=1, source_target_pairs={{0,2},{1,3},{2,0},{3,1},{4,6},{5,7},{6,4},{7,5},{8,10},{9,11},{10,... | collective-permute-start | bytes 393224 | tf_op jit(solution)/shard_map/ppermute | solution.py:272
